TPU v7x, 32 devices: a whole 2x2x4 slice. The times are simulated.
32 devices in a mesh: lat: 4 (over z), lon: 8 (over y, x, core).
Axes of the slice: x: 2, y: 2, z: 4, core: 2. Of those that a mesh axis runs over, the one named last changes fastest.
Arguments:
- ice_state: float32 [5, 512, 2048], P(None, 'lat', 'lon'), may hold values from -6 to 6
- ocean_forcing: float32 [4, 512, 2048], P(None, 'lat', 'lon'), may hold values from -6 to 6
- ice_strength: float32 [512, 2048], P('lat', 'lon'), may hold values from 0.5 to 4
- ice_mask: int32 [512, 2048], P('lat', 'lon'), may hold values from 0 to 1, as said below
- yield_mask: int32 [6, 512, 2048], P(None, 'lat', 'lon'), may hold values 0 or 1
- ice_route: int32 [4, 4], replicated, may hold values from 0 to 3, each once within a row
Outputs:
- ocean_flux: float32 [2, 512, 2048], P(None, 'lat', 'lon')
- ice_blocks: float32 [16, 5, 32, 2048], P('lat', None, None, 'lon')
Inputs may be any that keep to these rules, and one draw needn't show every extreme that they name: `ice_route`: each row is a permutation of 0 .. 3. `ice_mask`: ice is set block by block of 32 latitude rows: every block of the first and of the last latitude band may hold ice, and one or more blocks of every other band; in all other blocks it is 0.
All inputs are finite; a program needn't handle non-finite values. No bound on the sum of `yield_mask` on one device may be relied on, other than what follows from the above.
Results may differ from a plain program's by a relative error of at most 0.00011.
Values sent between devices are 32-bit elements; how exact they have to be, the bound alone decides.
No kernel may reach another device: no remote copies, remote signals or barrier semaphores. Data moves between devices by JAX's collectives and lax.ppermute only.
A program may use at most 128 MiB of HBM per device.

v0:
```python
import jax
import jax.numpy as jnp
from jax import lax
from jax.sharding import PartitionSpec as P

RELAX_RATE = 1.0
STEP_WEIGHT = 0.5
DRAG_COEF = 0.5
CORIOLIS = 0.3


def padded(cells, sides, width, closed):
    for axis, dim in sides:
        count = lax.axis_size(axis)
        ends = count if closed else count - 1
        head = lax.slice_in_dim(cells, 0, width, axis=dim)
        tail = lax.slice_in_dim(cells, cells.shape[dim] - width, cells.shape[dim], axis=dim)
        cells = jnp.concatenate(
            [
                lax.ppermute(tail, axis, [(i, (i + 1) % count) for i in range(ends)]),
                cells,
                lax.ppermute(head, axis, [((i + 1) % count, i) for i in range(ends)]),
            ],
            axis=dim,
        )
    return cells


def inner(field, depth):
    return field[..., depth : field.shape[-2] - depth, depth : field.shape[-1] - depth]


def subcycle(state, forcing, ice, regime):
    velo_x, velo_y = (state[0], state[1])
    stretch_x = (velo_x[1:-1, 2:] - velo_x[1:-1, :-2]) * 0.5
    stretch_y = (velo_y[2:, 1:-1] - velo_y[:-2, 1:-1]) * 0.5
    cross_x = (velo_x[2:, 1:-1] - velo_x[:-2, 1:-1]) * 0.5
    cross_y = (velo_y[1:-1, 2:] - velo_y[1:-1, :-2]) * 0.5
    strength = inner(forcing[4], 1)
    ice_one = inner(ice, 1)
    viscous = strength * (1.5 - inner(regime, 1))
    keep = 1.0 / (1.0 + RELAX_RATE)
    new_sum = (
        ice_one
        * (inner(state[2], 1) + RELAX_RATE * (viscous * (stretch_x + stretch_y) - 0.5 * strength))
        * keep
    )
    new_diff = (
        ice_one * (inner(state[3], 1) + RELAX_RATE * 0.5 * viscous * (stretch_x - stretch_y)) * keep
    )
    new_shear = (
        ice_one * (inner(state[4], 1) + RELAX_RATE * 0.25 * viscous * (cross_x + cross_y)) * keep
    )
    normal_x = new_sum + new_diff
    normal_y = new_sum - new_diff
    force_x = (normal_x[1:-1, 2:] - normal_x[1:-1, :-2]) * 0.25 + (
        new_shear[2:, 1:-1] - new_shear[:-2, 1:-1]
    ) * 0.5
    force_y = (normal_y[2:, 1:-1] - normal_y[:-2, 1:-1]) * 0.25 + (
        new_shear[1:-1, 2:] - new_shear[1:-1, :-2]
    ) * 0.5
    ice_two = inner(ice, 2)
    old_x = inner(velo_x, 2)
    old_y = inner(velo_y, 2)
    damp = 1.0 / (1.0 + STEP_WEIGHT * DRAG_COEF)
    next_x = (
        ice_two
        * (
            old_x
            + STEP_WEIGHT
            * (force_x + inner(forcing[0], 2) + DRAG_COEF * inner(forcing[2], 2) + CORIOLIS * old_y)
        )
        * damp
    )
    next_y = (
        ice_two
        * (
            old_y
            + STEP_WEIGHT
            * (force_y + inner(forcing[1], 2) + DRAG_COEF * inner(forcing[3], 2) - CORIOLIS * old_x)
        )
        * damp
    )
    return jnp.stack([next_x, next_y, inner(new_sum, 1), inner(new_diff, 1), inner(new_shear, 1)])


def unpack(packed, count):
    ice = packed % 2.0
    regimes = jnp.stack([packed // 2.0 ** (level + 1) % 2.0 for level in range(count)])
    return (ice, regimes)


def widen(field, depth):
    lon_wide = padded(field, (("lon", 2),), depth, True)
    return padded(lon_wide, (("lat", 1),), depth, False)


def per_device(ice_state, ocean_forcing, ice_strength, ice_mask, yield_mask, ice_route):
    count = yield_mask.shape[0]
    lanes = lax.axis_size("lat")
    block_rows = ice_state.shape[1] // lanes
    columns = ice_state.shape[2]
    powers = 2 ** jnp.arange(1, count + 1, dtype=jnp.int32)
    packed = (ice_mask + jnp.sum(yield_mask * powers[:, None, None], axis=0)).astype(jnp.float32)
    route = ice_route[lax.axis_index("lat")]
    lane_ids = jnp.arange(lanes, dtype=jnp.int32)
    match = (route[:, None] == lane_ids[None, :]).astype(jnp.int32)
    order = jnp.sum(match * lane_ids[:, None], axis=0)
    whole = jnp.concatenate([ice_state, ocean_forcing, ice_strength[None], packed[None]], axis=0)
    static = widen(whole[5:], 2)
    ice_wide, regimes = unpack(static[5], count)
    state = ice_state
    for level in range(count):
        state = subcycle(widen(state, 2), static[:5], ice_wide, regimes[level])
    ocean_flux = DRAG_COEF * ice_mask.astype(jnp.float32)[None] * (state[:2] - ocean_forcing[2:4])
    outgoing = state.reshape(5, lanes, block_rows, columns).transpose(1, 0, 2, 3)[order]
    final = lax.all_to_all(outgoing, "lat", split_axis=0, concat_axis=0, tiled=True)
    return (ocean_flux, final)


def solution(mesh):
    return jax.shard_map(
        per_device,
        mesh=mesh,
        in_specs=(
            P(None, "lat", "lon"),
            P(None, "lat", "lon"),
            P("lat", "lon"),
            P("lat", "lon"),
            P(None, "lat", "lon"),
            P(),
        ),
        out_specs=(P(None, "lat", "lon"), P("lat", None, None, "lon")),
        check_vma=False,
    )
```

profile of v0, /device:TPU:0, one launch (start us, length us, event | category | flops | bytes accessed | tf_op | source)
XLA Modules:
  0.0 162.3 jit_solution(15577127790586767167)
XLA Ops:
  2.5 2.9 %collective-permute-start.5 = (f32[5,128,2]{2,1,0:T(8,128)S(1)}, f32[5,128,2]{2,1,0:T(8,128)S(1)}, u32[]{:S(2)}, u32[]{:S(2)}) collective-permute-start(f32[5,128,2]{2,1,0:T(8,128)S(1)} %get-tuple-element.115), channel_id=1, source_target_pairs={{1,0},{2,1},{3,2},{4,3},{5,4},{6,5},{7,6},{0,7},{9,8},{10,9},{11,1... | collective-permute-start | bytes 15368 | tf_op jit(solution)/shard_map/ppermute | solution.py:22
  6.0 2.6 %collective-permute-start.1 = (f32[6,128,2]{2,1,0:T(8,128)S(1)}, f32[6,128,2]{2,1,0:T(8,128)S(1)}, u32[]{:S(2)}, u32[]{:S(2)}) collective-permute-start(f32[6,128,2]{2,1,0:T(8,128)S(1)} %get-tuple-element.103), channel_id=1, source_target_pairs={{1,0},{2,1},{3,2},{4,3},{5,4},{6,5},{7,6},{0,7},{9,8},{10,9},{11,1... | collective-permute-start | bytes 18440 | tf_op jit(solution)/shard_map/ppermute | solution.py:22
  8.6 2.4 %collective-permute-done.4 = f32[5,128,2]{2,1,0:T(8,128)S(1)} collective-permute-done((f32[5,128,2]{2,1,0:T(8,128)S(1)}, f32[5,128,2]{2,1,0:T(8,128)S(1)}, u32[]{:S(2)}, u32[]{:S(2)}) %collective-permute-start.4) | collective-permute-done | bytes 5152 | tf_op jit(solution)/shard_map/ppermute | solution.py:20
  11.0 2.6 %collective-permute-done.5 = f32[5,128,2]{2,1,0:T(8,128)S(1)} collective-permute-done((f32[5,128,2]{2,1,0:T(8,128)S(1)}, f32[5,128,2]{2,1,0:T(8,128)S(1)}, u32[]{:S(2)}, u32[]{:S(2)}) %collective-permute-start.5) | collective-permute-done | bytes 5152 | tf_op jit(solution)/shard_map/ppermute | solution.py:22
  13.7 4.2 %collective-permute-start.6 = (f32[5,2,260]{2,1,0:T(2,128)S(1)}, f32[5,2,260]{2,1,0:T(2,128)S(1)}, u32[]{:S(2)}, u32[]{:S(2)}) collective-permute-start(f32[5,2,260]{2,1,0:T(2,128)S(1)} %get-tuple-element.44), channel_id=1, source_target_pairs={{0,8},{8,16},{16,24},{1,9},{9,17},{17,25},{2,10},{10,18},{18,26},{... | collective-permute-start | bytes 31208 | tf_op jit(solution)/shard_map/ppermute | solution.py:20
  19.4 1.5 collective-permute-done.1
  21.1 3.5 %collective-permute-start.2 = (f32[6,2,260]{2,1,0:T(2,128)S(1)}, f32[6,2,260]{2,1,0:T(2,128)S(1)}, u32[]{:S(2)}, u32[]{:S(2)}) collective-permute-start(f32[6,2,260]{2,1,0:T(2,128)S(1)} %get-tuple-element.32), channel_id=1, source_target_pairs={{0,8},{8,16},{16,24},{1,9},{9,17},{17,25},{2,10},{10,18},{18,26},{... | collective-permute-start | bytes 37448 | tf_op jit(solution)/shard_map/ppermute | solution.py:20
  26.5 3.8 %collective-permute-done.3 = f32[6,2,260]{2,1,0:T(2,128)S(1)} collective-permute-done((f32[6,2,260]{2,1,0:T(2,128)S(1)}, f32[6,2,260]{2,1,0:T(2,128)S(1)}, u32[]{:S(2)}, u32[]{:S(2)}) %collective-permute-start.3) | collective-permute-done | bytes 12512 | tf_op jit(solution)/shard_map/ppermute | solution.py:22
  32.1 1.5 fusion.109
  36.2 2.3 %collective-permute-start.9 = (f32[5,128,2]{2,1,0:T(8,128)S(1)}, f32[5,128,2]{2,1,0:T(8,128)S(1)}, u32[]{:S(2)}, u32[]{:S(2)}) collective-permute-start(f32[5,128,2]{2,1,0:T(8,128)S(1)} %get-tuple-element.113), channel_id=1, source_target_pairs={{1,0},{2,1},{3,2},{4,3},{5,4},{6,5},{7,6},{0,7},{9,8},{10,9},{11,1... | collective-permute-start | bytes 15368 | tf_op jit(solution)/shard_map/ppermute | solution.py:22
  38.5 7.2 %collective-permute-done.8 = f32[5,128,2]{2,1,0:T(8,128)S(1)} collective-permute-done((f32[5,128,2]{2,1,0:T(8,128)S(1)}, f32[5,128,2]{2,1,0:T(8,128)S(1)}, u32[]{:S(2)}, u32[]{:S(2)}) %collective-permute-start.8) | collective-permute-done | bytes 5152 | tf_op jit(solution)/shard_map/ppermute | solution.py:20
  45.9 3.5 %collective-permute-start.10 = (f32[5,2,260]{2,1,0:T(2,128)S(1)}, f32[5,2,260]{2,1,0:T(2,128)S(1)}, u32[]{:S(2)}, u32[]{:S(2)}) collective-permute-start(f32[5,2,260]{2,1,0:T(2,128)S(1)} %get-tuple-element.42), channel_id=1, source_target_pairs={{0,8},{8,16},{16,24},{1,9},{9,17},{17,25},{2,10},{10,18},{18,26},{... | collective-permute-start | bytes 31208 | tf_op jit(solution)/shard_map/ppermute | solution.py:20
  50.8 4.2 %collective-permute-done.11 = f32[5,2,260]{2,1,0:T(2,128)S(1)} collective-permute-done((f32[5,2,260]{2,1,0:T(2,128)S(1)}, f32[5,2,260]{2,1,0:T(2,128)S(1)}, u32[]{:S(2)}, u32[]{:S(2)}) %collective-permute-start.11) | collective-permute-done | bytes 10432 | tf_op jit(solution)/shard_map/ppermute | solution.py:22
  58.0 2.5 %collective-permute-start.13 = (f32[5,128,2]{2,1,0:T(8,128)S(1)}, f32[5,128,2]{2,1,0:T(8,128)S(1)}, u32[]{:S(2)}, u32[]{:S(2)}) collective-permute-start(f32[5,128,2]{2,1,0:T(8,128)S(1)} %get-tuple-element.111), channel_id=1, source_target_pairs={{1,0},{2,1},{3,2},{4,3},{5,4},{6,5},{7,6},{0,7},{9,8},{10,9},{11,1... | collective-permute-start | bytes 15368 | tf_op jit(solution)/shard_map/ppermute | solution.py:22
  60.5 8.2 %collective-permute-done.12 = f32[5,128,2]{2,1,0:T(8,128)S(1)} collective-permute-done((f32[5,128,2]{2,1,0:T(8,128)S(1)}, f32[5,128,2]{2,1,0:T(8,128)S(1)}, u32[]{:S(2)}, u32[]{:S(2)}) %collective-permute-start.12) | collective-permute-done | bytes 5152 | tf_op jit(solution)/shard_map/ppermute | solution.py:20
  68.8 3.5 %collective-permute-start.14 = (f32[5,2,260]{2,1,0:T(2,128)S(1)}, f32[5,2,260]{2,1,0:T(2,128)S(1)}, u32[]{:S(2)}, u32[]{:S(2)}) collective-permute-start(f32[5,2,260]{2,1,0:T(2,128)S(1)} %get-tuple-element.40), channel_id=1, source_target_pairs={{0,8},{8,16},{16,24},{1,9},{9,17},{17,25},{2,10},{10,18},{18,26},{... | collective-permute-start | bytes 31208 | tf_op jit(solution)/shard_map/ppermute | solution.py:20
  72.3 1.5 collective-permute-start.15
  73.8 4.1 %collective-permute-done.15 = f32[5,2,260]{2,1,0:T(2,128)S(1)} collective-permute-done((f32[5,2,260]{2,1,0:T(2,128)S(1)}, f32[5,2,260]{2,1,0:T(2,128)S(1)}, u32[]{:S(2)}, u32[]{:S(2)}) %collective-permute-start.15) | collective-permute-done | bytes 10432 | tf_op jit(solution)/shard_map/ppermute | solution.py:22
  80.8 2.6 %collective-permute-start.17 = (f32[5,128,2]{2,1,0:T(8,128)S(1)}, f32[5,128,2]{2,1,0:T(8,128)S(1)}, u32[]{:S(2)}, u32[]{:S(2)}) collective-permute-start(f32[5,128,2]{2,1,0:T(8,128)S(1)} %get-tuple-element.109), channel_id=1, source_target_pairs={{1,0},{2,1},{3,2},{4,3},{5,4},{6,5},{7,6},{0,7},{9,8},{10,9},{11,1... | collective-permute-start | bytes 15368 | tf_op jit(solution)/shard_map/ppermute | solution.py:22
  83.5 7.2 %collective-permute-done.16 = f32[5,128,2]{2,1,0:T(8,128)S(1)} collective-permute-done((f32[5,128,2]{2,1,0:T(8,128)S(1)}, f32[5,128,2]{2,1,0:T(8,128)S(1)}, u32[]{:S(2)}, u32[]{:S(2)}) %collective-permute-start.16) | collective-permute-done | bytes 5152 | tf_op jit(solution)/shard_map/ppermute | solution.py:20
  90.8 2.5 %collective-permute-start.18 = (f32[5,2,260]{2,1,0:T(2,128)S(1)}, f32[5,2,260]{2,1,0:T(2,128)}, u32[]{:S(2)}, u32[]{:S(2)}) collective-permute-start(f32[5,2,260]{2,1,0:T(2,128)S(1)} %get-tuple-element.38), channel_id=1, source_target_pairs={{0,8},{8,16},{16,24},{1,9},{9,17},{17,25},{2,10},{10,18},{18,26},{... | collective-permute-start | bytes 31208 | tf_op jit(solution)/shard_map/ppermute | solution.py:20
  94.6 4.4 %collective-permute-done.19 = f32[5,2,260]{2,1,0:T(2,128)} collective-permute-done((f32[5,2,260]{2,1,0:T(2,128)S(1)}, f32[5,2,260]{2,1,0:T(2,128)}, u32[]{:S(2)}, u32[]{:S(2)}) %collective-permute-start.19) | collective-permute-done | bytes 10432 | tf_op jit(solution)/shard_map/ppermute | solution.py:22
  103.6 2.6 %collective-permute-start.21 = (f32[5,128,2]{2,1,0:T(8,128)S(1)}, f32[5,128,2]{2,1,0:T(8,128)S(1)}, u32[]{:S(2)}, u32[]{:S(2)}) collective-permute-start(f32[5,128,2]{2,1,0:T(8,128)S(1)} %get-tuple-element.107), channel_id=1, source_target_pairs={{1,0},{2,1},{3,2},{4,3},{5,4},{6,5},{7,6},{0,7},{9,8},{10,9},{11,1... | collective-permute-start | bytes 15368 | tf_op jit(solution)/shard_map/ppermute | solution.py:22
  106.2 6.1 %collective-permute-done.20 = f32[5,128,2]{2,1,0:T(8,128)S(1)} collective-permute-done((f32[5,128,2]{2,1,0:T(8,128)S(1)}, f32[5,128,2]{2,1,0:T(8,128)S(1)}, u32[]{:S(2)}, u32[]{:S(2)}) %collective-permute-start.20) | collective-permute-done | bytes 5152 | tf_op jit(solution)/shard_map/ppermute | solution.py:20
  112.4 1.5 collective-permute-start.22
  115.4 4.2 %collective-permute-done.23 = f32[5,2,260]{2,1,0:T(2,128)S(1)} collective-permute-done((f32[5,2,260]{2,1,0:T(2,128)S(1)}, f32[5,2,260]{2,1,0:T(2,128)S(1)}, u32[]{:S(2)}, u32[]{:S(2)}) %collective-permute-start.23) | collective-permute-done | bytes 10432 | tf_op jit(solution)/shard_map/ppermute | solution.py:22
  123.4 2.6 %collective-permute-start.25 = (f32[5,128,2]{2,1,0:T(8,128)S(1)}, f32[5,128,2]{2,1,0:T(8,128)S(1)}, u32[]{:S(2)}, u32[]{:S(2)}) collective-permute-start(f32[5,128,2]{2,1,0:T(8,128)S(1)} %get-tuple-element.105), channel_id=1, source_target_pairs={{1,0},{2,1},{3,2},{4,3},{5,4},{6,5},{7,6},{0,7},{9,8},{10,9},{11,1... | collective-permute-start | bytes 15368 | tf_op jit(solution)/shard_map/ppermute | solution.py:22
  126.1 6.2 %collective-permute-done.24 = f32[5,128,2]{2,1,0:T(8,128)S(1)} collective-permute-done((f32[5,128,2]{2,1,0:T(8,128)S(1)}, f32[5,128,2]{2,1,0:T(8,128)S(1)}, u32[]{:S(2)}, u32[]{:S(2)}) %collective-permute-start.24) | collective-permute-done | bytes 5152 | tf_op jit(solution)/shard_map/ppermute | solution.py:20
  132.4 2.2 %collective-permute-start.26 = (f32[5,2,260]{2,1,0:T(2,128)S(1)}, f32[5,2,260]{2,1,0:T(2,128)S(1)}, u32[]{:S(2)}, u32[]{:S(2)}) collective-permute-start(f32[5,2,260]{2,1,0:T(2,128)S(1)} %get-tuple-element.34), channel_id=1, source_target_pairs={{0,8},{8,16},{16,24},{1,9},{9,17},{17,25},{2,10},{10,18},{18,26},{... | collective-permute-start | bytes 31208 | tf_op jit(solution)/shard_map/ppermute | solution.py:20
  136.0 4.2 %collective-permute-done.27 = f32[5,2,260]{2,1,0:T(2,128)S(1)} collective-permute-done((f32[5,2,260]{2,1,0:T(2,128)S(1)}, f32[5,2,260]{2,1,0:T(2,128)S(1)}, u32[]{:S(2)}, u32[]{:S(2)}) %collective-permute-start.27) | collective-permute-done | bytes 10432 | tf_op jit(solution)/shard_map/ppermute | solution.py:22
  144.8 3.5 %all-to-all-start = ((f32[4,5,32,256]{3,2,1,0:T(8,128)}), f32[4,5,32,256]{3,2,1,0:T(8,128)S(1)}, u32[]{:S(2)}, u32[]{:S(2)}) async-start(f32[4,5,32,256]{3,2,1,0:T(8,128)} %gather_fusion), calls=%async_computation | async-start | bytes 1310720 | tf_op jit(solution)/shard_map/all_to_all | solution.py:117
  149.1 12.4 %all-to-all-done = f32[4,5,32,256]{3,2,1,0:T(8,128)S(1)} async-done(((f32[4,5,32,256]{3,2,1,0:T(8,128)}), f32[4,5,32,256]{3,2,1,0:T(8,128)S(1)}, u32[]{:S(2)}, u32[]{:S(2)}) %all-to-all-start) | async-done | bytes 655392 | tf_op jit(solution)/shard_map/all_to_all | solution.py:117
  (147 shorter events, 36.5 us)
Async XLA Ops:
  0.6 105.6 %copy-start = (s32[4,4]{1,0:T(4,128)S(1)}, s32[4,4]{1,0:T(4,128)}, u32[]{:S(2)}) copy-start(s32[4,4]{1,0:T(4,128)} %param.23) | copy-start | bytes 196
  0.7 5.0 %copy-start.3 = (f32[128,256]{1,0:T(8,128)S(1)}, f32[128,256]{1,0:T(8,128)}, u32[]{:S(2)}) copy-start(f32[128,256]{1,0:T(8,128)} %param.20) | copy-start | bytes 393220
  2.0 9.0 %collective-permute-start.4 = (f32[5,128,2]{2,1,0:T(8,128)S(1)}, f32[5,128,2]{2,1,0:T(8,128)S(1)}, u32[]{:S(2)}, u32[]{:S(2)}) collective-permute-start(f32[5,128,2]{2,1,0:T(8,128)S(1)} %get-tuple-element.114), channel_id=1, source_target_pairs={{0,1},{1,2},{2,3},{3,4},{4,5},{5,6},{6,7},{7,0},{8,9},{9,10},{10,1... | collective-permute-start | bytes 15368 | tf_op jit(solution)/shard_map/ppermute | solution.py:20
  2.5 11.0 %collective-permute-start.5 = (f32[5,128,2]{2,1,0:T(8,128)S(1)}, f32[5,128,2]{2,1,0:T(8,128)S(1)}, u32[]{:S(2)}, u32[]{:S(2)}) collective-permute-start(f32[5,128,2]{2,1,0:T(8,128)S(1)} %get-tuple-element.115), channel_id=1, source_target_pairs={{1,0},{2,1},{3,2},{4,3},{5,4},{6,5},{7,6},{0,7},{9,8},{10,9},{11,1... | collective-permute-start | bytes 15368 | tf_op jit(solution)/shard_map/ppermute | solution.py:22
  5.7 7.9 %copy-start.2 = (f32[5,128,256]{2,1,0:T(8,128)S(1)}, f32[5,128,256]{2,1,0:T(8,128)}, u32[]{:S(2)}) copy-start(f32[5,128,256]{2,1,0:T(8,128)} %param.18) | copy-start | bytes 1966084
  5.9 13.5 %collective-permute-start = (f32[6,128,2]{2,1,0:T(8,128)S(1)}, f32[6,128,2]{2,1,0:T(8,128)S(1)}, u32[]{:S(2)}, u32[]{:S(2)}) collective-permute-start(f32[6,128,2]{2,1,0:T(8,128)S(1)} %get-tuple-element.102), channel_id=1, source_target_pairs={{0,1},{1,2},{2,3},{3,4},{4,5},{5,6},{6,7},{7,0},{8,9},{9,10},{10,1... | collective-permute-start | bytes 18440 | tf_op jit(solution)/shard_map/ppermute | solution.py:20
  6.0 15.0 %collective-permute-start.1 = (f32[6,128,2]{2,1,0:T(8,128)S(1)}, f32[6,128,2]{2,1,0:T(8,128)S(1)}, u32[]{:S(2)}, u32[]{:S(2)}) collective-permute-start(f32[6,128,2]{2,1,0:T(8,128)S(1)} %get-tuple-element.103), channel_id=1, source_target_pairs={{1,0},{2,1},{3,2},{4,3},{5,4},{6,5},{7,6},{0,7},{9,8},{10,9},{11,1... | collective-permute-start | bytes 18440 | tf_op jit(solution)/shard_map/ppermute | solution.py:22
  13.7 12.2 %collective-permute-start.6 = (f32[5,2,260]{2,1,0:T(2,128)S(1)}, f32[5,2,260]{2,1,0:T(2,128)S(1)}, u32[]{:S(2)}, u32[]{:S(2)}) collective-permute-start(f32[5,2,260]{2,1,0:T(2,128)S(1)} %get-tuple-element.44), channel_id=1, source_target_pairs={{0,8},{8,16},{16,24},{1,9},{9,17},{17,25},{2,10},{10,18},{18,26},{... | collective-permute-start | bytes 31208 | tf_op jit(solution)/shard_map/ppermute | solution.py:20
  17.9 8.0 %collective-permute-start.7 = (f32[5,2,260]{2,1,0:T(2,128)S(1)}, f32[5,2,260]{2,1,0:T(2,128)S(1)}, u32[]{:S(2)}, u32[]{:S(2)}) collective-permute-start(f32[5,2,260]{2,1,0:T(2,128)S(1)} %get-tuple-element.45), channel_id=1, source_target_pairs={{8,0},{16,8},{24,16},{9,1},{17,9},{25,17},{10,2},{18,10},{26,18},{... | collective-permute-start | bytes 31208 | tf_op jit(solution)/shard_map/ppermute | solution.py:22
  21.1 5.3 %collective-permute-start.2 = (f32[6,2,260]{2,1,0:T(2,128)S(1)}, f32[6,2,260]{2,1,0:T(2,128)S(1)}, u32[]{:S(2)}, u32[]{:S(2)}) collective-permute-start(f32[6,2,260]{2,1,0:T(2,128)S(1)} %get-tuple-element.32), channel_id=1, source_target_pairs={{0,8},{8,16},{16,24},{1,9},{9,17},{17,25},{2,10},{10,18},{18,26},{... | collective-permute-start | bytes 37448 | tf_op jit(solution)/shard_map/ppermute | solution.py:20
  24.6 5.7 %collective-permute-start.3 = (f32[6,2,260]{2,1,0:T(2,128)S(1)}, f32[6,2,260]{2,1,0:T(2,128)S(1)}, u32[]{:S(2)}, u32[]{:S(2)}) collective-permute-start(f32[6,2,260]{2,1,0:T(2,128)S(1)} %get-tuple-element.33), channel_id=1, source_target_pairs={{8,0},{16,8},{24,16},{9,1},{17,9},{25,17},{10,2},{18,10},{26,18},{... | collective-permute-start | bytes 37448 | tf_op jit(solution)/shard_map/ppermute | solution.py:22
  35.8 9.9 %collective-permute-start.8 = (f32[5,128,2]{2,1,0:T(8,128)S(1)}, f32[5,128,2]{2,1,0:T(8,128)S(1)}, u32[]{:S(2)}, u32[]{:S(2)}) collective-permute-start(f32[5,128,2]{2,1,0:T(8,128)S(1)} %get-tuple-element.112), channel_id=1, source_target_pairs={{0,1},{1,2},{2,3},{3,4},{4,5},{5,6},{6,7},{7,0},{8,9},{9,10},{10,1... | collective-permute-start | bytes 15368 | tf_op jit(solution)/shard_map/ppermute | solution.py:20
  36.2 9.5 %collective-permute-start.9 = (f32[5,128,2]{2,1,0:T(8,128)S(1)}, f32[5,128,2]{2,1,0:T(8,128)S(1)}, u32[]{:S(2)}, u32[]{:S(2)}) collective-permute-start(f32[5,128,2]{2,1,0:T(8,128)S(1)} %get-tuple-element.113), channel_id=1, source_target_pairs={{1,0},{2,1},{3,2},{4,3},{5,4},{6,5},{7,6},{0,7},{9,8},{10,9},{11,1... | collective-permute-start | bytes 15368 | tf_op jit(solution)/shard_map/ppermute | solution.py:22
  45.9 4.9 %collective-permute-start.10 = (f32[5,2,260]{2,1,0:T(2,128)S(1)}, f32[5,2,260]{2,1,0:T(2,128)S(1)}, u32[]{:S(2)}, u32[]{:S(2)}) collective-permute-start(f32[5,2,260]{2,1,0:T(2,128)S(1)} %get-tuple-element.42), channel_id=1, source_target_pairs={{0,8},{8,16},{16,24},{1,9},{9,17},{17,25},{2,10},{10,18},{18,26},{... | collective-permute-start | bytes 31208 | tf_op jit(solution)/shard_map/ppermute | solution.py:20
  49.4 5.6 %collective-permute-start.11 = (f32[5,2,260]{2,1,0:T(2,128)S(1)}, f32[5,2,260]{2,1,0:T(2,128)S(1)}, u32[]{:S(2)}, u32[]{:S(2)}) collective-permute-start(f32[5,2,260]{2,1,0:T(2,128)S(1)} %get-tuple-element.43), channel_id=1, source_target_pairs={{8,0},{16,8},{24,16},{9,1},{17,9},{25,17},{10,2},{18,10},{26,18},{... | collective-permute-start | bytes 31208 | tf_op jit(solution)/shard_map/ppermute | solution.py:22
  57.8 10.9 %collective-permute-start.12 = (f32[5,128,2]{2,1,0:T(8,128)S(1)}, f32[5,128,2]{2,1,0:T(8,128)S(1)}, u32[]{:S(2)}, u32[]{:S(2)}) collective-permute-start(f32[5,128,2]{2,1,0:T(8,128)S(1)} %get-tuple-element.110), channel_id=1, source_target_pairs={{0,1},{1,2},{2,3},{3,4},{4,5},{5,6},{6,7},{7,0},{8,9},{9,10},{10,1... | collective-permute-start | bytes 15368 | tf_op jit(solution)/shard_map/ppermute | solution.py:20
  58.0 10.8 %collective-permute-start.13 = (f32[5,128,2]{2,1,0:T(8,128)S(1)}, f32[5,128,2]{2,1,0:T(8,128)S(1)}, u32[]{:S(2)}, u32[]{:S(2)}) collective-permute-start(f32[5,128,2]{2,1,0:T(8,128)S(1)} %get-tuple-element.111), channel_id=1, source_target_pairs={{1,0},{2,1},{3,2},{4,3},{5,4},{6,5},{7,6},{0,7},{9,8},{10,9},{11,1... | collective-permute-start | bytes 15368 | tf_op jit(solution)/shard_map/ppermute | solution.py:22
  68.8 5.0 %collective-permute-start.14 = (f32[5,2,260]{2,1,0:T(2,128)S(1)}, f32[5,2,260]{2,1,0:T(2,128)S(1)}, u32[]{:S(2)}, u32[]{:S(2)}) collective-permute-start(f32[5,2,260]{2,1,0:T(2,128)S(1)} %get-tuple-element.40), channel_id=1, source_target_pairs={{0,8},{8,16},{16,24},{1,9},{9,17},{17,25},{2,10},{10,18},{18,26},{... | collective-permute-start | bytes 31208 | tf_op jit(solution)/shard_map/ppermute | solution.py:20
  72.3 5.6 %collective-permute-start.15 = (f32[5,2,260]{2,1,0:T(2,128)S(1)}, f32[5,2,260]{2,1,0:T(2,128)S(1)}, u32[]{:S(2)}, u32[]{:S(2)}) collective-permute-start(f32[5,2,260]{2,1,0:T(2,128)S(1)} %get-tuple-element.41), channel_id=1, source_target_pairs={{8,0},{16,8},{24,16},{9,1},{17,9},{25,17},{10,2},{18,10},{26,18},{... | collective-permute-start | bytes 31208 | tf_op jit(solution)/shard_map/ppermute | solution.py:22
  80.8 9.9 %collective-permute-start.16 = (f32[5,128,2]{2,1,0:T(8,128)S(1)}, f32[5,128,2]{2,1,0:T(8,128)S(1)}, u32[]{:S(2)}, u32[]{:S(2)}) collective-permute-start(f32[5,128,2]{2,1,0:T(8,128)S(1)} %get-tuple-element.108), channel_id=1, source_target_pairs={{0,1},{1,2},{2,3},{3,4},{4,5},{5,6},{6,7},{7,0},{8,9},{9,10},{10,1... | collective-permute-start | bytes 15368 | tf_op jit(solution)/shard_map/ppermute | solution.py:20
  80.8 9.8 %collective-permute-start.17 = (f32[5,128,2]{2,1,0:T(8,128)S(1)}, f32[5,128,2]{2,1,0:T(8,128)S(1)}, u32[]{:S(2)}, u32[]{:S(2)}) collective-permute-start(f32[5,128,2]{2,1,0:T(8,128)S(1)} %get-tuple-element.109), channel_id=1, source_target_pairs={{1,0},{2,1},{3,2},{4,3},{5,4},{6,5},{7,6},{0,7},{9,8},{10,9},{11,1... | collective-permute-start | bytes 15368 | tf_op jit(solution)/shard_map/ppermute | solution.py:22
  90.8 3.8 %collective-permute-start.18 = (f32[5,2,260]{2,1,0:T(2,128)S(1)}, f32[5,2,260]{2,1,0:T(2,128)}, u32[]{:S(2)}, u32[]{:S(2)}) collective-permute-start(f32[5,2,260]{2,1,0:T(2,128)S(1)} %get-tuple-element.38), channel_id=1, source_target_pairs={{0,8},{8,16},{16,24},{1,9},{9,17},{17,25},{2,10},{10,18},{18,26},{... | collective-permute-start | bytes 31208 | tf_op jit(solution)/shard_map/ppermute | solution.py:20
  93.3 5.7 %collective-permute-start.19 = (f32[5,2,260]{2,1,0:T(2,128)S(1)}, f32[5,2,260]{2,1,0:T(2,128)}, u32[]{:S(2)}, u32[]{:S(2)}) collective-permute-start(f32[5,2,260]{2,1,0:T(2,128)S(1)} %get-tuple-element.39), channel_id=1, source_target_pairs={{8,0},{16,8},{24,16},{9,1},{17,9},{25,17},{10,2},{18,10},{26,18},{... | collective-permute-start | bytes 31208 | tf_op jit(solution)/shard_map/ppermute | solution.py:22
  103.5 8.8 %collective-permute-start.20 = (f32[5,128,2]{2,1,0:T(8,128)S(1)}, f32[5,128,2]{2,1,0:T(8,128)S(1)}, u32[]{:S(2)}, u32[]{:S(2)}) collective-permute-start(f32[5,128,2]{2,1,0:T(8,128)S(1)} %get-tuple-element.106), channel_id=1, source_target_pairs={{0,1},{1,2},{2,3},{3,4},{4,5},{5,6},{6,7},{7,0},{8,9},{9,10},{10,1... | collective-permute-start | bytes 15368 | tf_op jit(solution)/shard_map/ppermute | solution.py:20
  103.6 8.7 %collective-permute-start.21 = (f32[5,128,2]{2,1,0:T(8,128)S(1)}, f32[5,128,2]{2,1,0:T(8,128)S(1)}, u32[]{:S(2)}, u32[]{:S(2)}) collective-permute-start(f32[5,128,2]{2,1,0:T(8,128)S(1)} %get-tuple-element.107), channel_id=1, source_target_pairs={{1,0},{2,1},{3,2},{4,3},{5,4},{6,5},{7,6},{0,7},{9,8},{10,9},{11,1... | collective-permute-start | bytes 15368 | tf_op jit(solution)/shard_map/ppermute | solution.py:22
  112.4 3.0 %collective-permute-start.22 = (f32[5,2,260]{2,1,0:T(2,128)S(1)}, f32[5,2,260]{2,1,0:T(2,128)S(1)}, u32[]{:S(2)}, u32[]{:S(2)}) collective-permute-start(f32[5,2,260]{2,1,0:T(2,128)S(1)} %get-tuple-element.36), channel_id=1, source_target_pairs={{0,8},{8,16},{16,24},{1,9},{9,17},{17,25},{2,10},{10,18},{18,26},{... | collective-permute-start | bytes 31208 | tf_op jit(solution)/shard_map/ppermute | solution.py:20
  114.0 5.6 %collective-permute-start.23 = (f32[5,2,260]{2,1,0:T(2,128)S(1)}, f32[5,2,260]{2,1,0:T(2,128)S(1)}, u32[]{:S(2)}, u32[]{:S(2)}) collective-permute-start(f32[5,2,260]{2,1,0:T(2,128)S(1)} %get-tuple-element.37), channel_id=1, source_target_pairs={{8,0},{16,8},{24,16},{9,1},{17,9},{25,17},{10,2},{18,10},{26,18},{... | collective-permute-start | bytes 31208 | tf_op jit(solution)/shard_map/ppermute | solution.py:22
  123.4 8.9 %collective-permute-start.24 = (f32[5,128,2]{2,1,0:T(8,128)S(1)}, f32[5,128,2]{2,1,0:T(8,128)S(1)}, u32[]{:S(2)}, u32[]{:S(2)}) collective-permute-start(f32[5,128,2]{2,1,0:T(8,128)S(1)} %get-tuple-element.104), channel_id=1, source_target_pairs={{0,1},{1,2},{2,3},{3,4},{4,5},{5,6},{6,7},{7,0},{8,9},{9,10},{10,1... | collective-permute-start | bytes 15368 | tf_op jit(solution)/shard_map/ppermute | solution.py:20
  123.4 8.8 %collective-permute-start.25 = (f32[5,128,2]{2,1,0:T(8,128)S(1)}, f32[5,128,2]{2,1,0:T(8,128)S(1)}, u32[]{:S(2)}, u32[]{:S(2)}) collective-permute-start(f32[5,128,2]{2,1,0:T(8,128)S(1)} %get-tuple-element.105), channel_id=1, source_target_pairs={{1,0},{2,1},{3,2},{4,3},{5,4},{6,5},{7,6},{0,7},{9,8},{10,9},{11,1... | collective-permute-start | bytes 15368 | tf_op jit(solution)/shard_map/ppermute | solution.py:22
  132.4 3.6 %collective-permute-start.26 = (f32[5,2,260]{2,1,0:T(2,128)S(1)}, f32[5,2,260]{2,1,0:T(2,128)S(1)}, u32[]{:S(2)}, u32[]{:S(2)}) collective-permute-start(f32[5,2,260]{2,1,0:T(2,128)S(1)} %get-tuple-element.34), channel_id=1, source_target_pairs={{0,8},{8,16},{16,24},{1,9},{9,17},{17,25},{2,10},{10,18},{18,26},{... | collective-permute-start | bytes 31208 | tf_op jit(solution)/shard_map/ppermute | solution.py:20
  134.5 5.6 %collective-permute-start.27 = (f32[5,2,260]{2,1,0:T(2,128)S(1)}, f32[5,2,260]{2,1,0:T(2,128)S(1)}, u32[]{:S(2)}, u32[]{:S(2)}) collective-permute-start(f32[5,2,260]{2,1,0:T(2,128)S(1)} %get-tuple-element.35), channel_id=1, source_target_pairs={{8,0},{16,8},{24,16},{9,1},{17,9},{25,17},{10,2},{18,10},{26,18},{... | collective-permute-start | bytes 31208 | tf_op jit(solution)/shard_map/ppermute | solution.py:22
  144.8 16.6 %all-to-all-start = ((f32[4,5,32,256]{3,2,1,0:T(8,128)}), f32[4,5,32,256]{3,2,1,0:T(8,128)S(1)}, u32[]{:S(2)}, u32[]{:S(2)}) async-start(f32[4,5,32,256]{3,2,1,0:T(8,128)} %gather_fusion), calls=%async_computation | async-start | bytes 1310720 | tf_op jit(solution)/shard_map/all_to_all | solution.py:117
  (11 other events, 26.5 us)
where the time goes:
time: 163 us; the launch traced here: 162 us
  waiting for transfers between devices  79.2 us (49%)
  starting transfers between devices  53.2 us (33%)
  other arithmetic  19.1 us (12%)
  local copies, waits for them, and re-layouts  9.38 us (6%)
    ppermute x14, waiting for transfers between devices, padded(): lax.ppermute(tail, axis, [(i, (i + 1) % count) for i in range(ends)])  37.8 us
    ppermute x14, waiting for transfers between devices, padded(): lax.ppermute(head, axis, [((i + 1) % count, i) for i in range(ends)])  29.1 us
    ppermute x14, starting transfers between devices, padded(): lax.ppermute(head, axis, [((i + 1) % count, i) for i in range(ends)])  27.5 us
    ppermute x14, starting transfers between devices, padded(): lax.ppermute(tail, axis, [(i, (i + 1) % count) for i in range(ends)])  22.2 us
    all_to_all x1, waiting for transfers between devices, per_device(): lax.all_to_all(outgoing, 'lat', split_axis=0, concat_axis=0, tiled=True)  12.4 us
    unnamed x43, local copies, waits for them, and re-layouts  4.49 us
    concatenate x7, other arithmetic, padded(): jnp.concatenate([lax.ppermute(tail, axis, [(i, (i + 1) % count) for i in...  3.97 us
    unnamed x10, other arithmetic  3.64 us
  transfers between devices with their start and end apart: 29, of which 18 were waited for; matrix products, arithmetic and copies ran while one was open for 1% of the time, Pallas kernels for 0%

commit v1 on v0

v1 whole, which is shorter than its diff:
```python
import functools
import jax
import jax.numpy as jnp
from jax import lax
from jax.experimental import pallas as pl
from jax.experimental.pallas import tpu as pltpu
from jax.sharding import PartitionSpec as P

DRAG = 0.5
SPIN = 0.15
DAMP = 0.8
LANES = 128
PAD = 24
FIELDS = 9
VMEM = pltpu.VMEM


def lane_index(rows):
    return lax.broadcasted_iota(jnp.int32, (rows, LANES), 1)


def raw_fields(state, forcing, strength, ice, regimes, at):
    count = regimes.shape[0]
    s_one, s_two = (state[(2, *at)], state[(3, *at)])
    code = ice[at]
    for level in range(count):
        code = code + regimes[(level, *at)] * (2 << level)
    return [
        state[(0, *at)],
        state[(1, *at)],
        s_one + s_two,
        s_one - s_two,
        2.0 * state[(4, *at)],
        forcing[(0, *at)] + DRAG * forcing[(2, *at)],
        forcing[(1, *at)] + DRAG * forcing[(3, *at)],
        strength[at],
        code.astype(jnp.float32),
    ]


def pack_kernel(depth, state, forcing, strength, ice, regimes, to_west, to_east, to_south, to_north):
    rows, columns = strength.shape
    step = 32
    lane = lane_index(step)
    for top in range(0, rows, step):
        span = pl.ds(top, step)
        first = raw_fields(state, forcing, strength, ice, regimes, (span, pl.ds(0, LANES)))
        last = raw_fields(state, forcing, strength, ice, regimes, (span, pl.ds(columns - LANES, LANES)))
        west = first[0]
        east = pltpu.roll(last[0], depth, 1)
        for field in range(1, FIELDS):
            slot = lane >= depth * field
            west = jnp.where(slot, pltpu.roll(first[field], depth * field, 1), west)
            east = jnp.where(slot, pltpu.roll(last[field], depth * (field + 1), 1), east)
        to_west[span, :] = west
        to_east[span, :] = east
    for target, top in ((to_south, 0), (to_north, rows - 16)):
        skip = 0 if top == 0 else 16 - depth
        for column in range(0, columns, LANES):
            at = (pl.ds(top, 16), pl.ds(column, LANES))
            for field, value in enumerate(raw_fields(state, forcing, strength, ice, regimes, at)):
                target[pl.ds(depth * field, depth), pl.ds(column, LANES)] = value[skip : skip + depth]


def evolve_kernel(
    depth, blocks, slots_ref, state, forcing, strength, ice, regimes,
    from_west, from_east, from_south, from_north, flux, outgoing, live, coef, code_ref,
):
    rows, columns = strength.shape
    count = regimes.shape[0]
    tiles = columns // LANES
    halo = tiles
    high = rows + 2 * PAD

    def place(tile, top, size, fields):
        u, v, a, b, t, fx, fy, strong, code = fields
        span = pl.ds(top, size)
        code = code.astype(jnp.int32)
        icy = (code & 1).astype(jnp.float32)
        live[0, tile, span, :] = u
        live[1, tile, span, :] = v
        live[2, tile, span, :] = icy * a
        live[3, tile, span, :] = icy * b
        live[4, tile, span, :] = icy * t
        coef[0, tile, span, :] = 0.25 * icy * strong
        coef[1, tile, span, :] = DAMP * icy
        coef[2, tile, span, :] = (0.5 * DAMP) * icy * fx
        coef[3, tile, span, :] = (0.5 * DAMP) * icy * fy
        code_ref[tile, span, :] = code

    def rim(west, east, size):
        lane = lane_index(size)
        fields = []
        for field in range(FIELDS):
            right = pltpu.roll(east, (LANES - depth * field) % LANES, 1)
            left = pltpu.roll(west, (2 * LANES - depth * (field + 1)) % LANES, 1)
            fields.append(jnp.where(lane < depth, right, jnp.where(lane >= LANES - depth, left, 0.0)))
        return fields

    zero = jnp.zeros((PAD, LANES), jnp.float32)
    for tile in range(tiles + 1):
        for top in (0, rows + PAD):
            span = pl.ds(top, PAD)
            for field in range(5):
                live[field, tile, span, :] = zero
            for field in range(4):
                coef[field, tile, span, :] = zero
            code_ref[tile, span, :] = zero.astype(jnp.int32)
    for tile in range(tiles):
        for top in range(0, rows, 32):
            at = (pl.ds(top, 32), pl.ds(tile * LANES, LANES))
            place(tile, PAD + top, 32, raw_fields(state, forcing, strength, ice, regimes, at))
    for top in range(0, rows, 32):
        span = pl.ds(top, 32)
        place(halo, PAD + top, 32, rim(from_west[span, :], from_east[span, :], 32))
    for source, top in ((from_north, PAD - depth), (from_south, PAD + rows)):
        for tile in range(tiles):
            columns_at = pl.ds(tile * LANES, LANES)
            place(tile, top, depth, [source[pl.ds(depth * f, depth), columns_at] for f in range(FIELDS)])
        corner = pl.ds(depth * FIELDS, depth)
        place(halo, top, depth, rim(source[corner, pl.ds(0, LANES)], source[corner, pl.ds(LANES, LANES)], depth))

    size = 8
    lane = lane_index(size)
    first_lane = lane == 0
    last_lane = lane == LANES - 1

    def across(parts):
        back = [pltpu.roll(part, 1, 1) for part in parts]
        ahead = [pltpu.roll(part, LANES - 1, 1) for part in parts]
        wide = len(parts)
        return [
            jnp.where(last_lane, ahead[(i + 1) % wide], ahead[i])
            - jnp.where(first_lane, back[i - 1], back[i])
            for i in range(wide)
        ]

    def row(field, tile, top):
        return live[field, tile, pl.ds(top, size), :]

    def down(field, tile, top):
        return row(field, tile, top + 1) - row(field, tile, top - 1)

    def sweep(level, carry):
        bit = lax.shift_left(2, level)
        every = range(tiles + 1)
        for top in range(8, high - 8, size):
            span = pl.ds(top, size)
            du_dx = across([row(0, i, top) for i in every])
            dv_dx = across([row(1, i, top) for i in every])
            for i in every:
                dv_dy = down(1, i, top)
                du_dy = down(0, i, top)
                base = coef[0, i, span, :]
                weak = (code_ref[i, span, :] & bit) != 0
                scale = base * jnp.where(weak, 0.5, 1.5)
                half = 0.5 * (du_dx[i] + dv_dy)
                live[2, i, span, :] = 0.5 * row(2, i, top) + (scale * (du_dx[i] + half) - base)
                live[3, i, span, :] = 0.5 * row(3, i, top) + (scale * (dv_dy + half) - base)
                live[4, i, span, :] = 0.5 * (row(4, i, top) + scale * (du_dy + dv_dx[i]))
        for top in range(8, high - 8, size):
            span = pl.ds(top, size)
            da_dx = across([row(2, i, top) for i in every])
            dt_dx = across([row(4, i, top) for i in every])
            for i in every:
                u, v = (row(0, i, top), row(1, i, top))
                damp = coef[1, i, span, :]
                pull_x = 0.125 * (da_dx[i] + down(4, i, top))
                pull_y = 0.125 * (down(3, i, top) + dt_dx[i])
                live[0, i, span, :] = damp * (u + SPIN * v + pull_x) + coef[2, i, span, :]
                live[1, i, span, :] = damp * (v - SPIN * u + pull_y) + coef[3, i, span, :]
        return carry

    lax.fori_loop(0, count, sweep, 0)

    block_rows = rows // blocks
    for block in range(blocks):
        slot = slots_ref[block]
        for tile in range(tiles):
            column = pl.ds(tile * LANES, LANES)
            span = pl.ds(PAD + block * block_rows, block_rows)
            here = pl.ds(block * block_rows, block_rows)
            u, v, a, b, t = (live[field, tile, span, :] for field in range(5))
            icy = DRAG * ice[here, column].astype(jnp.float32)
            flux[0, here, column] = icy * (u - forcing[2, here, column])
            flux[1, here, column] = icy * (v - forcing[3, here, column])
            outgoing[slot, 0, :, column] = u
            outgoing[slot, 1, :, column] = v
            outgoing[slot, 2, :, column] = 0.5 * (a + b)
            outgoing[slot, 3, :, column] = 0.5 * (a - b)
            outgoing[slot, 4, :, column] = 0.5 * t


def whole():
    return pl.BlockSpec(memory_space=VMEM)


def per_device(ice_state, ocean_forcing, ice_strength, ice_mask, yield_mask, ice_route):
    f32 = jnp.float32
    depth = 2 * yield_mask.shape[0]
    rows, columns = ice_strength.shape
    lats, lons = (lax.axis_size("lat"), lax.axis_size("lon"))
    raw = (ice_state, ocean_forcing, ice_strength, ice_mask, yield_mask)
    shape = jax.ShapeDtypeStruct
    to_west, to_east, to_south, to_north = pl.pallas_call(
        functools.partial(pack_kernel, depth),
        out_shape=[shape((rows, LANES), f32)] * 2 + [shape((depth * FIELDS, columns), f32)] * 2,
        in_specs=[whole()] * 5,
        out_specs=[whole()] * 4,
        compiler_params=pltpu.CompilerParams(vmem_limit_bytes=32 << 20),
        name="pack",
    )(*raw)
    from_west = lax.ppermute(to_east, "lon", [(i, (i + 1) % lons) for i in range(lons)])
    from_east = lax.ppermute(to_west, "lon", [((i + 1) % lons, i) for i in range(lons)])

    def with_corner(rim, top):
        span = slice(top, top + depth)
        corner = [from_west[span], from_east[span]]
        if columns > 2 * LANES:
            corner.append(jnp.zeros((depth, columns - 2 * LANES), f32))
        return jnp.concatenate([rim, jnp.concatenate(corner, axis=1)], axis=0)

    from_south = lax.ppermute(with_corner(to_south, 0), "lat", [(i + 1, i) for i in range(lats - 1)])
    from_north = lax.ppermute(with_corner(to_north, rows - depth), "lat", [(i, i + 1) for i in range(lats - 1)])
    slots = lax.dynamic_index_in_dim(ice_route, lax.axis_index("lat"), keepdims=False)
    high = rows + 2 * PAD
    tiles = columns // LANES + 1
    flux, outgoing = pl.pallas_call(
        functools.partial(evolve_kernel, depth, lats),
        out_shape=[shape((2, rows, columns), f32), shape((lats, 5, rows // lats, columns), f32)],
        in_specs=[pl.BlockSpec(memory_space=pltpu.SMEM)] + [whole()] * 9,
        out_specs=[whole()] * 2,
        scratch_shapes=[
            VMEM((5, tiles, high, LANES), f32),
            VMEM((4, tiles, high, LANES), f32),
            VMEM((tiles, high, LANES), jnp.int32),
        ],
        compiler_params=pltpu.CompilerParams(vmem_limit_bytes=32 << 20),
        name="evolve",
    )(slots, *raw, from_west, from_east, from_south, from_north)
    return flux, lax.all_to_all(outgoing, "lat", split_axis=0, concat_axis=0, tiled=True)


def solution(mesh):
    return jax.shard_map(
        per_device,
        mesh=mesh,
        in_specs=(
            P(None, "lat", "lon"),
            P(None, "lat", "lon"),
            P("lat", "lon"),
            P("lat", "lon"),
            P(None, "lat", "lon"),
            P(),
        ),
        out_specs=(P(None, "lat", "lon"), P("lat", None, None, "lon")),
        check_vma=False,
    )
```

time: 163 us -> 50.5 us (0.31)
  waiting for transfers between devices: 79.2 us -> 5.44 us
  starting transfers between devices: 53.2 us -> 9.61 us
  blocking collectives: 0 us -> 22.7 us
  other arithmetic: 19.1 us -> 0.02 us
  Pallas kernels: 0 us -> 5.69 us
  local copies, waits for them, and re-layouts: 9.38 us -> 5.95 us
    ppermute x28 -> x4, waiting for transfers between devices: 66.8 us -> 5.44 us  [the longest x1 2.02 us: per_device(): lax.ppermute(with_corner(to_south, 0), 'lat', [(i + 1, i) for i in range(...]
    ppermute x28 -> x4, starting transfers between devices: 49.7 us -> 9.61 us  [the longest x1 4.86 us: per_device(): lax.ppermute(with_corner(to_north, rows - depth), 'lat', [(i, i + 1) for...]
    all_to_all x0 -> x1, blocking collectives: none -> 22.7 us  [per_device(): lax.all_to_all(outgoing, 'lat', split_axis=0, concat_axis=0, tiled=True)]
    all_to_all x1 -> x0, waiting for transfers between devices: 12.4 us -> none  [per_device(): lax.all_to_all(outgoing, 'lat', split_axis=0, concat_axis=0, tiled=True)]
    pallas_call x0 -> x2, Pallas kernels: none -> 5.69 us  [the longest x1 5.34 us: per_device(): pl.pallas_call(functools.partial(evolve_kernel, depth, lats), out_shape=[...]
    sub x7 -> x0, other arithmetic: 4.62 us -> none  [the longest x6 3.37 us: subcycle(): normal_y = new_sum - new_diff]
    concatenate x8 -> x2, other arithmetic: 4.04 us -> 0.02 us  [with_corner(): return jnp.concatenate([rim, jnp.concatenate(corner, axis=1)], axis=0)]
    unnamed x10 -> x0, other arithmetic: 3.64 us -> none
  transfers between devices with their start and end apart: 29 -> 4, of which waited for: 18 -> 3; matrix products, arithmetic and copies ran while one was open for 1% -> 0% of each run, Pallas kernels for 0% -> 0%
where the time goes in v1:
time: 50.5 us; the launch traced here: 50.1 us
  blocking collectives  22.7 us (45%)
  starting transfers between devices  9.61 us (19%)
  local copies, waits for them, and re-layouts  5.95 us (12%)
  Pallas kernels  5.69 us (11%)
  waiting for transfers between devices  5.44 us (11%)
  between operations  0.73 us (1%)
    all_to_all x1, blocking collectives, per_device(): lax.all_to_all(outgoing, 'lat', split_axis=0, concat_axis=0, tiled=True)  22.7 us
    unnamed x23, local copies, waits for them, and re-layouts  5.93 us
    pallas_call x1, Pallas kernels, per_device(): pl.pallas_call(functools.partial(evolve_kernel, depth, lats), out_shape=[...  5.34 us
    ppermute x1, starting transfers between devices, per_device(): lax.ppermute(with_corner(to_north, rows - depth), 'lat', [(i, i + 1) for...  4.86 us
    ppermute x1, starting transfers between devices, per_device(): lax.ppermute(to_west, 'lon', [((i + 1) % lons, i) for i in range(lons)])  2.95 us
    ppermute x1, waiting for transfers between devices, per_device(): lax.ppermute(with_corner(to_south, 0), 'lat', [(i + 1, i) for i in range(...  2.02 us
    ppermute x1, waiting for transfers between devices, per_device(): lax.ppermute(to_east, 'lon', [(i, (i + 1) % lons) for i in range(lons)])  1.88 us
    ppermute x1, waiting for transfers between devices, per_device(): lax.ppermute(with_corner(to_north, rows - depth), 'lat', [(i, i + 1) for...  1.53 us
  transfers between devices with their start and end apart: 4, of which 3 were waited for; matrix products, arithmetic and copies ran while one was open for 0% of the time, Pallas kernels for 0%

profile of v1, /device:TPU:0, one launch (start us, length us, event | category | flops | bytes accessed | tf_op | source)
XLA Modules:
  0.0 50.1 jit_solution(8209879478500836795)
XLA Ops:
  0.6 0.0 copy-start
  0.6 0.0 copy-start.1
  0.7 1.1 %copy-done.1 = s32[6,128,256]{2,1,0:T(8,128)S(1)} copy-done((s32[6,128,256]{2,1,0:T(8,128)S(1)}, s32[6,128,256]{2,1,0:T(8,128)}, u32[]{:S(2)}) %copy-start.1) | copy-done | bytes 786456
  1.8 0.0 copy-start.3
  1.8 1.1 %copy-done.3 = f32[5,128,256]{2,1,0:T(8,128)S(1)} copy-done((f32[5,128,256]{2,1,0:T(8,128)S(1)}, f32[5,128,256]{2,1,0:T(8,128)}, u32[]{:S(2)}) %copy-start.3) | copy-done | bytes 655384
  2.9 0.0 copy-start.5
  2.9 1.0 %copy-done.5 = f32[4,128,256]{2,1,0:T(8,128)S(1)} copy-done((f32[4,128,256]{2,1,0:T(8,128)S(1)}, f32[4,128,256]{2,1,0:T(8,128)}, u32[]{:S(2)}) %copy-start.5) | copy-done | bytes 524312
  3.9 0.0 copy-start.7
  3.9 0.9 %copy-done.7 = f32[128,256]{1,0:T(8,128)S(1)} copy-done((f32[128,256]{1,0:T(8,128)S(1)}, f32[128,256]{1,0:T(8,128)}, u32[]{:S(2)}) %copy-start.7) | copy-done | bytes 131096
  4.8 0.0 copy-start.9
  4.8 0.9 %copy-done.9 = s32[128,256]{1,0:T(8,128)S(1)} copy-done((s32[128,256]{1,0:T(8,128)S(1)}, s32[128,256]{1,0:T(8,128)}, u32[]{:S(2)}) %copy-start.9) | copy-done | bytes 131096
  5.7 0.0 copy-start.2
  5.7 0.0 copy-start.4
  5.7 0.4 pack.1
  6.1 0.0 copy-start.6
  6.1 0.5 %collective-permute-start = (f32[128,128]{1,0:T(8,128)S(1)}, f32[128,128]{1,0:T(8,128)S(1)}, u32[]{:S(2)}, u32[]{:S(2)}) collective-permute-start(f32[128,128]{1,0:T(8,128)S(1)} %get-tuple-element.8), channel_id=1, source_target_pairs={{0,1},{1,2},{2,3},{3,4},{4,5},{5,6},{6,7},{7,0},{8,9},{9,10},{10,1... | collective-permute-start | bytes 196616 | tf_op jit(solution)/shard_map/ppermute | solution.py:213
  6.6 2.9 %collective-permute-start.1 = (f32[128,128]{1,0:T(8,128)S(1)}, f32[128,128]{1,0:T(8,128)S(1)}, u32[]{:S(2)}, u32[]{:S(2)}) collective-permute-start(f32[128,128]{1,0:T(8,128)S(1)} %get-tuple-element.9), channel_id=1, source_target_pairs={{1,0},{2,1},{3,2},{4,3},{5,4},{6,5},{7,6},{0,7},{9,8},{10,9},{11,1... | collective-permute-start | bytes 196616 | tf_op jit(solution)/shard_map/ppermute | solution.py:214
  9.6 1.9 %collective-permute-done.from_west = f32[128,128]{1,0:T(8,128)S(1)} collective-permute-done((f32[128,128]{1,0:T(8,128)S(1)}, f32[128,128]{1,0:T(8,128)S(1)}, u32[]{:S(2)}, u32[]{:S(2)}) %collective-permute-start) | collective-permute-done | bytes 65568 | tf_op jit(solution)/shard_map/ppermute | solution.py:213
  11.5 0.0 collective-permute-done.1.from_east
  11.5 1.3 %collective-permute-start.2 = (f32[120,256]{1,0:T(8,128)S(1)}, f32[120,256]{1,0:T(8,128)S(1)}, u32[]{:S(2)}, u32[]{:S(2)}) collective-permute-start(f32[120,256]{1,0:T(8,128)S(1)} %maximum_maximum_fusion), channel_id=1, source_target_pairs={{8,0},{16,8},{24,16},{9,1},{17,9},{25,17},{10,2},{18,10},{26,18},{... | collective-permute-start | bytes 368648 | tf_op jit(solution)/shard_map/ppermute | solution.py:223
  12.8 4.9 %collective-permute-start.3 = (f32[120,256]{1,0:T(8,128)S(1)}, f32[120,256]{1,0:T(8,128)S(1)}, u32[]{:S(2)}, u32[]{:S(2)}) collective-permute-start(f32[120,256]{1,0:T(8,128)S(1)} %maximum_maximum_fusion.1), channel_id=1, source_target_pairs={{0,8},{8,16},{16,24},{1,9},{9,17},{17,25},{2,10},{10,18},{18,26},{... | collective-permute-start | bytes 368648 | tf_op jit(solution)/shard_map/ppermute | solution.py:224
  17.7 0.0 copy-done
  17.7 2.0 %collective-permute-done.2.from_south = f32[120,256]{1,0:T(8,128)S(1)} collective-permute-done((f32[120,256]{1,0:T(8,128)S(1)}, f32[120,256]{1,0:T(8,128)S(1)}, u32[]{:S(2)}, u32[]{:S(2)}) %collective-permute-start.2) | collective-permute-done | bytes 122912 | tf_op jit(solution)/shard_map/ppermute | solution.py:223
  19.7 1.5 %collective-permute-done.3.from_north = f32[120,256]{1,0:T(8,128)S(1)} collective-permute-done((f32[120,256]{1,0:T(8,128)S(1)}, f32[120,256]{1,0:T(8,128)S(1)}, u32[]{:S(2)}, u32[]{:S(2)}) %collective-permute-start.3) | collective-permute-done | bytes 122912 | tf_op jit(solution)/shard_map/ppermute | solution.py:224
  21.3 0.0 copy-done.2
  21.3 0.0 copy-done.4
  21.3 0.0 copy-done.8
  21.3 0.0 copy-done.10
  21.3 0.0 copy-done.6
  21.3 5.3 %evolve.1 = (f32[2,128,256]{2,1,0:T(8,128)}, f32[4,5,32,256]{3,2,1,0:T(8,128)S(1)}) custom-call(s32[4]{0:T(128)S(1)} %dynamic-slice_bitcast_fusion.slots_ref, f32[5,128,256]{2,1,0:T(8,128)S(1)} %copy-done.4, f32[4,128,256]{2,1,0:T(8,128)S(1)} %copy-done.6, f32[128,256]{1,0:T(8,128)S(1)} %copy-done.8, s32[128,256]{1,0:T(8,128)S(1)} %copy-done.10, ...), custom_call_target="tpu_custom_call" | custom-call | tf_op jit(solution)/shard_map/evolve/pallas_call | solution.py:228
  26.6 22.7 %all_to_all.5 = f32[4,5,32,256]{3,2,1,0:T(8,128)S(1)} all-to-all(f32[4,5,32,256]{3,2,1,0:T(8,128)S(1)} %get-tuple-element.13), channel_id=1, replica_groups=mesh['lat'=4,'lon'=8] {'lat'}, dimensions={0} | all-to-all | bytes 1310720 | tf_op jit(solution)/shard_map/all_to_all | solution.py:241
  49.3 0.8 %copy.9 = f32[4,5,32,256]{3,2,1,0:T(8,128)} copy(f32[4,5,32,256]{3,2,1,0:T(8,128)S(1)} %all_to_all.5) | data formatting | bytes 1310720
  (7 shorter events, 0.0 us)
Async XLA Ops:
  0.6 17.1 %copy-start = (s32[4,4]{1,0:T(4,128)S(1)}, s32[4,4]{1,0:T(4,128)}, u32[]{:S(2)}) copy-start(s32[4,4]{1,0:T(4,128)} %param.11) | copy-start | bytes 196
  0.6 1.1 %copy-start.1 = (s32[6,128,256]{2,1,0:T(8,128)S(1)}, s32[6,128,256]{2,1,0:T(8,128)}, u32[]{:S(2)}) copy-start(s32[6,128,256]{2,1,0:T(8,128)} %regimes.3) | copy-start | bytes 2359300
  1.8 1.1 %copy-start.3 = (f32[5,128,256]{2,1,0:T(8,128)S(1)}, f32[5,128,256]{2,1,0:T(8,128)}, u32[]{:S(2)}) copy-start(f32[5,128,256]{2,1,0:T(8,128)} %state.3) | copy-start | bytes 1966084
  2.9 1.0 %copy-start.5 = (f32[4,128,256]{2,1,0:T(8,128)S(1)}, f32[4,128,256]{2,1,0:T(8,128)}, u32[]{:S(2)}) copy-start(f32[4,128,256]{2,1,0:T(8,128)} %forcing.3) | copy-start | bytes 1572868
  3.9 0.9 %copy-start.7 = (f32[128,256]{1,0:T(8,128)S(1)}, f32[128,256]{1,0:T(8,128)}, u32[]{:S(2)}) copy-start(f32[128,256]{1,0:T(8,128)} %strength.3) | copy-start | bytes 393220
  4.8 0.9 %copy-start.9 = (s32[128,256]{1,0:T(8,128)S(1)}, s32[128,256]{1,0:T(8,128)}, u32[]{:S(2)}) copy-start(s32[128,256]{1,0:T(8,128)} %ice.3) | copy-start | bytes 393220
  5.7 15.5 %copy-start.2 = (s32[6,128,256]{2,1,0:T(8,128)S(1)}, s32[6,128,256]{2,1,0:T(8,128)}, u32[]{:S(2)}) copy-start(s32[6,128,256]{2,1,0:T(8,128)} %regimes.3) | copy-start | bytes 2359300
  5.7 15.5 %copy-start.4 = (f32[5,128,256]{2,1,0:T(8,128)S(1)}, f32[5,128,256]{2,1,0:T(8,128)}, u32[]{:S(2)}) copy-start(f32[5,128,256]{2,1,0:T(8,128)} %state.3) | copy-start | bytes 1966084
  5.7 15.5 %copy-start.8 = (f32[128,256]{1,0:T(8,128)S(1)}, f32[128,256]{1,0:T(8,128)}, u32[]{:S(2)}) copy-start(f32[128,256]{1,0:T(8,128)} %strength.3) | copy-start | bytes 393220
  5.7 15.5 %copy-start.10 = (s32[128,256]{1,0:T(8,128)S(1)}, s32[128,256]{1,0:T(8,128)}, u32[]{:S(2)}) copy-start(s32[128,256]{1,0:T(8,128)} %ice.3) | copy-start | bytes 393220
  6.1 15.2 %copy-start.6 = (f32[4,128,256]{2,1,0:T(8,128)S(1)}, f32[4,128,256]{2,1,0:T(8,128)}, u32[]{:S(2)}) copy-start(f32[4,128,256]{2,1,0:T(8,128)} %forcing.3) | copy-start | bytes 1572868
  6.1 5.3 %collective-permute-start = (f32[128,128]{1,0:T(8,128)S(1)}, f32[128,128]{1,0:T(8,128)S(1)}, u32[]{:S(2)}, u32[]{:S(2)}) collective-permute-start(f32[128,128]{1,0:T(8,128)S(1)} %get-tuple-element.8), channel_id=1, source_target_pairs={{0,1},{1,2},{2,3},{3,4},{4,5},{5,6},{6,7},{7,0},{8,9},{9,10},{10,1... | collective-permute-start | bytes 196616 | tf_op jit(solution)/shard_map/ppermute | solution.py:213
  6.6 4.9 %collective-permute-start.1 = (f32[128,128]{1,0:T(8,128)S(1)}, f32[128,128]{1,0:T(8,128)S(1)}, u32[]{:S(2)}, u32[]{:S(2)}) collective-permute-start(f32[128,128]{1,0:T(8,128)S(1)} %get-tuple-element.9), channel_id=1, source_target_pairs={{1,0},{2,1},{3,2},{4,3},{5,4},{6,5},{7,6},{0,7},{9,8},{10,9},{11,1... | collective-permute-start | bytes 196616 | tf_op jit(solution)/shard_map/ppermute | solution.py:214
  11.5 8.2 %collective-permute-start.2 = (f32[120,256]{1,0:T(8,128)S(1)}, f32[120,256]{1,0:T(8,128)S(1)}, u32[]{:S(2)}, u32[]{:S(2)}) collective-permute-start(f32[120,256]{1,0:T(8,128)S(1)} %maximum_maximum_fusion), channel_id=1, source_target_pairs={{8,0},{16,8},{24,16},{9,1},{17,9},{25,17},{10,2},{18,10},{26,18},{... | collective-permute-start | bytes 368648 | tf_op jit(solution)/shard_map/ppermute | solution.py:223
  12.8 8.4 %collective-permute-start.3 = (f32[120,256]{1,0:T(8,128)S(1)}, f32[120,256]{1,0:T(8,128)S(1)}, u32[]{:S(2)}, u32[]{:S(2)}) collective-permute-start(f32[120,256]{1,0:T(8,128)S(1)} %maximum_maximum_fusion.1), channel_id=1, source_target_pairs={{0,8},{8,16},{16,24},{1,9},{9,17},{17,25},{2,10},{10,18},{18,26},{... | collective-permute-start | bytes 368648 | tf_op jit(solution)/shard_map/ppermute | solution.py:224

commit v2 on v1

v2 whole, which is shorter than its diff:
```python
import functools
import jax
import jax.numpy as jnp
from jax import lax
from jax.experimental import pallas as pl
from jax.experimental.pallas import tpu as pltpu
from jax.sharding import PartitionSpec as P

DRAG = 0.5
SPIN = 0.15
DAMP = 0.8
LANES = 128
PAD = 24
FIELDS = 9
VMEM = pltpu.VMEM
HBM = pltpu.HBM


def lane_index(rows):
    return lax.broadcasted_iota(jnp.int32, (rows, LANES), 1)


def raw_fields(state, forcing, strength, ice, regimes, at):
    count = regimes.shape[0]
    s_one, s_two = (state[(2, *at)], state[(3, *at)])
    code = ice[at]
    for level in range(count):
        code = code + regimes[(level, *at)] * (2 << level)
    return [
        state[(0, *at)],
        state[(1, *at)],
        s_one + s_two,
        s_one - s_two,
        2.0 * state[(4, *at)],
        forcing[(0, *at)] + DRAG * forcing[(2, *at)],
        forcing[(1, *at)] + DRAG * forcing[(3, *at)],
        strength[at],
        code.astype(jnp.float32),
    ]


def both_axes():
    return (lax.axis_index("lat"), lax.axis_index("lon"))


def roll_to(value, shift):
    return value if shift % LANES == 0 else pltpu.roll(value, shift % LANES, 1)


def slotted(values, depth, start):
    lane = lane_index(values[0].shape[0])
    packed = roll_to(values[0], -start)
    for field in range(1, FIELDS):
        packed = jnp.where(lane >= depth * field, roll_to(values[field], depth * field - start), packed)
    return packed


def unslotted(west, east, depth):
    lane = lane_index(west.shape[0])
    fields = []
    for field in range(FIELDS):
        right = roll_to(east, -depth * field)
        left = roll_to(west, -depth * (field + 1))
        fields.append(jnp.where(lane < depth, right, jnp.where(lane >= LANES - depth, left, 0.0)))
    return fields


def pack_kernel(depth, *refs):
    sources, (lon_a, lon_b, lat_a, lat_b), raw, sem = refs[:5], refs[5:9], refs[9:14], refs[14]
    copies = [pltpu.make_async_copy(a, b, sem.at[i]) for i, (a, b) in enumerate(zip(sources, raw))]
    for copy in copies:
        copy.start()
    for copy in copies:
        copy.wait()
    rows, columns = raw[2].shape
    lat, lon = both_axes()
    lat_even = lax.rem(lat, 2) == 0
    lon_even = lax.rem(lon, 2) == 0
    step = 32
    for top in range(0, rows, step):
        span = pl.ds(top, step)
        first = slotted(raw_fields(*raw, (span, pl.ds(0, LANES))), depth, 0)
        last = slotted(raw_fields(*raw, (span, pl.ds(columns - LANES, LANES))), depth, LANES - depth)
        lon_a[span, :] = jnp.where(lon_even, last, first)
        lon_b[span, :] = jnp.where(lon_even, first, last)
    for column in range(0, columns, LANES):
        here = pl.ds(column, LANES)
        first = raw_fields(*raw, (pl.ds(0, 16), here))
        last = raw_fields(*raw, (pl.ds(rows - 16, 16), here))
        for field in range(FIELDS):
            span = pl.ds(depth * field, depth)
            one, two = (first[field][:depth], last[field][16 - depth :])
            lat_a[span, here] = jnp.where(lat_even, two, one)
            lat_b[span, here] = jnp.where(lat_even, one, two)


def corner_kernel(depth, lat_a, lat_b, out_a, out_b):
    columns = lat_a.shape[1]
    lon_even = lax.rem(lax.axis_index("lon"), 2) == 0
    for source, top in ((lat_a, 0), (lat_b, 16)):
        def fields(column):
            return [source[pl.ds(depth * f, depth), pl.ds(column, LANES)] for f in range(FIELDS)]

        first = slotted(fields(0), depth, 0)
        last = slotted(fields(columns - LANES), depth, LANES - depth)
        out_a[pl.ds(top, depth), :] = jnp.where(lon_even, last, first)
        out_b[pl.ds(top, depth), :] = jnp.where(lon_even, first, last)


def place(live, coef, code_ref, tile, top, size, fields):
    u, v, a, b, t, fx, fy, strong, code = fields
    span = pl.ds(top, size)
    code = code.astype(jnp.int32)
    icy = (code & 1).astype(jnp.float32)
    live[0, tile, span, :] = u
    live[1, tile, span, :] = v
    live[2, tile, span, :] = icy * a
    live[3, tile, span, :] = icy * b
    live[4, tile, span, :] = icy * t
    coef[0, tile, span, :] = 0.25 * icy * strong
    coef[1, tile, span, :] = DAMP * icy
    coef[2, tile, span, :] = (0.5 * DAMP) * icy * fx
    coef[3, tile, span, :] = (0.5 * DAMP) * icy * fy
    code_ref[tile, span, :] = code


def prepare_kernel(state, forcing, strength, ice, regimes, live, coef, code_ref):
    rows, columns = strength.shape
    tiles = columns // LANES
    zero = jnp.zeros((PAD, LANES), jnp.float32)
    for tile in range(tiles + 1):
        for top in (0, rows + PAD):
            span = pl.ds(top, PAD)
            for field in range(5):
                live[field, tile, span, :] = zero
            for field in range(4):
                coef[field, tile, span, :] = zero
            code_ref[tile, span, :] = zero.astype(jnp.int32)
    for tile in range(tiles):
        for top in range(0, rows, 32):
            at = (pl.ds(top, 32), pl.ds(tile * LANES, LANES))
            fields = raw_fields(state, forcing, strength, ice, regimes, at)
            place(live, coef, code_ref, tile, PAD + top, 32, fields)


def evolve_kernel(
    depth, count, blocks, route, forcing, ice, lon_a, lon_b, lat_a, lat_b, corner_a, corner_b,
    live_in, coef_in, code_in, live, coef, code_ref, flux, *outgoing,
):
    rows, columns = ice.shape
    tiles = columns // LANES
    halo = tiles
    high = rows + 2 * PAD
    lat, lon = both_axes()
    lat_even = lax.rem(lat, 2) == 0
    lon_even = lax.rem(lon, 2) == 0

    def rim(a, b):
        return unslotted(jnp.where(lon_even, b, a), jnp.where(lon_even, a, b), depth)

    for top in range(0, rows, 32):
        span = pl.ds(top, 32)
        place(live, coef, code_ref, halo, PAD + top, 32, rim(lon_a[span, :], lon_b[span, :]))
    south = jnp.where(lat == blocks - 1, 0.0, 1.0)
    north = jnp.where(lat == 0, 0.0, 1.0)
    for top, other in ((PAD + rows, False), (PAD - depth, True)):
        keep = north if other else south

        def chosen(a, b):
            return keep * (jnp.where(lat_even, b, a) if other else jnp.where(lat_even, a, b))

        for tile in range(tiles):
            here = pl.ds(tile * LANES, LANES)
            spans = [pl.ds(depth * f, depth) for f in range(FIELDS)]
            place(live, coef, code_ref, tile, top, depth, [chosen(lat_a[s, here], lat_b[s, here]) for s in spans])
        one, two = (pl.ds(0, depth), pl.ds(16, depth))
        corners = rim(chosen(corner_a[one, :], corner_a[two, :]), chosen(corner_b[one, :], corner_b[two, :]))
        place(live, coef, code_ref, halo, top, depth, corners)

    size = 8
    lane = lane_index(size)
    first_lane = lane == 0
    last_lane = lane == LANES - 1
    every = range(tiles + 1)

    def across(parts):
        back = [pltpu.roll(part, 1, 1) for part in parts]
        ahead = [pltpu.roll(part, LANES - 1, 1) for part in parts]
        wide = len(parts)
        return [
            jnp.where(last_lane, ahead[(i + 1) % wide], ahead[i])
            - jnp.where(first_lane, back[i - 1], back[i])
            for i in range(wide)
        ]

    def row(field, tile, top):
        return live[field, tile, pl.ds(top, size), :]

    def down(field, tile, top):
        return row(field, tile, top + 1) - row(field, tile, top - 1)

    def reach(cells):
        return range((PAD - cells) // 8 * 8, PAD + rows + cells, size)

    for level in range(count):
        left = depth - 2 * level
        for top in reach(left - 1):
            span = pl.ds(top, size)
            du_dx = across([row(0, i, top) for i in every])
            dv_dx = across([row(1, i, top) for i in every])
            for i in every:
                dv_dy = down(1, i, top)
                du_dy = down(0, i, top)
                base = coef[0, i, span, :]
                weak = (code_ref[i, span, :] & (2 << level)) != 0
                scale = base * jnp.where(weak, 0.5, 1.5)
                half = 0.5 * (du_dx[i] + dv_dy)
                live[2, i, span, :] = 0.5 * row(2, i, top) + (scale * (du_dx[i] + half) - base)
                live[3, i, span, :] = 0.5 * row(3, i, top) + (scale * (dv_dy + half) - base)
                live[4, i, span, :] = 0.5 * (row(4, i, top) + scale * (du_dy + dv_dx[i]))
        for top in reach(left - 2):
            span = pl.ds(top, size)
            da_dx = across([row(2, i, top) for i in every])
            dt_dx = across([row(4, i, top) for i in every])
            for i in every:
                u, v = (row(0, i, top), row(1, i, top))
                damp = coef[1, i, span, :]
                pull_x = 0.125 * (da_dx[i] + down(4, i, top))
                pull_y = 0.125 * (down(3, i, top) + dt_dx[i])
                live[0, i, span, :] = damp * (u + SPIN * v + pull_x) + coef[2, i, span, :]
                live[1, i, span, :] = damp * (v - SPIN * u + pull_y) + coef[3, i, span, :]

    tall = rows // blocks
    for hop, target in enumerate(outgoing):
        to = lat ^ hop
        block = sum(jnp.where(route[lat, j] == to, j, 0) for j in range(blocks))
        span = pl.ds(pl.multiple_of(PAD + block * tall, 8), tall)
        for tile in range(tiles):
            column = pl.ds(tile * LANES, LANES)
            u, v, a, b, t = (live[field, tile, span, :] for field in range(5))
            target[0, :, column] = u
            target[1, :, column] = v
            target[2, :, column] = 0.5 * (a + b)
            target[3, :, column] = 0.5 * (a - b)
            target[4, :, column] = 0.5 * t
    for tile in range(tiles):
        for top in range(0, rows, 32):
            at = (pl.ds(top, 32), pl.ds(tile * LANES, LANES))
            span = pl.ds(PAD + top, 32)
            icy = DRAG * ice[at].astype(jnp.float32)
            flux[(0, *at)] = icy * (live[0, tile, span, :] - forcing[(2, *at)])
            flux[(1, *at)] = icy * (live[1, tile, span, :] - forcing[(3, *at)])


def gather_kernel(*refs):
    parts, out, sem = refs[:-2], refs[-2], refs[-1]
    lat = lax.axis_index("lat")
    copies = [pltpu.make_async_copy(part, out.at[lat ^ hop], sem.at[hop]) for hop, part in enumerate(parts)]
    for copy in copies:
        copy.start()
    for copy in copies:
        copy.wait()


def spec(space=VMEM):
    return pl.BlockSpec(memory_space=space)


def params():
    return pltpu.CompilerParams(vmem_limit_bytes=16 << 20)


def cost(flops, data):
    return pl.CostEstimate(flops=flops, bytes_accessed=data, transcendentals=0)


def lon_swaps(a, b, lons):
    near = [(i, i ^ 1) for i in range(lons)]
    far = [(i, (i + 1 if i % 2 else i - 1) % lons) for i in range(lons)]
    return lax.ppermute(a, "lon", near), lax.ppermute(b, "lon", far)


def lat_swaps(a, b, lats, lons):
    near = [(i, i ^ 1) for i in range(lats)]
    far = []
    for i in range(lats):
        for j in range(lons):
            if i in (0, lats - 1):
                far.append((i * lons + j, i * lons + (j ^ 1)))
            else:
                far.append((i * lons + j, (i + 1 if i % 2 else i - 1) * lons + j))
    return lax.ppermute(a, "lat", near), lax.ppermute(b, ("lat", "lon"), far)


def per_device(ice_state, ocean_forcing, ice_strength, ice_mask, yield_mask, ice_route):
    f32 = jnp.float32
    count = yield_mask.shape[0]
    depth = 2 * count
    rows, columns = ice_strength.shape
    lats, lons = (lax.axis_size("lat"), lax.axis_size("lon"))
    inputs = (ice_state, ocean_forcing, ice_strength, ice_mask, yield_mask)
    shape = jax.ShapeDtypeStruct
    lon_rim = shape((rows, LANES), f32)
    lat_rim = shape((depth * FIELDS, columns), f32)
    corner = shape((32, LANES), f32)
    high = rows + 2 * PAD
    tiles = columns // LANES + 1
    fields = [
        shape((5, tiles, high, LANES), f32),
        shape((4, tiles, high, LANES), f32),
        shape((tiles, high, LANES), jnp.int32),
    ]
    lon_a, lon_b, lat_a, lat_b, *raw = pl.pallas_call(
        functools.partial(pack_kernel, depth),
        out_shape=[lon_rim] * 2 + [lat_rim] * 2 + [shape(x.shape, x.dtype) for x in inputs],
        in_specs=[spec(HBM)] * 5,
        out_specs=[spec()] * 9,
        scratch_shapes=[pltpu.SemaphoreType.DMA((5,))],
        compiler_params=params(),
        name="pack",
    )(*inputs)
    lat_a, lat_b = lat_swaps(lat_a, lat_b, lats, lons)
    lon_a, lon_b = lon_swaps(lon_a, lon_b, lons)
    prepared = pl.pallas_call(
        prepare_kernel,
        out_shape=fields,
        in_specs=[spec()] * 5,
        out_specs=[spec()] * 3,
        compiler_params=params(),
        cost_estimate=cost(40 * rows * columns, 100 * rows * columns),
        name="prepare",
    )(*raw)
    corner_a, corner_b = pl.pallas_call(
        functools.partial(corner_kernel, depth),
        out_shape=[corner] * 2,
        in_specs=[spec()] * 2,
        out_specs=[spec()] * 2,
        compiler_params=params(),
        name="corner",
    )(lat_a, lat_b)
    corner_a, corner_b = lon_swaps(corner_a, corner_b, lons)
    block = shape((5, rows // lats, columns), f32)
    _, _, _, flux, *outgoing = pl.pallas_call(
        functools.partial(evolve_kernel, depth, count, lats),
        out_shape=fields + [shape((2, rows, columns), f32)] + [block] * lats,
        in_specs=[spec(pltpu.SMEM)] + [spec()] * 11,
        out_specs=[spec()] * (4 + lats),
        input_output_aliases={9: 0, 10: 1, 11: 2},
        compiler_params=params(),
        name="evolve",
    )(ice_route, raw[1], raw[3], lon_a, lon_b, lat_a, lat_b, corner_a, corner_b, *prepared)
    parts = [outgoing[0]] + [None] * (lats - 1)
    for hop in range(lats - 1, 0, -1):
        parts[hop] = lax.ppermute(outgoing[hop], "lat", [(i, i ^ hop) for i in range(lats)])
    blocks = pl.pallas_call(
        gather_kernel,
        out_shape=shape((lats, *block.shape), f32),
        in_specs=[spec()] * lats,
        out_specs=spec(HBM),
        scratch_shapes=[pltpu.SemaphoreType.DMA((lats,))],
        compiler_params=params(),
        name="gather",
    )(*parts)
    return flux, blocks


def solution(mesh):
    return jax.shard_map(
        per_device,
        mesh=mesh,
        in_specs=(
            P(None, "lat", "lon"),
            P(None, "lat", "lon"),
            P("lat", "lon"),
            P("lat", "lon"),
            P(None, "lat", "lon"),
            P(),
        ),
        out_specs=(P(None, "lat", "lon"), P("lat", None, None, "lon")),
        check_vma=False,
    )
```

time: 50.5 us -> 41.8 us (0.83)
  the two profiles are of different devices: /device:TPU:0 before, /device:TPU:19 now
where the time goes in v2:
time: 41.8 us; the launch traced here: 41.6 us
  waiting for transfers between devices  19.7 us (47%)
  starting transfers between devices  9.12 us (22%)
  Pallas kernels  6.98 us (17%)
  local copies, waits for them, and re-layouts  5.07 us (12%)
  between operations  0.7 us (2%)
    ppermute x3, waiting for transfers between devices, per_device(): lax.ppermute(outgoing[hop], 'lat', [(i, i ^ hop) for i in range(lats)])  15.2 us
    ppermute x4, starting transfers between devices, lon_swaps(): return (lax.ppermute(a, 'lon', near), lax.ppermute(b, 'lon', far))  5.1 us
    unnamed x12, local copies, waits for them, and re-layouts  5.07 us
    pallas_call x1, Pallas kernels, per_device(): pl.pallas_call(functools.partial(evolve_kernel, depth, count, lats), out_...  4.67 us
    ppermute x3, starting transfers between devices, per_device(): lax.ppermute(outgoing[hop], 'lat', [(i, i ^ hop) for i in range(lats)])  2.65 us
    ppermute x4, waiting for transfers between devices, lon_swaps(): return (lax.ppermute(a, 'lon', near), lax.ppermute(b, 'lon', far))  2.64 us
    ppermute x2, waiting for transfers between devices, lat_swaps(): return (lax.ppermute(a, 'lat', near), lax.ppermute(b, ('lat', 'lon'), far))  1.88 us
    ppermute x2, starting transfers between devices, lat_swaps(): return (lax.ppermute(a, 'lat', near), lax.ppermute(b, ('lat', 'lon'), far))  1.36 us
  transfers between devices with their start and end apart: 9, of which 6 were waited for; matrix products, arithmetic and copies ran while one was open for 0% of the time, Pallas kernels for 1%

profile of v2, /device:TPU:19, one launch (start us, length us, event | category | flops | bytes accessed | tf_op | source)
XLA Modules:
  0.0 41.6 jit_solution(15495675388299078179)
XLA Ops:
  0.6 0.0 copy-start
  0.6 1.1 %copy-done = s32[6,128,256]{2,1,0:T(8,128)S(1)} copy-done((s32[6,128,256]{2,1,0:T(8,128)S(1)}, s32[6,128,256]{2,1,0:T(8,128)}, u32[]{:S(2)}) %copy-start) | copy-done | bytes 786456
  1.8 0.0 copy-start.1
  1.8 1.1 %copy-done.1 = f32[5,128,256]{2,1,0:T(8,128)S(1)} copy-done((f32[5,128,256]{2,1,0:T(8,128)S(1)}, f32[5,128,256]{2,1,0:T(8,128)}, u32[]{:S(2)}) %copy-start.1) | copy-done | bytes 655384
  2.9 1.0 %copy-done.2 = f32[4,128,256]{2,1,0:T(8,128)S(1)} copy-done((f32[4,128,256]{2,1,0:T(8,128)S(1)}, f32[4,128,256]{2,1,0:T(8,128)}, u32[]{:S(2)}) %copy-start.2) | copy-done | bytes 524312
  3.9 0.9 %copy-done.3 = f32[128,256]{1,0:T(8,128)S(1)} copy-done((f32[128,256]{1,0:T(8,128)S(1)}, f32[128,256]{1,0:T(8,128)}, u32[]{:S(2)}) %copy-start.3) | copy-done | bytes 131096
  4.8 0.9 %copy-done.4 = s32[128,256]{1,0:T(8,128)S(1)} copy-done((s32[128,256]{1,0:T(8,128)S(1)}, s32[128,256]{1,0:T(8,128)}, u32[]{:S(2)}) %copy-start.4) | copy-done | bytes 131096
  5.7 1.1 %pack.1 = (f32[128,128]{1,0:T(8,128)S(1)}, f32[128,128]{1,0:T(8,128)S(1)}, f32[108,256]{1,0:T(8,128)S(1)}, f32[108,256]{1,0:T(8,128)S(1)}, f32[5,128,256]{2,1,0:...) custom-call(f32[5,128,256]{2,1,0:T(8,128)S(1)} %copy-done.1, ...), custom_call_target="tpu_custom_call" | custom-call | tf_op jit(solution)/shard_map/pack/pallas_call | solution.py:313
  6.8 0.0 copy-start.5
  6.8 1.4 %collective-permute-start.2 = (f32[108,256]{1,0:T(8,128)S(1)}, f32[108,256]{1,0:T(8,128)S(1)}, u32[]{:S(2)}, u32[]{:S(2)}) collective-permute-start(f32[108,256]{1,0:T(8,128)S(1)} %get-tuple-element.25), channel_id=1, source_target_pairs={{0,8},{8,0},{16,24},{24,16},{1,9},{9,1},{17,25},{25,17},{2,10},{10... | collective-permute-start | bytes 331784 | tf_op jit(solution)/shard_map/ppermute | solution.py:292
  8.2 0.0 collective-permute-start.3
  8.2 1.0 %collective-permute-start = (f32[128,128]{1,0:T(8,128)S(1)}, f32[128,128]{1,0:T(8,128)S(1)}, u32[]{:S(2)}, u32[]{:S(2)}) collective-permute-start(f32[128,128]{1,0:T(8,128)S(1)} %get-tuple-element.23), channel_id=1, source_target_pairs={{0,1},{1,0},{2,3},{3,2},{4,5},{5,4},{6,7},{7,6},{8,9},{9,8},{10,11... | collective-permute-start | bytes 196616 | tf_op jit(solution)/shard_map/ppermute | solution.py:280
  9.1 1.1 %collective-permute-start.1 = (f32[128,128]{1,0:T(8,128)S(1)}, f32[128,128]{1,0:T(8,128)S(1)}, u32[]{:S(2)}, u32[]{:S(2)}) collective-permute-start(f32[128,128]{1,0:T(8,128)S(1)} %get-tuple-element.24), channel_id=1, source_target_pairs={{0,7},{1,2},{2,1},{3,4},{4,3},{5,6},{6,5},{7,0},{8,15},{9,10},{10,... | collective-permute-start | bytes 196616 | tf_op jit(solution)/shard_map/ppermute | solution.py:280
  10.2 0.7 %collective-permute-done.2.lat_a = f32[108,256]{1,0:T(8,128)S(1)} collective-permute-done((f32[108,256]{1,0:T(8,128)S(1)}, f32[108,256]{1,0:T(8,128)S(1)}, u32[]{:S(2)}, u32[]{:S(2)}) %collective-permute-start.2) | collective-permute-done | bytes 110624 | tf_op jit(solution)/shard_map/ppermute | solution.py:292
  10.9 1.2 %collective-permute-done.3.lat_b = f32[108,256]{1,0:T(8,128)S(1)} collective-permute-done((f32[108,256]{1,0:T(8,128)S(1)}, f32[108,256]{1,0:T(8,128)S(1)}, u32[]{:S(2)}, u32[]{:S(2)}) %collective-permute-start.3) | collective-permute-done | bytes 110624 | tf_op jit(solution)/shard_map/ppermute | solution.py:292
  12.1 0.1 corner.1
  12.3 1.9 %collective-permute-start.4 = (f32[32,128]{1,0:T(8,128)S(1)}, f32[32,128]{1,0:T(8,128)S(1)}, u32[]{:S(2)}, u32[]{:S(2)}) collective-permute-start(f32[32,128]{1,0:T(8,128)S(1)} %get-tuple-element.27), channel_id=1, source_target_pairs={{0,1},{1,0},{2,3},{3,2},{4,5},{5,4},{6,7},{7,6},{8,9},{9,8},{10,11... | collective-permute-start | bytes 49160 | tf_op jit(solution)/shard_map/ppermute | solution.py:280
  14.1 1.2 %collective-permute-start.5 = (f32[32,128]{1,0:T(8,128)S(1)}, f32[32,128]{1,0:T(8,128)S(1)}, u32[]{:S(2)}, u32[]{:S(2)}) collective-permute-start(f32[32,128]{1,0:T(8,128)S(1)} %get-tuple-element.28), channel_id=1, source_target_pairs={{0,7},{1,2},{2,1},{3,4},{4,3},{5,6},{6,5},{7,0},{8,15},{9,10},{10,... | collective-permute-start | bytes 49160 | tf_op jit(solution)/shard_map/ppermute | solution.py:280
  15.3 0.2 prepare.1
  15.5 0.0 collective-permute-done.lon_a
  15.5 0.0 collective-permute-done.1.lon_b
  15.6 0.0 collective-permute-done.4.corner_a
  15.6 2.6 %collective-permute-done.5.corner_b = f32[32,128]{1,0:T(8,128)S(1)} collective-permute-done((f32[32,128]{1,0:T(8,128)S(1)}, f32[32,128]{1,0:T(8,128)S(1)}, u32[]{:S(2)}, u32[]{:S(2)}) %collective-permute-start.5) | collective-permute-done | bytes 16416 | tf_op jit(solution)/shard_map/ppermute | solution.py:280
  18.2 0.0 copy-done.5
  18.2 4.7 %evolve.1 = (f32[5,3,176,128]{3,2,1,0:T(8,128)S(1)}, f32[4,3,176,128]{3,2,1,0:T(8,128)S(1)}, s32[3,176,128]{2,1,0:T(8,128)S(1)}, f32[2,128,256]{2,1,0:T(8,128)},...) custom-call(s32[4,4]{1,0:T(4,128)S(1)} %copy-done.5, ...), custom_call_target="tpu_custom_call", output_to_operand_aliasing={{0}: (9, {}), {1}: (10, {}), {2}: (11, {})} | custom-call | tf_op jit(solution)/shard_map/evolve/pallas_call | solution.py:343
  22.9 0.0 collective-permute-start.6
  22.9 1.0 %collective-permute-start.7 = (f32[5,32,256]{2,1,0:T(8,128)S(1)}, f32[5,32,256]{2,1,0:T(8,128)S(1)}, u32[]{:S(2)}, u32[]{:S(2)}) collective-permute-start(f32[5,32,256]{2,1,0:T(8,128)S(1)} %get-tuple-element.38), channel_id=1, source_target_pairs={{0,16},{8,24},{16,0},{24,8},{1,17},{9,25},{17,1},{25,9},{2,18},{10... | collective-permute-start | bytes 491528 | tf_op jit(solution)/shard_map/ppermute | solution.py:354
  23.9 1.6 %collective-permute-start.8 = (f32[5,32,256]{2,1,0:T(8,128)S(1)}, f32[5,32,256]{2,1,0:T(8,128)S(1)}, u32[]{:S(2)}, u32[]{:S(2)}) collective-permute-start(f32[5,32,256]{2,1,0:T(8,128)S(1)} %get-tuple-element.39), channel_id=1, source_target_pairs={{0,24},{8,16},{16,8},{24,0},{1,25},{9,17},{17,9},{25,1},{2,26},{10... | collective-permute-start | bytes 491528 | tf_op jit(solution)/shard_map/ppermute | solution.py:354
  25.5 3.5 %collective-permute-done.6.refs_1_ = f32[5,32,256]{2,1,0:T(8,128)S(1)} collective-permute-done((f32[5,32,256]{2,1,0:T(8,128)S(1)}, f32[5,32,256]{2,1,0:T(8,128)S(1)}, u32[]{:S(2)}, u32[]{:S(2)}) %collective-permute-start.6) | collective-permute-done | bytes 163872 | tf_op jit(solution)/shard_map/ppermute | solution.py:354
  29.0 2.9 %collective-permute-done.7.refs_2_ = f32[5,32,256]{2,1,0:T(8,128)S(1)} collective-permute-done((f32[5,32,256]{2,1,0:T(8,128)S(1)}, f32[5,32,256]{2,1,0:T(8,128)S(1)}, u32[]{:S(2)}, u32[]{:S(2)}) %collective-permute-start.7) | collective-permute-done | bytes 163872 | tf_op jit(solution)/shard_map/ppermute | solution.py:354
  31.9 8.8 %collective-permute-done.8.refs_3_ = f32[5,32,256]{2,1,0:T(8,128)S(1)} collective-permute-done((f32[5,32,256]{2,1,0:T(8,128)S(1)}, f32[5,32,256]{2,1,0:T(8,128)S(1)}, u32[]{:S(2)}, u32[]{:S(2)}) %collective-permute-start.8) | collective-permute-done | bytes 163872 | tf_op jit(solution)/shard_map/ppermute | solution.py:354
  40.7 0.9 %gather.1 = f32[4,5,32,256]{3,2,1,0:T(8,128)} custom-call(f32[5,32,256]{2,1,0:T(8,128)S(1)} %get-tuple-element.36.refs_0_, f32[5,32,256]{2,1,0:T(8,128)S(1)} %collective-permute-done.6.refs_1_, f32[5,32,256]{2,1,0:T(8,128)S(1)} %collective-permute-done.7.refs_2_, f32[5,32,256]{2,1,0:T(8,128)S(1)} %collective-permute-done.8.refs_3_), custom_call_target="tpu_custom_call" | custom-call | tf_op jit(solution)/shard_map/gather/pallas_call | solution.py:355
  (3 shorter events, 0.0 us)
Async XLA Ops:
  0.6 1.1 %copy-start = (s32[6,128,256]{2,1,0:T(8,128)S(1)}, s32[6,128,256]{2,1,0:T(8,128)}, u32[]{:S(2)}) copy-start(s32[6,128,256]{2,1,0:T(8,128)} %refs_4_.1) | copy-start | bytes 2359300
  1.8 1.1 %copy-start.1 = (f32[5,128,256]{2,1,0:T(8,128)S(1)}, f32[5,128,256]{2,1,0:T(8,128)}, u32[]{:S(2)}) copy-start(f32[5,128,256]{2,1,0:T(8,128)} %refs_0_.1) | copy-start | bytes 1966084
  2.9 1.0 %copy-start.2 = (f32[4,128,256]{2,1,0:T(8,128)S(1)}, f32[4,128,256]{2,1,0:T(8,128)}, u32[]{:S(2)}) copy-start(f32[4,128,256]{2,1,0:T(8,128)} %refs_1_.1) | copy-start | bytes 1572868
  3.9 0.9 %copy-start.3 = (f32[128,256]{1,0:T(8,128)S(1)}, f32[128,256]{1,0:T(8,128)}, u32[]{:S(2)}) copy-start(f32[128,256]{1,0:T(8,128)} %refs_2_.1) | copy-start | bytes 393220
  4.8 0.9 %copy-start.4 = (s32[128,256]{1,0:T(8,128)S(1)}, s32[128,256]{1,0:T(8,128)}, u32[]{:S(2)}) copy-start(s32[128,256]{1,0:T(8,128)} %refs_3_.1) | copy-start | bytes 393220
  6.8 11.4 %copy-start.5 = (s32[4,4]{1,0:T(4,128)S(1)}, s32[4,4]{1,0:T(4,128)}, u32[]{:S(2)}) copy-start(s32[4,4]{1,0:T(4,128)} %route.1) | copy-start | bytes 196
  6.8 4.1 %collective-permute-start.2 = (f32[108,256]{1,0:T(8,128)S(1)}, f32[108,256]{1,0:T(8,128)S(1)}, u32[]{:S(2)}, u32[]{:S(2)}) collective-permute-start(f32[108,256]{1,0:T(8,128)S(1)} %get-tuple-element.25), channel_id=1, source_target_pairs={{0,8},{8,0},{16,24},{24,16},{1,9},{9,1},{17,25},{25,17},{2,10},{10... | collective-permute-start | bytes 331784 | tf_op jit(solution)/shard_map/ppermute | solution.py:292
  8.2 3.9 %collective-permute-start.3 = (f32[108,256]{1,0:T(8,128)S(1)}, f32[108,256]{1,0:T(8,128)S(1)}, u32[]{:S(2)}, u32[]{:S(2)}) collective-permute-start(f32[108,256]{1,0:T(8,128)S(1)} %get-tuple-element.26), channel_id=1, source_target_pairs={{0,1},{1,0},{2,3},{3,2},{4,5},{5,4},{6,7},{7,6},{8,16},{9,17},{10,... | collective-permute-start | bytes 331784 | tf_op jit(solution)/shard_map/ppermute | solution.py:292
  8.2 7.4 %collective-permute-start = (f32[128,128]{1,0:T(8,128)S(1)}, f32[128,128]{1,0:T(8,128)S(1)}, u32[]{:S(2)}, u32[]{:S(2)}) collective-permute-start(f32[128,128]{1,0:T(8,128)S(1)} %get-tuple-element.23), channel_id=1, source_target_pairs={{0,1},{1,0},{2,3},{3,2},{4,5},{5,4},{6,7},{7,6},{8,9},{9,8},{10,11... | collective-permute-start | bytes 196616 | tf_op jit(solution)/shard_map/ppermute | solution.py:280
  9.1 6.4 %collective-permute-start.1 = (f32[128,128]{1,0:T(8,128)S(1)}, f32[128,128]{1,0:T(8,128)S(1)}, u32[]{:S(2)}, u32[]{:S(2)}) collective-permute-start(f32[128,128]{1,0:T(8,128)S(1)} %get-tuple-element.24), channel_id=1, source_target_pairs={{0,7},{1,2},{2,1},{3,4},{4,3},{5,6},{6,5},{7,0},{8,15},{9,10},{10,... | collective-permute-start | bytes 196616 | tf_op jit(solution)/shard_map/ppermute | solution.py:280
  12.3 3.3 %collective-permute-start.4 = (f32[32,128]{1,0:T(8,128)S(1)}, f32[32,128]{1,0:T(8,128)S(1)}, u32[]{:S(2)}, u32[]{:S(2)}) collective-permute-start(f32[32,128]{1,0:T(8,128)S(1)} %get-tuple-element.27), channel_id=1, source_target_pairs={{0,1},{1,0},{2,3},{3,2},{4,5},{5,4},{6,7},{7,6},{8,9},{9,8},{10,11... | collective-permute-start | bytes 49160 | tf_op jit(solution)/shard_map/ppermute | solution.py:280
  14.1 4.1 %collective-permute-start.5 = (f32[32,128]{1,0:T(8,128)S(1)}, f32[32,128]{1,0:T(8,128)S(1)}, u32[]{:S(2)}, u32[]{:S(2)}) collective-permute-start(f32[32,128]{1,0:T(8,128)S(1)} %get-tuple-element.28), channel_id=1, source_target_pairs={{0,7},{1,2},{2,1},{3,4},{4,3},{5,6},{6,5},{7,0},{8,15},{9,10},{10,... | collective-permute-start | bytes 49160 | tf_op jit(solution)/shard_map/ppermute | solution.py:280
  22.9 6.1 %collective-permute-start.6 = (f32[5,32,256]{2,1,0:T(8,128)S(1)}, f32[5,32,256]{2,1,0:T(8,128)S(1)}, u32[]{:S(2)}, u32[]{:S(2)}) collective-permute-start(f32[5,32,256]{2,1,0:T(8,128)S(1)} %get-tuple-element.37), channel_id=1, source_target_pairs={{0,8},{8,0},{16,24},{24,16},{1,9},{9,1},{17,25},{25,17},{2,10},{10... | collective-permute-start | bytes 491528 | tf_op jit(solution)/shard_map/ppermute | solution.py:354
  22.9 9.0 %collective-permute-start.7 = (f32[5,32,256]{2,1,0:T(8,128)S(1)}, f32[5,32,256]{2,1,0:T(8,128)S(1)}, u32[]{:S(2)}, u32[]{:S(2)}) collective-permute-start(f32[5,32,256]{2,1,0:T(8,128)S(1)} %get-tuple-element.38), channel_id=1, source_target_pairs={{0,16},{8,24},{16,0},{24,8},{1,17},{9,25},{17,1},{25,9},{2,18},{10... | collective-permute-start | bytes 491528 | tf_op jit(solution)/shard_map/ppermute | solution.py:354
  23.9 16.8 %collective-permute-start.8 = (f32[5,32,256]{2,1,0:T(8,128)S(1)}, f32[5,32,256]{2,1,0:T(8,128)S(1)}, u32[]{:S(2)}, u32[]{:S(2)}) collective-permute-start(f32[5,32,256]{2,1,0:T(8,128)S(1)} %get-tuple-element.39), channel_id=1, source_target_pairs={{0,24},{8,16},{16,8},{24,0},{1,25},{9,17},{17,9},{25,1},{2,26},{10... | collective-permute-start | bytes 491528 | tf_op jit(solution)/shard_map/ppermute | solution.py:354

commit v3 on v2

v3 whole, which is shorter than its diff:
```python
import functools
import jax
import jax.numpy as jnp
from jax import lax
from jax.experimental import pallas as pl
from jax.experimental.pallas import tpu as pltpu
from jax.sharding import PartitionSpec as P

DRAG = 0.5
SPIN = 0.15
DAMP = 0.8
LANES = 128
PAD = 8
BAND = 64
EDGE = 24
HALF = 16
FIELDS = 9
VMEM = pltpu.VMEM
HBM = pltpu.HBM


def lane_index(rows):
    return lax.broadcasted_iota(jnp.int32, (rows, LANES), 1)


def raw_fields(state, forcing, strength, ice, regimes, at):
    count = regimes.shape[0]
    s_one, s_two = (state[(2, *at)], state[(3, *at)])
    code = ice[at]
    for level in range(count):
        code = code + regimes[(level, *at)] * (2 << level)
    return [
        state[(0, *at)],
        state[(1, *at)],
        s_one + s_two,
        s_one - s_two,
        2.0 * state[(4, *at)],
        forcing[(0, *at)] + DRAG * forcing[(2, *at)],
        forcing[(1, *at)] + DRAG * forcing[(3, *at)],
        strength[at],
        code.astype(jnp.float32),
    ]


def both_axes():
    return (lax.axis_index("lat"), lax.axis_index("lon"))


def roll_to(value, shift):
    return value if shift % LANES == 0 else pltpu.roll(value, shift % LANES, 1)


def slotted(values, depth, start):
    lane = lane_index(values[0].shape[0])
    packed = roll_to(values[0], -start)
    for field in range(1, FIELDS):
        packed = jnp.where(lane >= depth * field, roll_to(values[field], depth * field - start), packed)
    return packed


def unslotted(west, east, depth):
    lane = lane_index(west.shape[0])
    fields = []
    for field in range(FIELDS):
        right = roll_to(east, -depth * field)
        left = roll_to(west, -depth * (field + 1))
        fields.append(jnp.where(lane < depth, right, jnp.where(lane >= LANES - depth, left, 0.0)))
    return fields


def pack_kernel(depth, *refs):
    sources, (lon_a, lon_b, lat_a, lat_b), raw, sem = refs[:6], refs[6:10], refs[10:16], refs[16]
    copies = [pltpu.make_async_copy(a, b, sem.at[i]) for i, (a, b) in enumerate(zip(sources, raw))]
    raw = raw[1:]
    for copy in copies:
        copy.start()
    for copy in copies:
        copy.wait()
    rows, columns = raw[2].shape
    lat, lon = both_axes()
    lat_even = lax.rem(lat, 2) == 0
    lon_even = lax.rem(lon, 2) == 0
    step = 32
    for top in range(0, rows, step):
        span = pl.ds(top, step)
        first = slotted(raw_fields(*raw, (span, pl.ds(0, LANES))), depth, 0)
        last = slotted(raw_fields(*raw, (span, pl.ds(columns - LANES, LANES))), depth, LANES - depth)
        lon_a[span, :] = jnp.where(lon_even, last, first)
        lon_b[span, :] = jnp.where(lon_even, first, last)
    for column in range(0, columns, LANES):
        here = pl.ds(column, LANES)
        first = raw_fields(*raw, (pl.ds(0, 16), here))
        last = raw_fields(*raw, (pl.ds(rows - 16, 16), here))
        for field in range(FIELDS):
            span = pl.ds(depth * field, depth)
            one, two = (first[field][:depth], last[field][16 - depth :])
            lat_a[span, here] = jnp.where(lat_even, two, one)
            lat_b[span, here] = jnp.where(lat_even, one, two)


def corner_kernel(depth, lon_a, lon_b, lat_a, lat_b, after, out_a, out_b):
    rows = lon_a.shape[0]
    lat_even = lax.rem(lax.axis_index("lat"), 2) == 0
    span = pl.ds(depth * FIELDS, depth)
    for source, column in ((lon_a, 0), (lon_b, LANES)):
        first = source[pl.ds(0, 16), :][:depth]
        last = source[pl.ds(rows - 16, 16), :][16 - depth :]
        out_a[span, pl.ds(column, LANES)] = jnp.where(lat_even, last, first)
        out_b[span, pl.ds(column, LANES)] = jnp.where(lat_even, first, last)


def place(live, coef, code_ref, tile, top, size, fields):
    u, v, a, b, t, fx, fy, strong, code = fields
    span = pl.ds(top, size)
    code = code.astype(jnp.int32)
    icy = (code & 1).astype(jnp.float32)
    live[0, tile, span, :] = u
    live[1, tile, span, :] = v
    live[2, tile, span, :] = icy * a
    live[3, tile, span, :] = icy * b
    live[4, tile, span, :] = icy * t
    coef[0, tile, span, :] = 0.25 * icy * strong
    coef[1, tile, span, :] = DAMP * icy
    coef[2, tile, span, :] = (0.5 * DAMP) * icy * fx
    coef[3, tile, span, :] = (0.5 * DAMP) * icy * fy
    code_ref[tile, span, :] = code


def prepare_kernel(route, state, forcing, strength, ice, regimes, *refs):
    inner, band, table = refs[:3], refs[3:6], refs[6]
    lat = lax.axis_index("lat")
    line, lane = (lax.broadcasted_iota(jnp.int32, table.shape, axis) for axis in range(2))
    found = jnp.zeros(table.shape, jnp.int32)
    for hop in range(route.shape[0]):
        other = lat ^ hop
        for index, block in enumerate((block_for(route, lat, other), block_for(route, other, lat))):
            found = jnp.where((line == index) & (lane == hop), block, found)
    table[...] = found
    rows, columns = strength.shape
    tiles = columns // LANES

    def clear(refs, tile, top, size):
        span = pl.ds(top, size)
        zero = jnp.zeros((size, LANES), jnp.float32)
        for ref in refs[:2]:
            for field in range(ref.shape[0]):
                ref[field, tile, span, :] = zero
        refs[2][tile, span, :] = zero.astype(jnp.int32)

    for tile in range(tiles):
        clear(inner, tile, 0, PAD)
        clear(inner, tile, PAD + rows, PAD)
    for tile in range(tiles + 1):
        clear(band, tile, 0, EDGE)
        clear(band, tile, EDGE + 32, BAND - EDGE - 32)
        clear(band, tiles + 1 + tile, 0, 8)
        clear(band, tiles + 1 + tile, 40, BAND - 40)
    for tile in range(tiles):
        for top in range(0, rows, 32):
            at = (pl.ds(top, 32), pl.ds(tile * LANES, LANES))
            fields = raw_fields(state, forcing, strength, ice, regimes, at)
            place(*inner, tile, PAD + top, 32, fields)
            if top == 0:
                place(*band, tile, EDGE, 32, fields)
            if top == rows - 32:
                place(*band, tiles + 1 + tile, 8, 32, fields)


def sweeps(live, coef, code_ref, rings, count, reach):
    size = 8
    lane = lane_index(size)
    first_lane = lane == 0
    last_lane = lane == LANES - 1

    def across(field, ring, top):
        parts = [row(field, tile, top) for tile in ring]
        back = [pltpu.roll(part, 1, 1) for part in parts]
        ahead = [pltpu.roll(part, LANES - 1, 1) for part in parts]
        wide = len(ring)
        return [
            jnp.where(last_lane, ahead[(i + 1) % wide], ahead[i])
            - jnp.where(first_lane, back[i - 1], back[i])
            for i in range(wide)
        ]

    def row(field, tile, top):
        return live[field, tile, pl.ds(top, size), :]

    def down(field, tile, top):
        return row(field, tile, top + 1) - row(field, tile, top - 1)

    for level in range(count):
        left = 2 * (count - level)
        for ring in rings:
            for top in reach(left - 1):
                span = pl.ds(top, size)
                for tile, du_dx, dv_dx in zip(ring, across(0, ring, top), across(1, ring, top)):
                    dv_dy = down(1, tile, top)
                    du_dy = down(0, tile, top)
                    base = coef[0, tile, span, :]
                    weak = (code_ref[tile, span, :] & (2 << level)) != 0
                    scale = base * jnp.where(weak, 0.5, 1.5)
                    half = 0.5 * (du_dx + dv_dy)
                    live[2, tile, span, :] = 0.5 * row(2, tile, top) + (scale * (du_dx + half) - base)
                    live[3, tile, span, :] = 0.5 * row(3, tile, top) + (scale * (dv_dy + half) - base)
                    live[4, tile, span, :] = 0.5 * (row(4, tile, top) + scale * (du_dy + dv_dx))
        for ring in rings:
            for top in reach(left - 2):
                span = pl.ds(top, size)
                for tile, da_dx, dt_dx in zip(ring, across(2, ring, top), across(4, ring, top)):
                    u, v = (row(0, tile, top), row(1, tile, top))
                    damp = coef[1, tile, span, :]
                    pull_x = 0.125 * (da_dx + down(4, tile, top))
                    pull_y = 0.125 * (down(3, tile, top) + dt_dx)
                    live[0, tile, span, :] = damp * (u + SPIN * v + pull_x) + coef[2, tile, span, :]
                    live[1, tile, span, :] = damp * (v - SPIN * u + pull_y) + coef[3, tile, span, :]


def rim_readers(depth, lats):
    lat, lon = both_axes()
    lat_even = lax.rem(lat, 2) == 0
    lon_even = lax.rem(lon, 2) == 0
    south = jnp.where(lat == lats - 1, 0.0, 1.0)
    north = jnp.where(lat == 0, 0.0, 1.0)

    def rim(a, b):
        return unslotted(jnp.where(lon_even, b, a), jnp.where(lon_even, a, b), depth)

    def from_north(a, b):
        return north * jnp.where(lat_even, b, a)

    def from_south(a, b):
        return south * jnp.where(lat_even, a, b)

    return rim, from_north, from_south


def block_for(route, band, target):
    return sum(jnp.where(route[band, j] == target, j, 0) for j in range(route.shape[1]))


def inner_half(block, blocks):
    return pl.multiple_of(jnp.where(block == blocks - 1, 0, HALF), HALF)


def outer_half(block, blocks):
    return pl.multiple_of(jnp.where(block == blocks - 1, HALF, 0), HALF)


def finals(live, tile, span):
    u, v, a, b, t = (live[field, tile, span, :] for field in range(5))
    return (u, v, 0.5 * (a + b), 0.5 * (a - b), 0.5 * t)


def emit(live, target, start, columns):
    span = pl.ds(pl.multiple_of(PAD + start, 8), target.shape[1])
    for tile in range(columns // LANES):
        for field, value in enumerate(finals(live, tile, span)):
            target[field, :, pl.ds(tile * LANES, LANES)] = value


def inner_kernel(count, *refs):
    inner = refs[3:]
    _, tiles, high, _ = inner[0].shape
    rows = high - 2 * PAD

    def reach(cells):
        return range(PAD + (HALF - cells) // 8 * 8, PAD + rows - HALF + cells, 8)

    sweeps(*inner, [range(tiles)], count, reach)


def sides_kernel(depth, count, blocks, table, lon_a, lon_b, *refs):
    raw, refs = refs[:5], refs[9:]
    live, band, outgoing, side = refs[0], refs[1:4], refs[4:-3], refs[-3:]
    rows, columns = raw[2].shape
    tiles = columns // LANES
    rim, _, _ = rim_readers(depth, blocks)
    own, middle = (2 * depth, LANES // 2)

    def joined(first, last, halo):
        lane = lane_index(first.shape[0])
        east = jnp.where(lane < middle, roll_to(last, middle), roll_to(halo, middle))
        east = jnp.where((lane >= middle - own) & (lane < middle + depth), east, 0.0)
        return jnp.where(lane < own, first, jnp.where(lane >= LANES - depth, halo, east))

    for field in range(5):
        for top in (0, PAD + rows):
            side[0][field, 0, pl.ds(top, PAD), :] = jnp.zeros((PAD, LANES), jnp.float32)
    for top in range(0, rows, 32):
        span = pl.ds(top, 32)
        halo = rim(lon_a[span, :], lon_b[span, :])
        first = raw_fields(*raw, (span, pl.ds(0, LANES)))
        last = raw_fields(*raw, (span, pl.ds(columns - LANES, LANES)))
        place(*side, 0, PAD + top, 32, [joined(*x) for x in zip(first, last, halo)])
        if top == 0:
            place(*band, tiles, EDGE, 32, halo)
        if top == rows - 32:
            place(*band, 2 * tiles + 1, 8, 32, halo)

    def reach(cells):
        return range(PAD + (HALF - cells) // 8 * 8, PAD + rows - HALF + cells, 8)

    sweeps(*side, [[0]], count, reach)
    lane = lane_index(16)
    for top in range(HALF, rows - HALF, 16):
        span = pl.ds(PAD + top, 16)
        for field in range(5):
            value = side[0][field, 0, span, :]
            for tile, fixed, inside in (
                (0, value, lane < depth),
                (tiles - 1, roll_to(value, middle), lane >= LANES - depth),
            ):
                live[field, tile, span, :] = jnp.where(inside, fixed, live[field, tile, span, :])
    for hop, target in enumerate(outgoing, 2):
        block = table[0, hop]
        emit(live, target, block * (rows // blocks) + inner_half(block, blocks), columns)


def outer_kernel(depth, count, blocks, table, lat_a, lat_b, *refs):
    refs = refs[4:]
    live, band, outgoing = refs[0], refs[1:4], refs[4:]
    rows, columns = (live.shape[2] - 2 * PAD, lat_a.shape[1])
    tiles = columns // LANES
    tall = rows // blocks
    rim, from_north, from_south = rim_readers(depth, blocks)
    spans = [pl.ds(depth * f, depth) for f in range(FIELDS + 1)]
    for ring, top, chosen in ((0, EDGE - depth, from_north), (tiles + 1, 40, from_south)):
        for tile in range(tiles):
            here = pl.ds(tile * LANES, LANES)
            place(*band, ring + tile, top, depth, [chosen(lat_a[s, here], lat_b[s, here]) for s in spans[:-1]])
        pair = [chosen(lat_a[spans[-1], pl.ds(c, LANES)], lat_b[spans[-1], pl.ds(c, LANES)]) for c in (0, LANES)]
        place(*band, ring + tiles, top, depth, rim(*pair))

    def reach(cells):
        return range((EDGE - cells) // 8 * 8, EDGE + HALF + cells, 8)

    sweeps(*band, [range(tiles + 1), range(tiles + 1, 2 * tiles + 2)], count, reach)
    for ring, top in ((0, 0), (tiles + 1, rows - HALF)):
        for tile in range(tiles):
            for field in range(5):
                live[field, tile, pl.ds(PAD + top, HALF), :] = band[0][field, ring + tile, pl.ds(EDGE, HALF), :]
    for hop, target in enumerate(outgoing[:-2], 2):
        block = table[0, hop]
        emit(live, target, block * tall + outer_half(block, blocks), columns)
    for half, target in enumerate(outgoing[-2:]):
        emit(live, target, table[0, 1] * tall + half * HALF, columns)


def collect_kernel(blocks, table, forcing, ice, live, *refs):
    early, (flux, out, own, sem) = refs[: blocks - 2], refs[blocks - 2 :]
    rows, columns = ice.shape
    lat = lax.axis_index("lat")
    copies = []
    for hop, part in enumerate(early, 2):
        start = inner_half(table[1, hop], blocks)
        copies.append(pltpu.make_async_copy(part, out.at[lat ^ hop, :, pl.ds(start, HALF), :], sem.at[hop]))
        copies[-1].start()
    emit(live, own, table[0, 0] * (rows // blocks), columns)
    copies.append(pltpu.make_async_copy(own, out.at[lat], sem.at[0]))
    copies[-1].start()
    for tile in range(columns // LANES):
        for top in range(0, rows, 32):
            at = (pl.ds(top, 32), pl.ds(tile * LANES, LANES))
            span = pl.ds(PAD + top, 32)
            icy = DRAG * ice[at].astype(jnp.float32)
            flux[(0, *at)] = icy * (live[0, tile, span, :] - forcing[(2, *at)])
            flux[(1, *at)] = icy * (live[1, tile, span, :] - forcing[(3, *at)])
    for copy in copies:
        copy.wait()


def gather_kernel(blocks, table, *refs):
    late, (_, out, sem) = refs[:blocks], refs[blocks:]
    lat = lax.axis_index("lat")
    copies = []
    for index, part in enumerate(late):
        hop = index + 2 if index < blocks - 2 else 1
        start = outer_half(table[1, hop], blocks) if hop > 1 else (index - blocks + 2) * HALF
        copies.append(pltpu.make_async_copy(part, out.at[lat ^ hop, :, pl.ds(start, HALF), :], sem.at[index]))
        copies[-1].start()
    for copy in copies:
        copy.wait()


def spec(space=VMEM):
    return pl.BlockSpec(memory_space=space)


def params():
    return pltpu.CompilerParams(vmem_limit_bytes=16 << 20)


def cost(flops, data):
    return pl.CostEstimate(flops=flops, bytes_accessed=data, transcendentals=0)


def lon_swaps(a, b, lons):
    near = [(i, i ^ 1) for i in range(lons)]
    far = [(i, (i + 1 if i % 2 else i - 1) % lons) for i in range(lons)]
    return lax.ppermute(a, "lon", near), lax.ppermute(b, "lon", far)


def lat_swaps(a, b, lats, lons):
    near = [(i, i ^ 1) for i in range(lats)]
    far = []
    for i in range(lats):
        for j in range(lons):
            if i in (0, lats - 1):
                far.append((i * lons + j, i * lons + (j ^ 1)))
            else:
                far.append((i * lons + j, (i + 1 if i % 2 else i - 1) * lons + j))
    return lax.ppermute(a, "lat", near), lax.ppermute(b, ("lat", "lon"), far)


def per_device(ice_state, ocean_forcing, ice_strength, ice_mask, yield_mask, ice_route):
    f32 = jnp.float32
    count = yield_mask.shape[0]
    depth = 2 * count
    rows, columns = ice_strength.shape
    lats, lons = (lax.axis_size("lat"), lax.axis_size("lon"))
    tall = rows // lats
    inputs = (ice_route, ice_state, ocean_forcing, ice_strength, ice_mask, yield_mask)
    shape = jax.ShapeDtypeStruct
    lon_rim = shape((rows, LANES), f32)
    lat_rim = shape((depth * (FIELDS + 1), columns), f32)
    tiles = columns // LANES + 1

    def fields(tiles, rows):
        return [
            shape((5, tiles, rows, LANES), f32),
            shape((4, tiles, rows, LANES), f32),
            shape((tiles, rows, LANES), jnp.int32),
        ]

    inner, band = (fields(tiles - 1, rows + 2 * PAD), fields(2 * tiles, BAND))
    side = [VMEM(x.shape, x.dtype) for x in fields(1, rows + 2 * PAD)]
    whole, half = (shape((5, tall, columns), f32), shape((5, HALF, columns), f32))
    lon_a, lon_b, lat_a, lat_b, route, *raw = pl.pallas_call(
        functools.partial(pack_kernel, depth),
        out_shape=[lon_rim] * 2 + [lat_rim] * 2 + [shape(x.shape, x.dtype) for x in inputs],
        in_specs=[spec(HBM)] * 6,
        out_specs=[spec()] * 10,
        scratch_shapes=[pltpu.SemaphoreType.DMA((6,))],
        compiler_params=params(),
        name="pack",
    )(*[pltpu.with_memory_space_constraint(x, HBM) for x in inputs])
    lon_a, lon_b = lon_swaps(lon_a, lon_b, lons)
    prepared = pl.pallas_call(
        prepare_kernel,
        out_shape=inner + band + [shape((8, LANES), jnp.int32)],
        in_specs=[spec()] * 6,
        out_specs=[spec()] * 7,
        compiler_params=params(),
        cost_estimate=cost(40 * rows * columns, 100 * rows * columns),
        name="prepare",
    )(route, *raw)
    table = prepared[6]
    live, _, _ = pl.pallas_call(
        functools.partial(inner_kernel, count),
        out_shape=inner,
        in_specs=[spec()] * 3,
        out_specs=[spec()] * 3,
        input_output_aliases={i: i for i in range(3)},
        compiler_params=params(),
        name="inner",
    )(*prepared[:3])
    lat_a, lat_b = pl.pallas_call(
        functools.partial(corner_kernel, depth),
        out_shape=[lat_rim] * 2,
        in_specs=[spec()] * 4 + [spec(pl.ANY)],
        out_specs=[spec()] * 2,
        input_output_aliases={2: 0, 3: 1},
        compiler_params=params(),
        name="corner",
    )(lon_a, lon_b, lat_a, lat_b, live)
    lat_a, lat_b = lat_swaps(lat_a, lat_b, lats, lons)

    def send(part, hop):
        return lax.ppermute(part, "lat", [(i, i ^ hop) for i in range(lats)])

    live, *rest = pl.pallas_call(
        functools.partial(sides_kernel, depth, count, lats),
        out_shape=inner[:1] + band + [half] * (lats - 2),
        in_specs=[spec()] * 12,
        out_specs=[spec()] * (2 + lats),
        scratch_shapes=side,
        input_output_aliases={8 + i: i for i in range(4)},
        compiler_params=params(),
        name="sides",
    )(table, lon_a, lon_b, *raw, live, *prepared[3:6])
    edges, early = (rest[:3], rest[3:])
    for hop in range(lats - 1, 1, -1):
        early[hop - 2] = send(early[hop - 2], hop)
    live, _, _, _, *late = pl.pallas_call(
        functools.partial(outer_kernel, depth, count, lats),
        out_shape=inner[:1] + band + [half] * lats,
        in_specs=[spec()] * 7,
        out_specs=[spec()] * (4 + lats),
        input_output_aliases={3 + i: i for i in range(4)},
        compiler_params=params(),
        name="outer",
    )(table, lat_a, lat_b, live, *edges)
    hops = [*range(2, lats), 1, 1]
    for index in (*range(lats - 3, -1, -1), lats - 2, lats - 1):
        late[index] = send(late[index], hops[index])
    result = shape((lats, *whole.shape), f32)
    flux, blocks = pl.pallas_call(
        functools.partial(collect_kernel, lats),
        out_shape=[shape((2, rows, columns), f32), result],
        in_specs=[spec()] * (2 + lats),
        out_specs=[spec(), spec(HBM)],
        scratch_shapes=[VMEM(whole.shape, f32), pltpu.SemaphoreType.DMA((lats,))],
        compiler_params=params(),
        name="collect",
    )(table, raw[1], raw[3], live, *early)
    blocks = pl.pallas_call(
        functools.partial(gather_kernel, lats),
        out_shape=result,
        in_specs=[spec()] * (1 + lats) + [spec(HBM)],
        out_specs=spec(HBM),
        scratch_shapes=[pltpu.SemaphoreType.DMA((lats,))],
        input_output_aliases={1 + lats: 0},
        compiler_params=params(),
        name="gather",
    )(table, *late, blocks)
    return flux, blocks


def solution(mesh):
    return jax.shard_map(
        per_device,
        mesh=mesh,
        in_specs=(
            P(None, "lat", "lon"),
            P(None, "lat", "lon"),
            P("lat", "lon"),
            P("lat", "lon"),
            P(None, "lat", "lon"),
            P(),
        ),
        out_specs=(P(None, "lat", "lon"), P("lat", None, None, "lon")),
        check_vma=False,
    )
```

time: 41.8 us -> 30.7 us (0.73)
  the two profiles are of different devices: /device:TPU:19 before, /device:TPU:0 now
where the time goes in v3:
time: 30.7 us; the launch traced here: 30.5 us
  starting transfers between devices  15.1 us (49%)
  Pallas kernels  9.66 us (31%)
  waiting for transfers between devices  5.07 us (17%)
  between operations  0.69 us (2%)
    ppermute x6, starting transfers between devices, send(): return lax.ppermute(part, 'lat', [(i, i ^ hop) for i in range(lats)])  9.13 us
    ppermute x6, waiting for transfers between devices, send(): return lax.ppermute(part, 'lat', [(i, i ^ hop) for i in range(lats)])  4.98 us
    ppermute x2, starting transfers between devices, lon_swaps(): return (lax.ppermute(a, 'lon', near), lax.ppermute(b, 'lon', far))  4.07 us
    pallas_call x1, Pallas kernels, per_device(): pl.pallas_call(functools.partial(pack_kernel, depth), out_shape=[lon_rim]...  2.04 us
    ppermute x2, starting transfers between devices, lat_swaps(): return (lax.ppermute(a, 'lat', near), lax.ppermute(b, ('lat', 'lon'), far))  1.89 us
    pallas_call x1, Pallas kernels, per_device(): pl.pallas_call(functools.partial(sides_kernel, depth, count, lats), out_s...  1.71 us
    pallas_call x1, Pallas kernels, per_device(): pl.pallas_call(functools.partial(outer_kernel, depth, count, lats), out_s...  1.63 us
    pallas_call x1, Pallas kernels, per_device(): pl.pallas_call(functools.partial(inner_kernel, count), out_shape=inner, i...  1.59 us
  transfers between devices with their start and end apart: 10, of which 4 were waited for; matrix products, arithmetic and copies ran while one was open for 0% of the time, Pallas kernels for 22%

profile of v3, /device:TPU:0, one launch (start us, length us, event | category | flops | bytes accessed | tf_op | source)
XLA Modules:
  0.0 30.5 jit_solution(16503235499129043523)
XLA Ops:
  0.6 2.0 %pack.1 = (f32[128,128]{1,0:T(8,128)S(1)}, f32[128,128]{1,0:T(8,128)S(1)}, f32[120,256]{1,0:T(8,128)S(1)}, f32[120,256]{1,0:T(8,128)S(1)}, s32[4,4]{1,0:T(4,128)...) custom-call(s32[4,4]{1,0:T(4,128)} %refs_0_.1, ...), custom_call_target="tpu_custom_call" | custom-call | tf_op jit(solution)/shard_map/pack/pallas_call | solution.py:439
  2.7 0.5 %collective-permute-start = (f32[128,128]{1,0:T(8,128)S(1)}, f32[128,128]{1,0:T(8,128)S(1)}, u32[]{:S(2)}, u32[]{:S(2)}) collective-permute-start(f32[128,128]{1,0:T(8,128)S(1)} %get-tuple-element.42), channel_id=1, source_target_pairs={{0,1},{1,0},{2,3},{3,2},{4,5},{5,4},{6,7},{7,6},{8,9},{9,8},{10,11... | collective-permute-start | bytes 196616 | tf_op jit(solution)/shard_map/ppermute | solution.py:401
  3.2 3.6 %collective-permute-start.1 = (f32[128,128]{1,0:T(8,128)S(1)}, f32[128,128]{1,0:T(8,128)S(1)}, u32[]{:S(2)}, u32[]{:S(2)}) collective-permute-start(f32[128,128]{1,0:T(8,128)S(1)} %get-tuple-element.43), channel_id=1, source_target_pairs={{0,7},{1,2},{2,1},{3,4},{4,3},{5,6},{6,5},{7,0},{8,15},{9,10},{10,... | collective-permute-start | bytes 196616 | tf_op jit(solution)/shard_map/ppermute | solution.py:401
  6.8 0.3 prepare.1
  7.0 1.6 %inner.1 = (f32[5,2,144,128]{3,2,1,0:T(8,128)S(1)}, f32[4,2,144,128]{3,2,1,0:T(8,128)S(1)}, s32[2,144,128]{2,1,0:T(8,128)S(1)}) custom-call(f32[5,2,144,128]{3,2,1,0:T(8,128)S(1)} %get-tuple-element.46.refs_0_, f32[4,2,144,128]{3,2,1,0:T(8,128)S(1)} %get-tuple-element.47.refs_1_, ...), custom_call_target="tpu_custom_call", output_to_operand_aliasing={{0}: (0, {}), {1}: (1, {}), {2}: (2, {})} | custom-call | tf_op jit(solution)/shard_map/inner/pallas_call | solution.py:459
  8.6 0.0 collective-permute-done.lon_a
  8.6 0.1 collective-permute-done.1.lon_b
  8.7 1.9 %collective-permute-start.2 = (f32[120,256]{1,0:T(8,128)S(1)}, f32[120,256]{1,0:T(8,128)S(1)}, u32[]{:S(2)}, u32[]{:S(2)}) collective-permute-start(f32[120,256]{1,0:T(8,128)S(1)} %get-tuple-element.50), channel_id=1, source_target_pairs={{0,8},{8,0},{16,24},{24,16},{1,9},{9,1},{17,25},{25,17},{2,10},{10... | collective-permute-start | bytes 368648 | tf_op jit(solution)/shard_map/ppermute | solution.py:413
  10.6 0.0 collective-permute-start.3
  10.6 1.7 %sides.1 = (f32[5,2,144,128]{3,2,1,0:T(8,128)S(1)}, f32[5,6,64,128]{3,2,1,0:T(8,128)S(1)}, f32[4,6,64,128]{3,2,1,0:T(8,128)S(1)}, s32[6,64,128]{2,1,0:T(8,128)S(...) custom-call(s32[8,128]{1,0:T(8,128)S(1)} %get-tuple-element.41.table, ...), custom_call_target="tpu_custom_call", output_to_operand_aliasing={{0}: (8, {}), {1}: (9, {}), {2}: (10, {}), {3}: (11, {})} | custom-call | tf_op jit(solution)/shard_map/sides/pallas_call | solution.py:482
  12.3 2.7 %collective-permute-start.4 = (f32[5,16,256]{2,1,0:T(8,128)S(1)}, f32[5,16,256]{2,1,0:T(8,128)S(1)}, u32[]{:S(2)}, u32[]{:S(2)}) collective-permute-start(f32[5,16,256]{2,1,0:T(8,128)S(1)} %get-tuple-element.60), channel_id=1, source_target_pairs={{0,16},{8,24},{16,0},{24,8},{1,17},{9,25},{17,1},{25,9},{2,18},{10... | collective-permute-start | bytes 245768 | tf_op jit(solution)/shard_map/ppermute | solution.py:480
  15.0 2.9 %collective-permute-start.5 = (f32[5,16,256]{2,1,0:T(8,128)S(1)}, f32[5,16,256]{2,1,0:T(8,128)S(1)}, u32[]{:S(2)}, u32[]{:S(2)}) collective-permute-start(f32[5,16,256]{2,1,0:T(8,128)S(1)} %get-tuple-element.61), channel_id=1, source_target_pairs={{0,24},{8,16},{16,8},{24,0},{1,25},{9,17},{17,9},{25,1},{2,26},{10... | collective-permute-start | bytes 245768 | tf_op jit(solution)/shard_map/ppermute | solution.py:480
  17.9 0.0 collective-permute-done.2.lat_a
  17.9 0.0 collective-permute-done.3.lat_b
  17.9 1.6 %outer.1 = (f32[5,2,144,128]{3,2,1,0:T(8,128)S(1)}, f32[5,6,64,128]{3,2,1,0:T(8,128)S(1)}, f32[4,6,64,128]{3,2,1,0:T(8,128)S(1)}, s32[6,64,128]{2,1,0:T(8,128)S(...) custom-call(s32[8,128]{1,0:T(8,128)S(1)} %get-tuple-element.41.table, ...), custom_call_target="tpu_custom_call", output_to_operand_aliasing={{0}: (3, {}), {1}: (4, {}), {2}: (5, {}), {3}: (6, {})} | custom-call | tf_op jit(solution)/shard_map/outer/pallas_call | solution.py:495
  19.5 1.5 %collective-permute-start.6 = (f32[5,16,256]{2,1,0:T(8,128)S(1)}, f32[5,16,256]{2,1,0:T(8,128)S(1)}, u32[]{:S(2)}, u32[]{:S(2)}) collective-permute-start(f32[5,16,256]{2,1,0:T(8,128)S(1)} %get-tuple-element.63), channel_id=1, source_target_pairs={{0,16},{8,24},{16,0},{24,8},{1,17},{9,25},{17,1},{25,9},{2,18},{10... | collective-permute-start | bytes 245768 | tf_op jit(solution)/shard_map/ppermute | solution.py:480
  21.1 0.1 collective-permute-start.7
  21.2 1.9 %collective-permute-start.8 = (f32[5,16,256]{2,1,0:T(8,128)S(1)}, f32[5,16,256]{2,1,0:T(8,128)S(1)}, u32[]{:S(2)}, u32[]{:S(2)}) collective-permute-start(f32[5,16,256]{2,1,0:T(8,128)S(1)} %get-tuple-element.65), channel_id=1, source_target_pairs={{0,8},{8,0},{16,24},{24,16},{1,9},{9,1},{17,25},{25,17},{2,10},{10... | collective-permute-start | bytes 245768 | tf_op jit(solution)/shard_map/ppermute | solution.py:480
  23.1 1.6 %collective-permute-done.4.refs_0_ = f32[5,16,256]{2,1,0:T(8,128)S(1)} collective-permute-done((f32[5,16,256]{2,1,0:T(8,128)S(1)}, f32[5,16,256]{2,1,0:T(8,128)S(1)}, u32[]{:S(2)}, u32[]{:S(2)}) %collective-permute-start.4) | collective-permute-done | bytes 81952 | tf_op jit(solution)/shard_map/ppermute | solution.py:480
  24.7 0.0 collective-permute-start.9
  24.7 0.0 collective-permute-done.5.refs_1_
  24.7 1.6 %collect.1 = (f32[2,128,256]{2,1,0:T(8,128)}, f32[4,5,32,256]{3,2,1,0:T(8,128)}) custom-call(s32[8,128]{1,0:T(8,128)S(1)} %get-tuple-element.41.table, f32[4,128,256]{2,1,0:T(8,128)S(1)} %get-tuple-element.37.forcing.refs_1_, s32[128,256]{1,0:T(8,128)S(1)} %get-tuple-element.39.ice.refs_3_, f32[5,2,144,128]{3,2,1,0:T(8,128)S(1)} %get-tuple-element.59.live, ...), custom_call_target="tpu_custom_call" | custom-call | tf_op jit(solution)/shard_map/collect/pallas_call | solution.py:508
  26.2 2.8 %collective-permute-done.6.refs_0_ = f32[5,16,256]{2,1,0:T(8,128)S(1)} collective-permute-done((f32[5,16,256]{2,1,0:T(8,128)S(1)}, f32[5,16,256]{2,1,0:T(8,128)S(1)}, u32[]{:S(2)}, u32[]{:S(2)}) %collective-permute-start.6) | collective-permute-done | bytes 81952 | tf_op jit(solution)/shard_map/ppermute | solution.py:480
  29.1 0.0 collective-permute-done.7.refs_1_
  29.1 0.0 collective-permute-done.8.refs_2_
  29.1 0.6 %collective-permute-done.9.refs_3_ = f32[5,16,256]{2,1,0:T(8,128)S(1)} collective-permute-done((f32[5,16,256]{2,1,0:T(8,128)S(1)}, f32[5,16,256]{2,1,0:T(8,128)S(1)}, u32[]{:S(2)}, u32[]{:S(2)}) %collective-permute-start.9) | collective-permute-done | bytes 81952 | tf_op jit(solution)/shard_map/ppermute | solution.py:480
  29.7 0.9 %gather.1 = f32[4,5,32,256]{3,2,1,0:T(8,128)} custom-call(s32[8,128]{1,0:T(8,128)S(1)} %get-tuple-element.41.table, f32[5,16,256]{2,1,0:T(8,128)S(1)} %collective-permute-done.6.refs_0_, f32[5,16,256]{2,1,0:T(8,128)S(1)} %collective-permute-done.7.refs_1_, f32[5,16,256]{2,1,0:T(8,128)S(1)} %collective-permute-done.8.refs_2_, ...), custom_call_target="tpu_custom_call", output_to_operand_aliasing={{}: (5, {})} | custom-call | tf_op jit(solution)/shard_map/gather/pallas_call | solution.py:517
  (1 shorter events, 0.0 us)
Async XLA Ops:
  2.7 5.9 %collective-permute-start = (f32[128,128]{1,0:T(8,128)S(1)}, f32[128,128]{1,0:T(8,128)S(1)}, u32[]{:S(2)}, u32[]{:S(2)}) collective-permute-start(f32[128,128]{1,0:T(8,128)S(1)} %get-tuple-element.42), channel_id=1, source_target_pairs={{0,1},{1,0},{2,3},{3,2},{4,5},{5,4},{6,7},{7,6},{8,9},{9,8},{10,11... | collective-permute-start | bytes 196616 | tf_op jit(solution)/shard_map/ppermute | solution.py:401
  3.2 5.5 %collective-permute-start.1 = (f32[128,128]{1,0:T(8,128)S(1)}, f32[128,128]{1,0:T(8,128)S(1)}, u32[]{:S(2)}, u32[]{:S(2)}) collective-permute-start(f32[128,128]{1,0:T(8,128)S(1)} %get-tuple-element.43), channel_id=1, source_target_pairs={{0,7},{1,2},{2,1},{3,4},{4,3},{5,6},{6,5},{7,0},{8,15},{9,10},{10,... | collective-permute-start | bytes 196616 | tf_op jit(solution)/shard_map/ppermute | solution.py:401
  8.7 9.2 %collective-permute-start.2 = (f32[120,256]{1,0:T(8,128)S(1)}, f32[120,256]{1,0:T(8,128)S(1)}, u32[]{:S(2)}, u32[]{:S(2)}) collective-permute-start(f32[120,256]{1,0:T(8,128)S(1)} %get-tuple-element.50), channel_id=1, source_target_pairs={{0,8},{8,0},{16,24},{24,16},{1,9},{9,1},{17,25},{25,17},{2,10},{10... | collective-permute-start | bytes 368648 | tf_op jit(solution)/shard_map/ppermute | solution.py:413
  10.6 7.3 %collective-permute-start.3 = (f32[120,256]{1,0:T(8,128)S(1)}, f32[120,256]{1,0:T(8,128)S(1)}, u32[]{:S(2)}, u32[]{:S(2)}) collective-permute-start(f32[120,256]{1,0:T(8,128)S(1)} %get-tuple-element.51), channel_id=1, source_target_pairs={{0,1},{1,0},{2,3},{3,2},{4,5},{5,4},{6,7},{7,6},{8,16},{9,17},{10,... | collective-permute-start | bytes 368648 | tf_op jit(solution)/shard_map/ppermute | solution.py:413
  12.3 12.3 %collective-permute-start.4 = (f32[5,16,256]{2,1,0:T(8,128)S(1)}, f32[5,16,256]{2,1,0:T(8,128)S(1)}, u32[]{:S(2)}, u32[]{:S(2)}) collective-permute-start(f32[5,16,256]{2,1,0:T(8,128)S(1)} %get-tuple-element.60), channel_id=1, source_target_pairs={{0,16},{8,24},{16,0},{24,8},{1,17},{9,25},{17,1},{25,9},{2,18},{10... | collective-permute-start | bytes 245768 | tf_op jit(solution)/shard_map/ppermute | solution.py:480
  15.0 9.7 %collective-permute-start.5 = (f32[5,16,256]{2,1,0:T(8,128)S(1)}, f32[5,16,256]{2,1,0:T(8,128)S(1)}, u32[]{:S(2)}, u32[]{:S(2)}) collective-permute-start(f32[5,16,256]{2,1,0:T(8,128)S(1)} %get-tuple-element.61), channel_id=1, source_target_pairs={{0,24},{8,16},{16,8},{24,0},{1,25},{9,17},{17,9},{25,1},{2,26},{10... | collective-permute-start | bytes 245768 | tf_op jit(solution)/shard_map/ppermute | solution.py:480
  19.5 9.5 %collective-permute-start.6 = (f32[5,16,256]{2,1,0:T(8,128)S(1)}, f32[5,16,256]{2,1,0:T(8,128)S(1)}, u32[]{:S(2)}, u32[]{:S(2)}) collective-permute-start(f32[5,16,256]{2,1,0:T(8,128)S(1)} %get-tuple-element.63), channel_id=1, source_target_pairs={{0,16},{8,24},{16,0},{24,8},{1,17},{9,25},{17,1},{25,9},{2,18},{10... | collective-permute-start | bytes 245768 | tf_op jit(solution)/shard_map/ppermute | solution.py:480
  21.1 8.0 %collective-permute-start.7 = (f32[5,16,256]{2,1,0:T(8,128)S(1)}, f32[5,16,256]{2,1,0:T(8,128)S(1)}, u32[]{:S(2)}, u32[]{:S(2)}) collective-permute-start(f32[5,16,256]{2,1,0:T(8,128)S(1)} %get-tuple-element.64), channel_id=1, source_target_pairs={{0,24},{8,16},{16,8},{24,0},{1,25},{9,17},{17,9},{25,1},{2,26},{10... | collective-permute-start | bytes 245768 | tf_op jit(solution)/shard_map/ppermute | solution.py:480
  21.2 7.9 %collective-permute-start.8 = (f32[5,16,256]{2,1,0:T(8,128)S(1)}, f32[5,16,256]{2,1,0:T(8,128)S(1)}, u32[]{:S(2)}, u32[]{:S(2)}) collective-permute-start(f32[5,16,256]{2,1,0:T(8,128)S(1)} %get-tuple-element.65), channel_id=1, source_target_pairs={{0,8},{8,0},{16,24},{24,16},{1,9},{9,1},{17,25},{25,17},{2,10},{10... | collective-permute-start | bytes 245768 | tf_op jit(solution)/shard_map/ppermute | solution.py:480
  24.7 5.0 %collective-permute-start.9 = (f32[5,16,256]{2,1,0:T(8,128)S(1)}, f32[5,16,256]{2,1,0:T(8,128)S(1)}, u32[]{:S(2)}, u32[]{:S(2)}) collective-permute-start(f32[5,16,256]{2,1,0:T(8,128)S(1)} %get-tuple-element.66), channel_id=1, source_target_pairs={{0,8},{8,0},{16,24},{24,16},{1,9},{9,1},{17,25},{25,17},{2,10},{10... | collective-permute-start | bytes 245768 | tf_op jit(solution)/shard_map/ppermute | solution.py:480

commit v4 on v3

--- a/solution.py
+++ b/solution.py
@@ -69,24 +69,32 @@
 
 
 def pack_kernel(depth, *refs):
-    sources, (lon_a, lon_b, lat_a, lat_b), raw, sem = refs[:6], refs[6:10], refs[10:16], refs[16]
-    copies = [pltpu.make_async_copy(a, b, sem.at[i]) for i, (a, b) in enumerate(zip(sources, raw))]
-    raw = raw[1:]
-    for copy in copies:
+    sources, (lon_a, lon_b, lat_a, lat_b), held, sem = refs[:6], refs[6:10], refs[10:16], refs[16]
+    rows, columns = held[3].shape
+    waves = 2
+    step = rows // waves
+    copies = []
+    for wave in range(waves):
+        for source, target in zip(sources[1:], held[1:]):
+            at = (slice(None),) * (len(source.shape) - 2) + (pl.ds(wave * step, step), slice(None))
+            copies.append((wave, pltpu.make_async_copy(source.at[at], target.at[at], sem.at[wave])))
+    copies.append((waves - 1, pltpu.make_async_copy(sources[0], held[0], sem.at[waves])))
+    for _, copy in copies:
         copy.start()
-    for copy in copies:
-        copy.wait()
-    rows, columns = raw[2].shape
+    raw = held[1:]
     lat, lon = both_axes()
     lat_even = lax.rem(lat, 2) == 0
     lon_even = lax.rem(lon, 2) == 0
-    step = 32
-    for top in range(0, rows, step):
-        span = pl.ds(top, step)
-        first = slotted(raw_fields(*raw, (span, pl.ds(0, LANES))), depth, 0)
-        last = slotted(raw_fields(*raw, (span, pl.ds(columns - LANES, LANES))), depth, LANES - depth)
-        lon_a[span, :] = jnp.where(lon_even, last, first)
-        lon_b[span, :] = jnp.where(lon_even, first, last)
+    for wave in range(waves):
+        for index, copy in copies:
+            if index == wave:
+                copy.wait()
+        for top in range(wave * step, (wave + 1) * step, 32):
+            span = pl.ds(top, 32)
+            first = slotted(raw_fields(*raw, (span, pl.ds(0, LANES))), depth, 0)
+            last = slotted(raw_fields(*raw, (span, pl.ds(columns - LANES, LANES))), depth, LANES - depth)
+            lon_a[span, :] = jnp.where(lon_even, last, first)
+            lon_b[span, :] = jnp.where(lon_even, first, last)
     for column in range(0, columns, LANES):
         here = pl.ds(column, LANES)
         first = raw_fields(*raw, (pl.ds(0, 16), here))
@@ -109,25 +117,27 @@
         out_b[span, pl.ds(column, LANES)] = jnp.where(lat_even, first, last)
 
 
-def place(live, coef, code_ref, tile, top, size, fields):
+def evolved(fields):
     u, v, a, b, t, fx, fy, strong, code = fields
-    span = pl.ds(top, size)
     code = code.astype(jnp.int32)
     icy = (code & 1).astype(jnp.float32)
-    live[0, tile, span, :] = u
-    live[1, tile, span, :] = v
-    live[2, tile, span, :] = icy * a
-    live[3, tile, span, :] = icy * b
-    live[4, tile, span, :] = icy * t
-    coef[0, tile, span, :] = 0.25 * icy * strong
-    coef[1, tile, span, :] = DAMP * icy
-    coef[2, tile, span, :] = (0.5 * DAMP) * icy * fx
-    coef[3, tile, span, :] = (0.5 * DAMP) * icy * fy
+    kept = [u, v, icy * a, icy * b, icy * t]
+    scales = [0.25 * icy * strong, DAMP * icy, (0.5 * DAMP) * icy * fx, (0.5 * DAMP) * icy * fy]
+    return kept, scales, code
+
+
+def place(live, coef, code_ref, tile, top, size, fields):
+    span = pl.ds(top, size)
+    kept, scales, code = evolved(fields)
+    for field, value in enumerate(kept):
+        live[field, tile, span, :] = value
+    for field, value in enumerate(scales):
+        coef[field, tile, span, :] = value
     code_ref[tile, span, :] = code
 
 
-def prepare_kernel(route, state, forcing, strength, ice, regimes, *refs):
-    inner, band, table = refs[:3], refs[3:6], refs[6]
+def prepare_kernel(depth, route, state, forcing, strength, ice, regimes, *refs):
+    inner, band, table, side = refs[:3], refs[3:6], refs[6], refs[7:]
     lat = lax.axis_index("lat")
     line, lane = (lax.broadcasted_iota(jnp.int32, table.shape, axis) for axis in range(2))
     found = jnp.zeros(table.shape, jnp.int32)
@@ -155,8 +165,15 @@
         clear(band, tile, EDGE + 32, BAND - EDGE - 32)
         clear(band, tiles + 1 + tile, 0, 8)
         clear(band, tiles + 1 + tile, 40, BAND - 40)
-    for tile in range(tiles):
-        for top in range(0, rows, 32):
+    for field in range(5):
+        for top in (0, PAD + rows):
+            side[0][field, 0, pl.ds(top, PAD), :] = jnp.zeros((PAD, LANES), jnp.float32)
+    lane = lane_index(32)
+    own, middle = (2 * depth, LANES // 2)
+    east = (lane >= middle - own) & (lane < middle)
+    for top in range(0, rows, 32):
+        ends = []
+        for tile in range(tiles):
             at = (pl.ds(top, 32), pl.ds(tile * LANES, LANES))
             fields = raw_fields(state, forcing, strength, ice, regimes, at)
             place(*inner, tile, PAD + top, 32, fields)
@@ -164,6 +181,11 @@
                 place(*band, tile, EDGE, 32, fields)
             if top == rows - 32:
                 place(*band, tiles + 1 + tile, 8, 32, fields)
+            if tile in (0, tiles - 1):
+                ends.append(fields)
+        both = zip(ends[0], ends[-1])
+        joined = [jnp.where(lane < own, x, jnp.where(east, roll_to(y, middle), 0.0)) for x, y in both]
+        place(*side, 0, PAD + top, 32, joined)
 
 
 def sweeps(live, coef, code_ref, rings, count, reach):
@@ -239,6 +261,14 @@
     return sum(jnp.where(route[band, j] == target, j, 0) for j in range(route.shape[1]))
 
 
+def soon(blocks):
+    return [*range(blocks - 1, 0, -1)]
+
+
+def later(blocks):
+    return [(hop, None) for hop in range(1, blocks)]
+
+
 def inner_half(block, blocks):
     return pl.multiple_of(jnp.where(block == blocks - 1, 0, HALF), HALF)
 
@@ -271,32 +301,31 @@
 
 
 def sides_kernel(depth, count, blocks, table, lon_a, lon_b, *refs):
-    raw, refs = refs[:5], refs[9:]
-    live, band, outgoing, side = refs[0], refs[1:4], refs[4:-3], refs[-3:]
-    rows, columns = raw[2].shape
-    tiles = columns // LANES
+    refs = refs[7:]
+    live, band, side, outgoing = refs[0], refs[1:4], refs[4:7], refs[7:]
+    rows = lon_a.shape[0]
+    tiles = live.shape[1]
+    columns = tiles * LANES
     rim, _, _ = rim_readers(depth, blocks)
-    own, middle = (2 * depth, LANES // 2)
-
-    def joined(first, last, halo):
-        lane = lane_index(first.shape[0])
-        east = jnp.where(lane < middle, roll_to(last, middle), roll_to(halo, middle))
-        east = jnp.where((lane >= middle - own) & (lane < middle + depth), east, 0.0)
-        return jnp.where(lane < own, first, jnp.where(lane >= LANES - depth, halo, east))
-
-    for field in range(5):
-        for top in (0, PAD + rows):
-            side[0][field, 0, pl.ds(top, PAD), :] = jnp.zeros((PAD, LANES), jnp.float32)
+    middle = LANES // 2
+    lane = lane_index(32)
+    west = lane >= LANES - depth
+    east = (lane >= middle) & (lane < middle + depth)
     for top in range(0, rows, 32):
         span = pl.ds(top, 32)
         halo = rim(lon_a[span, :], lon_b[span, :])
-        first = raw_fields(*raw, (span, pl.ds(0, LANES)))
-        last = raw_fields(*raw, (span, pl.ds(columns - LANES, LANES)))
-        place(*side, 0, PAD + top, 32, [joined(*x) for x in zip(first, last, halo)])
         if top == 0:
             place(*band, tiles, EDGE, 32, halo)
         if top == rows - 32:
             place(*band, 2 * tiles + 1, 8, 32, halo)
+        span = pl.ds(PAD + top, 32)
+        kept, scales, code = evolved(halo)
+        for ref, values in ((side[0], kept), (side[1], scales)):
+            for field, value in enumerate(values):
+                value = jnp.where(west, value, roll_to(value, middle))
+                ref[field, 0, span, :] = jnp.where(west | east, value, ref[field, 0, span, :])
+        code = jnp.where(west, code, roll_to(code, middle))
+        side[2][0, span, :] = jnp.where(west | east, code, side[2][0, span, :])
 
     def reach(cells):
         return range(PAD + (HALF - cells) // 8 * 8, PAD + rows - HALF + cells, 8)
@@ -312,12 +341,12 @@
                 (tiles - 1, roll_to(value, middle), lane >= LANES - depth),
             ):
                 live[field, tile, span, :] = jnp.where(inside, fixed, live[field, tile, span, :])
-    for hop, target in enumerate(outgoing, 2):
+    for hop, target in zip(soon(blocks), outgoing):
         block = table[0, hop]
         emit(live, target, block * (rows // blocks) + inner_half(block, blocks), columns)
 
 
-def outer_kernel(depth, count, blocks, table, lat_a, lat_b, *refs):
+def outer_kernel(depth, count, blocks, table, lat_b, lat_a, *refs):
     refs = refs[4:]
     live, band, outgoing = refs[0], refs[1:4], refs[4:]
     rows, columns = (live.shape[2] - 2 * PAD, lat_a.shape[1])
@@ -340,19 +369,18 @@
         for tile in range(tiles):
             for field in range(5):
                 live[field, tile, pl.ds(PAD + top, HALF), :] = band[0][field, ring + tile, pl.ds(EDGE, HALF), :]
-    for hop, target in enumerate(outgoing[:-2], 2):
+    for (hop, half), target in zip(later(blocks), outgoing):
         block = table[0, hop]
-        emit(live, target, block * tall + outer_half(block, blocks), columns)
-    for half, target in enumerate(outgoing[-2:]):
-        emit(live, target, table[0, 1] * tall + half * HALF, columns)
+        start = outer_half(block, blocks) if half is None else half * HALF
+        emit(live, target, block * tall + start, columns)
 
 
 def collect_kernel(blocks, table, forcing, ice, live, *refs):
-    early, (flux, out, own, sem) = refs[: blocks - 2], refs[blocks - 2 :]
+    early, (flux, out, own, sem) = refs[:-4], refs[-4:]
     rows, columns = ice.shape
     lat = lax.axis_index("lat")
     copies = []
-    for hop, part in enumerate(early, 2):
+    for hop, part in zip(soon(blocks), early):
         start = inner_half(table[1, hop], blocks)
         copies.append(pltpu.make_async_copy(part, out.at[lat ^ hop, :, pl.ds(start, HALF), :], sem.at[hop]))
         copies[-1].start()
@@ -371,12 +399,11 @@
 
 
 def gather_kernel(blocks, table, *refs):
-    late, (_, out, sem) = refs[:blocks], refs[blocks:]
+    late, (_, out, sem) = refs[:-3], refs[-3:]
     lat = lax.axis_index("lat")
     copies = []
-    for index, part in enumerate(late):
-        hop = index + 2 if index < blocks - 2 else 1
-        start = outer_half(table[1, hop], blocks) if hop > 1 else (index - blocks + 2) * HALF
+    for index, ((hop, half), part) in enumerate(zip(later(blocks), late)):
+        start = outer_half(table[1, hop], blocks) if half is None else half * HALF
         copies.append(pltpu.make_async_copy(part, out.at[lat ^ hop, :, pl.ds(start, HALF), :], sem.at[index]))
         copies[-1].start()
     for copy in copies:
@@ -434,23 +461,23 @@
         ]
 
     inner, band = (fields(tiles - 1, rows + 2 * PAD), fields(2 * tiles, BAND))
-    side = [VMEM(x.shape, x.dtype) for x in fields(1, rows + 2 * PAD)]
+    side = fields(1, rows + 2 * PAD)
     whole, half = (shape((5, tall, columns), f32), shape((5, HALF, columns), f32))
     lon_a, lon_b, lat_a, lat_b, route, *raw = pl.pallas_call(
         functools.partial(pack_kernel, depth),
         out_shape=[lon_rim] * 2 + [lat_rim] * 2 + [shape(x.shape, x.dtype) for x in inputs],
         in_specs=[spec(HBM)] * 6,
         out_specs=[spec()] * 10,
-        scratch_shapes=[pltpu.SemaphoreType.DMA((6,))],
+        scratch_shapes=[pltpu.SemaphoreType.DMA((3,))],
         compiler_params=params(),
         name="pack",
     )(*[pltpu.with_memory_space_constraint(x, HBM) for x in inputs])
     lon_a, lon_b = lon_swaps(lon_a, lon_b, lons)
     prepared = pl.pallas_call(
-        prepare_kernel,
-        out_shape=inner + band + [shape((8, LANES), jnp.int32)],
+        functools.partial(prepare_kernel, depth),
+        out_shape=inner + band + [shape((8, LANES), jnp.int32)] + side,
         in_specs=[spec()] * 6,
-        out_specs=[spec()] * 7,
+        out_specs=[spec()] * 10,
         compiler_params=params(),
         cost_estimate=cost(40 * rows * columns, 100 * rows * columns),
         name="prepare",
@@ -481,34 +508,30 @@
 
     live, *rest = pl.pallas_call(
         functools.partial(sides_kernel, depth, count, lats),
-        out_shape=inner[:1] + band + [half] * (lats - 2),
-        in_specs=[spec()] * 12,
-        out_specs=[spec()] * (2 + lats),
-        scratch_shapes=side,
-        input_output_aliases={8 + i: i for i in range(4)},
+        out_shape=inner[:1] + band + side + [half] * len(soon(lats)),
+        in_specs=[spec()] * 10,
+        out_specs=[spec()] * (7 + len(soon(lats))),
+        input_output_aliases={3 + i: i for i in range(7)},
         compiler_params=params(),
         name="sides",
-    )(table, lon_a, lon_b, *raw, live, *prepared[3:6])
-    edges, early = (rest[:3], rest[3:])
-    for hop in range(lats - 1, 1, -1):
-        early[hop - 2] = send(early[hop - 2], hop)
+    )(table, lon_a, lon_b, live, *prepared[3:6], *prepared[7:])
+    edges, early = (rest[:3], rest[6:])
+    early = [send(part, hop) for hop, part in zip(soon(lats), early)]
     live, _, _, _, *late = pl.pallas_call(
         functools.partial(outer_kernel, depth, count, lats),
-        out_shape=inner[:1] + band + [half] * lats,
+        out_shape=inner[:1] + band + [half] * len(later(lats)),
         in_specs=[spec()] * 7,
-        out_specs=[spec()] * (4 + lats),
+        out_specs=[spec()] * (4 + len(later(lats))),
         input_output_aliases={3 + i: i for i in range(4)},
         compiler_params=params(),
         name="outer",
-    )(table, lat_a, lat_b, live, *edges)
-    hops = [*range(2, lats), 1, 1]
-    for index in (*range(lats - 3, -1, -1), lats - 2, lats - 1):
-        late[index] = send(late[index], hops[index])
+    )(table, lat_b, lat_a, live, *edges)
+    late = [send(part, hop) for (hop, _), part in zip(later(lats), late)]
     result = shape((lats, *whole.shape), f32)
     flux, blocks = pl.pallas_call(
         functools.partial(collect_kernel, lats),
         out_shape=[shape((2, rows, columns), f32), result],
-        in_specs=[spec()] * (2 + lats),
+        in_specs=[spec()] * (4 + len(early)),
         out_specs=[spec(), spec(HBM)],
         scratch_shapes=[VMEM(whole.shape, f32), pltpu.SemaphoreType.DMA((lats,))],
         compiler_params=params(),
@@ -517,10 +540,10 @@
     blocks = pl.pallas_call(
         functools.partial(gather_kernel, lats),
         out_shape=result,
-        in_specs=[spec()] * (1 + lats) + [spec(HBM)],
+        in_specs=[spec()] * (1 + len(late)) + [spec(HBM)],
         out_specs=spec(HBM),
-        scratch_shapes=[pltpu.SemaphoreType.DMA((lats,))],
-        input_output_aliases={1 + lats: 0},
+        scratch_shapes=[pltpu.SemaphoreType.DMA((len(late),))],
+        input_output_aliases={1 + len(late): 0},
         compiler_params=params(),
         name="gather",
     )(table, *late, blocks)

time: 30.7 us -> 30.2 us (0.984)
  waiting for transfers between devices: 5.07 us -> 3.27 us
  starting transfers between devices: 15.1 us -> 16.4 us
    ppermute x6, waiting for transfers between devices: 4.98 us -> 3.26 us  [send(): return lax.ppermute(part, 'lat', [(i, i ^ hop) for i in range(lats)])]
    ppermute x2, starting transfers between devices: 1.89 us -> 3.38 us  [lat_swaps(): return (lax.ppermute(a, 'lat', near), lax.ppermute(b, ('lat', 'lon'), far))]
  transfers between devices with their start and end apart: 10 -> 10, of which waited for: 4 -> 3; matrix products, arithmetic and copies ran while one was open for 0% -> 0% of each run, Pallas kernels for 22% -> 23%
where the time goes in v4:
time: 30.2 us; the launch traced here: 30 us
  starting transfers between devices  16.4 us (54%)
  Pallas kernels  9.69 us (32%)
  waiting for transfers between devices  3.27 us (11%)
  between operations  0.71 us (2%)
    ppermute x6, starting transfers between devices, send(): return lax.ppermute(part, 'lat', [(i, i ^ hop) for i in range(lats)])  8.9 us
    ppermute x2, starting transfers between devices, lon_swaps(): return (lax.ppermute(a, 'lon', near), lax.ppermute(b, 'lon', far))  4.07 us
    ppermute x2, starting transfers between devices, lat_swaps(): return (lax.ppermute(a, 'lat', near), lax.ppermute(b, ('lat', 'lon'), far))  3.38 us
    ppermute x6, waiting for transfers between devices, send(): return lax.ppermute(part, 'lat', [(i, i ^ hop) for i in range(lats)])  3.26 us
    pallas_call x1, Pallas kernels, per_device(): pl.pallas_call(functools.partial(pack_kernel, depth), out_shape=[lon_rim]...  1.85 us
    pallas_call x1, Pallas kernels, per_device(): pl.pallas_call(functools.partial(sides_kernel, depth, count, lats), out_s...  1.81 us
    pallas_call x1, Pallas kernels, per_device(): pl.pallas_call(functools.partial(outer_kernel, depth, count, lats), out_s...  1.63 us
    pallas_call x1, Pallas kernels, per_device(): pl.pallas_call(functools.partial(collect_kernel, lats), out_shape=[shape(...  1.59 us
  transfers between devices with their start and end apart: 10, of which 3 were waited for; matrix products, arithmetic and copies ran while one was open for 0% of the time, Pallas kernels for 23%

profile of v4, /device:TPU:0, one launch (start us, length us, event | category | flops | bytes accessed | tf_op | source)
XLA Modules:
  0.0 30.0 jit_solution(8807686213848862292)
XLA Ops:
  0.6 1.8 %pack.1 = (f32[128,128]{1,0:T(8,128)S(1)}, f32[128,128]{1,0:T(8,128)S(1)}, f32[120,256]{1,0:T(8,128)S(1)}, f32[120,256]{1,0:T(8,128)S(1)}, s32[4,4]{1,0:T(4,128)...) custom-call(s32[4,4]{1,0:T(4,128)} %refs_0_.1, ...), custom_call_target="tpu_custom_call" | custom-call | tf_op jit(solution)/shard_map/pack/pallas_call | solution.py:466
  2.5 0.5 %collective-permute-start = (f32[128,128]{1,0:T(8,128)S(1)}, f32[128,128]{1,0:T(8,128)S(1)}, u32[]{:S(2)}, u32[]{:S(2)}) collective-permute-start(f32[128,128]{1,0:T(8,128)S(1)} %get-tuple-element.45), channel_id=1, source_target_pairs={{0,1},{1,0},{2,3},{3,2},{4,5},{5,4},{6,7},{7,6},{8,9},{9,8},{10,11... | collective-permute-start | bytes 196616 | tf_op jit(solution)/shard_map/ppermute | solution.py:428
  3.0 3.6 %collective-permute-start.1 = (f32[128,128]{1,0:T(8,128)S(1)}, f32[128,128]{1,0:T(8,128)S(1)}, u32[]{:S(2)}, u32[]{:S(2)}) collective-permute-start(f32[128,128]{1,0:T(8,128)S(1)} %get-tuple-element.46), channel_id=1, source_target_pairs={{0,7},{1,2},{2,1},{3,4},{4,3},{5,6},{6,5},{7,0},{8,15},{9,10},{10,... | collective-permute-start | bytes 196616 | tf_op jit(solution)/shard_map/ppermute | solution.py:428
  6.6 0.4 %prepare.1 = (f32[5,2,144,128]{3,2,1,0:T(8,128)S(1)}, f32[4,2,144,128]{3,2,1,0:T(8,128)S(1)}, s32[2,144,128]{2,1,0:T(8,128)S(1)}, f32[5,6,64,128]{3,2,1,0:T(8,12...) custom-call(s32[4,4]{1,0:T(4,128)S(1)} %get-tuple-element.38.route, ...), custom_call_target="tpu_custom_call" | custom-call | flops 1310720 | bytes 3276800 | tf_op jit(solution)/shard_map/prepare/pallas_call | solution.py:476
  6.9 1.6 %inner.1 = (f32[5,2,144,128]{3,2,1,0:T(8,128)S(1)}, f32[4,2,144,128]{3,2,1,0:T(8,128)S(1)}, s32[2,144,128]{2,1,0:T(8,128)S(1)}) custom-call(f32[5,2,144,128]{3,2,1,0:T(8,128)S(1)} %get-tuple-element.49.refs_0_, f32[4,2,144,128]{3,2,1,0:T(8,128)S(1)} %get-tuple-element.50.refs_1_, ...), custom_call_target="tpu_custom_call", output_to_operand_aliasing={{0}: (0, {}), {1}: (1, {}), {2}: (2, {})} | custom-call | tf_op jit(solution)/shard_map/inner/pallas_call | solution.py:486
  8.5 0.0 collective-permute-done.lon_a
  8.6 0.0 collective-permute-done.1.lon_b
  8.6 0.1 collective-permute-start.2
  8.7 3.3 %collective-permute-start.3 = (f32[120,256]{1,0:T(8,128)S(1)}, f32[120,256]{1,0:T(8,128)S(1)}, u32[]{:S(2)}, u32[]{:S(2)}) collective-permute-start(f32[120,256]{1,0:T(8,128)S(1)} %get-tuple-element.54), channel_id=1, source_target_pairs={{0,8},{8,0},{16,24},{24,16},{1,9},{9,1},{17,25},{25,17},{2,10},{10... | collective-permute-start | bytes 368648 | tf_op jit(solution)/shard_map/ppermute | solution.py:440
  12.0 1.8 %sides.1 = (f32[5,2,144,128]{3,2,1,0:T(8,128)S(1)}, f32[5,6,64,128]{3,2,1,0:T(8,128)S(1)}, f32[4,6,64,128]{3,2,1,0:T(8,128)S(1)}, s32[6,64,128]{2,1,0:T(8,128)S(...) custom-call(s32[8,128]{1,0:T(8,128)S(1)} %get-tuple-element.44.table, ...), custom_call_target="tpu_custom_call", output_to_operand_aliasing={{0}: (3, {}), {1}: (4, {}), {2}: (5, {}), {3}: (6, {}), {4}... | custom-call | tf_op jit(solution)/shard_map/sides/pallas_call | solution.py:509
  13.8 1.4 %collective-permute-start.4 = (f32[5,16,256]{2,1,0:T(8,128)S(1)}, f32[5,16,256]{2,1,0:T(8,128)S(1)}, u32[]{:S(2)}, u32[]{:S(2)}) collective-permute-start(f32[5,16,256]{2,1,0:T(8,128)S(1)} %get-tuple-element.66), channel_id=1, source_target_pairs={{0,24},{8,16},{16,8},{24,0},{1,25},{9,17},{17,9},{25,1},{2,26},{10... | collective-permute-start | bytes 245768 | tf_op jit(solution)/shard_map/ppermute | solution.py:507
  15.2 0.1 collective-permute-start.5
  15.3 2.9 %collective-permute-start.6 = (f32[5,16,256]{2,1,0:T(8,128)S(1)}, f32[5,16,256]{2,1,0:T(8,128)S(1)}, u32[]{:S(2)}, u32[]{:S(2)}) collective-permute-start(f32[5,16,256]{2,1,0:T(8,128)S(1)} %get-tuple-element.68), channel_id=1, source_target_pairs={{0,8},{8,0},{16,24},{24,16},{1,9},{9,1},{17,25},{25,17},{2,10},{10... | collective-permute-start | bytes 245768 | tf_op jit(solution)/shard_map/ppermute | solution.py:507
  18.2 0.0 collective-permute-done.2.lat_b
  18.3 0.0 collective-permute-done.3.lat_a
  18.3 1.6 %outer.1 = (f32[5,2,144,128]{3,2,1,0:T(8,128)S(1)}, f32[5,6,64,128]{3,2,1,0:T(8,128)S(1)}, f32[4,6,64,128]{3,2,1,0:T(8,128)S(1)}, s32[6,64,128]{2,1,0:T(8,128)S(...) custom-call(s32[8,128]{1,0:T(8,128)S(1)} %get-tuple-element.44.table, ...), custom_call_target="tpu_custom_call", output_to_operand_aliasing={{0}: (3, {}), {1}: (4, {}), {2}: (5, {}), {3}: (6, {})} | custom-call | tf_op jit(solution)/shard_map/outer/pallas_call | solution.py:520
  19.9 0.1 collective-permute-start.7
  20.0 1.9 %collective-permute-start.8 = (f32[5,16,256]{2,1,0:T(8,128)S(1)}, f32[5,16,256]{2,1,0:T(8,128)S(1)}, u32[]{:S(2)}, u32[]{:S(2)}) collective-permute-start(f32[5,16,256]{2,1,0:T(8,128)S(1)} %get-tuple-element.71), channel_id=1, source_target_pairs={{0,16},{8,24},{16,0},{24,8},{1,17},{9,25},{17,1},{25,9},{2,18},{10... | collective-permute-start | bytes 245768 | tf_op jit(solution)/shard_map/ppermute | solution.py:507
  21.9 0.0 collective-permute-done.4.refs_0_
  21.9 2.5 %collective-permute-start.9 = (f32[5,16,256]{2,1,0:T(8,128)S(1)}, f32[5,16,256]{2,1,0:T(8,128)S(1)}, u32[]{:S(2)}, u32[]{:S(2)}) collective-permute-start(f32[5,16,256]{2,1,0:T(8,128)S(1)} %get-tuple-element.72), channel_id=1, source_target_pairs={{0,24},{8,16},{16,8},{24,0},{1,25},{9,17},{17,9},{25,1},{2,26},{10... | collective-permute-start | bytes 245768 | tf_op jit(solution)/shard_map/ppermute | solution.py:507
  24.3 0.0 collective-permute-done.5.refs_1_
  24.3 0.4 %collective-permute-done.6.refs_2_ = f32[5,16,256]{2,1,0:T(8,128)S(1)} collective-permute-done((f32[5,16,256]{2,1,0:T(8,128)S(1)}, f32[5,16,256]{2,1,0:T(8,128)S(1)}, u32[]{:S(2)}, u32[]{:S(2)}) %collective-permute-start.6) | collective-permute-done | bytes 81952 | tf_op jit(solution)/shard_map/ppermute | solution.py:507
  24.8 1.6 %collect.1 = (f32[2,128,256]{2,1,0:T(8,128)}, f32[4,5,32,256]{3,2,1,0:T(8,128)}) custom-call(s32[8,128]{1,0:T(8,128)S(1)} %get-tuple-element.44.table, f32[4,128,256]{2,1,0:T(8,128)S(1)} %get-tuple-element.40.forcing, s32[128,256]{1,0:T(8,128)S(1)} %get-tuple-element.42.ice, f32[5,2,144,128]{3,2,1,0:T(8,128)S(1)} %get-tuple-element.65.live, ...), custom_call_target="tpu_custom_call" | custom-call | tf_op jit(solution)/shard_map/collect/pallas_call | solution.py:531
  26.4 0.7 %collective-permute-done.7.refs_0_ = f32[5,16,256]{2,1,0:T(8,128)S(1)} collective-permute-done((f32[5,16,256]{2,1,0:T(8,128)S(1)}, f32[5,16,256]{2,1,0:T(8,128)S(1)}, u32[]{:S(2)}, u32[]{:S(2)}) %collective-permute-start.7) | collective-permute-done | bytes 81952 | tf_op jit(solution)/shard_map/ppermute | solution.py:507
  27.0 2.2 %collective-permute-done.8.refs_1_ = f32[5,16,256]{2,1,0:T(8,128)S(1)} collective-permute-done((f32[5,16,256]{2,1,0:T(8,128)S(1)}, f32[5,16,256]{2,1,0:T(8,128)S(1)}, u32[]{:S(2)}, u32[]{:S(2)}) %collective-permute-start.8) | collective-permute-done | bytes 81952 | tf_op jit(solution)/shard_map/ppermute | solution.py:507
  29.2 0.0 collective-permute-done.9.refs_2_
  29.2 0.8 %gather.1 = f32[4,5,32,256]{3,2,1,0:T(8,128)} custom-call(s32[8,128]{1,0:T(8,128)S(1)} %get-tuple-element.44.table, f32[5,16,256]{2,1,0:T(8,128)S(1)} %collective-permute-done.7.refs_0_, f32[5,16,256]{2,1,0:T(8,128)S(1)} %collective-permute-done.8.refs_1_, f32[5,16,256]{2,1,0:T(8,128)S(1)} %collective-permute-done.9.refs_2_, ...), custom_call_target="tpu_custom_call", output_to_operand_aliasing={{}: (4, {})} | custom-call | tf_op jit(solution)/shard_map/gather/pallas_call | solution.py:540
  (1 shorter events, 0.0 us)
Async XLA Ops:
  2.5 6.1 %collective-permute-start = (f32[128,128]{1,0:T(8,128)S(1)}, f32[128,128]{1,0:T(8,128)S(1)}, u32[]{:S(2)}, u32[]{:S(2)}) collective-permute-start(f32[128,128]{1,0:T(8,128)S(1)} %get-tuple-element.45), channel_id=1, source_target_pairs={{0,1},{1,0},{2,3},{3,2},{4,5},{5,4},{6,7},{7,6},{8,9},{9,8},{10,11... | collective-permute-start | bytes 196616 | tf_op jit(solution)/shard_map/ppermute | solution.py:428
  3.0 5.5 %collective-permute-start.1 = (f32[128,128]{1,0:T(8,128)S(1)}, f32[128,128]{1,0:T(8,128)S(1)}, u32[]{:S(2)}, u32[]{:S(2)}) collective-permute-start(f32[128,128]{1,0:T(8,128)S(1)} %get-tuple-element.46), channel_id=1, source_target_pairs={{0,7},{1,2},{2,1},{3,4},{4,3},{5,6},{6,5},{7,0},{8,15},{9,10},{10,... | collective-permute-start | bytes 196616 | tf_op jit(solution)/shard_map/ppermute | solution.py:428
  8.6 9.7 %collective-permute-start.2 = (f32[120,256]{1,0:T(8,128)S(1)}, f32[120,256]{1,0:T(8,128)S(1)}, u32[]{:S(2)}, u32[]{:S(2)}) collective-permute-start(f32[120,256]{1,0:T(8,128)S(1)} %get-tuple-element.53), channel_id=1, source_target_pairs={{0,1},{1,0},{2,3},{3,2},{4,5},{5,4},{6,7},{7,6},{8,16},{9,17},{10,... | collective-permute-start | bytes 368648 | tf_op jit(solution)/shard_map/ppermute | solution.py:440
  8.7 9.6 %collective-permute-start.3 = (f32[120,256]{1,0:T(8,128)S(1)}, f32[120,256]{1,0:T(8,128)S(1)}, u32[]{:S(2)}, u32[]{:S(2)}) collective-permute-start(f32[120,256]{1,0:T(8,128)S(1)} %get-tuple-element.54), channel_id=1, source_target_pairs={{0,8},{8,0},{16,24},{24,16},{1,9},{9,1},{17,25},{25,17},{2,10},{10... | collective-permute-start | bytes 368648 | tf_op jit(solution)/shard_map/ppermute | solution.py:440
  13.8 8.1 %collective-permute-start.4 = (f32[5,16,256]{2,1,0:T(8,128)S(1)}, f32[5,16,256]{2,1,0:T(8,128)S(1)}, u32[]{:S(2)}, u32[]{:S(2)}) collective-permute-start(f32[5,16,256]{2,1,0:T(8,128)S(1)} %get-tuple-element.66), channel_id=1, source_target_pairs={{0,24},{8,16},{16,8},{24,0},{1,25},{9,17},{17,9},{25,1},{2,26},{10... | collective-permute-start | bytes 245768 | tf_op jit(solution)/shard_map/ppermute | solution.py:507
  15.2 9.1 %collective-permute-start.5 = (f32[5,16,256]{2,1,0:T(8,128)S(1)}, f32[5,16,256]{2,1,0:T(8,128)S(1)}, u32[]{:S(2)}, u32[]{:S(2)}) collective-permute-start(f32[5,16,256]{2,1,0:T(8,128)S(1)} %get-tuple-element.67), channel_id=1, source_target_pairs={{0,16},{8,24},{16,0},{24,8},{1,17},{9,25},{17,1},{25,9},{2,18},{10... | collective-permute-start | bytes 245768 | tf_op jit(solution)/shard_map/ppermute | solution.py:507
  15.3 9.4 %collective-permute-start.6 = (f32[5,16,256]{2,1,0:T(8,128)S(1)}, f32[5,16,256]{2,1,0:T(8,128)S(1)}, u32[]{:S(2)}, u32[]{:S(2)}) collective-permute-start(f32[5,16,256]{2,1,0:T(8,128)S(1)} %get-tuple-element.68), channel_id=1, source_target_pairs={{0,8},{8,0},{16,24},{24,16},{1,9},{9,1},{17,25},{25,17},{2,10},{10... | collective-permute-start | bytes 245768 | tf_op jit(solution)/shard_map/ppermute | solution.py:507
  19.9 7.2 %collective-permute-start.7 = (f32[5,16,256]{2,1,0:T(8,128)S(1)}, f32[5,16,256]{2,1,0:T(8,128)S(1)}, u32[]{:S(2)}, u32[]{:S(2)}) collective-permute-start(f32[5,16,256]{2,1,0:T(8,128)S(1)} %get-tuple-element.70), channel_id=1, source_target_pairs={{0,8},{8,0},{16,24},{24,16},{1,9},{9,1},{17,25},{25,17},{2,10},{10... | collective-permute-start | bytes 245768 | tf_op jit(solution)/shard_map/ppermute | solution.py:507
  20.0 9.2 %collective-permute-start.8 = (f32[5,16,256]{2,1,0:T(8,128)S(1)}, f32[5,16,256]{2,1,0:T(8,128)S(1)}, u32[]{:S(2)}, u32[]{:S(2)}) collective-permute-start(f32[5,16,256]{2,1,0:T(8,128)S(1)} %get-tuple-element.71), channel_id=1, source_target_pairs={{0,16},{8,24},{16,0},{24,8},{1,17},{9,25},{17,1},{25,9},{2,18},{10... | collective-permute-start | bytes 245768 | tf_op jit(solution)/shard_map/ppermute | solution.py:507
  21.9 7.3 %collective-permute-start.9 = (f32[5,16,256]{2,1,0:T(8,128)S(1)}, f32[5,16,256]{2,1,0:T(8,128)S(1)}, u32[]{:S(2)}, u32[]{:S(2)}) collective-permute-start(f32[5,16,256]{2,1,0:T(8,128)S(1)} %get-tuple-element.72), channel_id=1, source_target_pairs={{0,24},{8,16},{16,8},{24,0},{1,25},{9,17},{17,9},{25,1},{2,26},{10... | collective-permute-start | bytes 245768 | tf_op jit(solution)/shard_map/ppermute | solution.py:507

commit v5 on v4

--- a/solution.py
+++ b/solution.py
@@ -266,7 +266,7 @@
 
 
 def later(blocks):
-    return [(hop, None) for hop in range(1, blocks)]
+    return [2, 1, *range(3, blocks)]
 
 
 def inner_half(block, blocks):
@@ -369,10 +369,9 @@
         for tile in range(tiles):
             for field in range(5):
                 live[field, tile, pl.ds(PAD + top, HALF), :] = band[0][field, ring + tile, pl.ds(EDGE, HALF), :]
-    for (hop, half), target in zip(later(blocks), outgoing):
+    for hop, target in zip(later(blocks), outgoing):
         block = table[0, hop]
-        start = outer_half(block, blocks) if half is None else half * HALF
-        emit(live, target, block * tall + start, columns)
+        emit(live, target, block * tall + outer_half(block, blocks), columns)
 
 
 def collect_kernel(blocks, table, forcing, ice, live, *refs):
@@ -402,9 +401,9 @@
     late, (_, out, sem) = refs[:-3], refs[-3:]
     lat = lax.axis_index("lat")
     copies = []
-    for index, ((hop, half), part) in enumerate(zip(later(blocks), late)):
-        start = outer_half(table[1, hop], blocks) if half is None else half * HALF
-        copies.append(pltpu.make_async_copy(part, out.at[lat ^ hop, :, pl.ds(start, HALF), :], sem.at[index]))
+    for hop, part in zip(later(blocks), late):
+        start = outer_half(table[1, hop], blocks)
+        copies.append(pltpu.make_async_copy(part, out.at[lat ^ hop, :, pl.ds(start, HALF), :], sem.at[hop - 1]))
         copies[-1].start()
     for copy in copies:
         copy.wait()
@@ -526,7 +525,7 @@
         compiler_params=params(),
         name="outer",
     )(table, lat_b, lat_a, live, *edges)
-    late = [send(part, hop) for (hop, _), part in zip(later(lats), late)]
+    late = [send(part, hop) for hop, part in zip(later(lats), late)]
     result = shape((lats, *whole.shape), f32)
     flux, blocks = pl.pallas_call(
         functools.partial(collect_kernel, lats),

time: 30.2 us -> 29.8 us (0.987)
  waiting for transfers between devices: 3.27 us -> 2.85 us
    ppermute x6, waiting for transfers between devices: 3.26 us -> 2.84 us  [send(): return lax.ppermute(part, 'lat', [(i, i ^ hop) for i in range(lats)])]
  transfers between devices with their start and end apart: 10 -> 10, of which waited for: 3 -> 1; matrix products, arithmetic and copies ran while one was open for 0% -> 0% of each run, Pallas kernels for 23% -> 24%
where the time goes in v5:
time: 29.8 us; the launch traced here: 29.6 us
  starting transfers between devices  16.4 us (55%)
  Pallas kernels  9.7 us (33%)
  waiting for transfers between devices  2.85 us (10%)
  between operations  0.71 us (2%)
    ppermute x6, starting transfers between devices, send(): return lax.ppermute(part, 'lat', [(i, i ^ hop) for i in range(lats)])  8.91 us
    ppermute x2, starting transfers between devices, lon_swaps(): return (lax.ppermute(a, 'lon', near), lax.ppermute(b, 'lon', far))  4.07 us
    ppermute x2, starting transfers between devices, lat_swaps(): return (lax.ppermute(a, 'lat', near), lax.ppermute(b, ('lat', 'lon'), far))  3.38 us
    ppermute x6, waiting for transfers between devices, send(): return lax.ppermute(part, 'lat', [(i, i ^ hop) for i in range(lats)])  2.84 us
    pallas_call x1, Pallas kernels, per_device(): pl.pallas_call(functools.partial(pack_kernel, depth), out_shape=[lon_rim]...  1.85 us
    pallas_call x1, Pallas kernels, per_device(): pl.pallas_call(functools.partial(sides_kernel, depth, count, lats), out_s...  1.81 us
    pallas_call x1, Pallas kernels, per_device(): pl.pallas_call(functools.partial(outer_kernel, depth, count, lats), out_s...  1.63 us
    pallas_call x1, Pallas kernels, per_device(): pl.pallas_call(functools.partial(collect_kernel, lats), out_shape=[shape(...  1.6 us
  transfers between devices with their start and end apart: 10, of which 1 were waited for; matrix products, arithmetic and copies ran while one was open for 0% of the time, Pallas kernels for 24%

profile of v5, /device:TPU:0, one launch (start us, length us, event | category | flops | bytes accessed | tf_op | source)
XLA Modules:
  0.0 29.6 jit_solution(15948741944549037511)
XLA Ops:
  0.6 1.8 %pack.1 = (f32[128,128]{1,0:T(8,128)S(1)}, f32[128,128]{1,0:T(8,128)S(1)}, f32[120,256]{1,0:T(8,128)S(1)}, f32[120,256]{1,0:T(8,128)S(1)}, s32[4,4]{1,0:T(4,128)...) custom-call(s32[4,4]{1,0:T(4,128)} %refs_0_.1, ...), custom_call_target="tpu_custom_call" | custom-call | tf_op jit(solution)/shard_map/pack/pallas_call | solution.py:465
  2.5 0.5 %collective-permute-start = (f32[128,128]{1,0:T(8,128)S(1)}, f32[128,128]{1,0:T(8,128)S(1)}, u32[]{:S(2)}, u32[]{:S(2)}) collective-permute-start(f32[128,128]{1,0:T(8,128)S(1)} %get-tuple-element.45), channel_id=1, source_target_pairs={{0,1},{1,0},{2,3},{3,2},{4,5},{5,4},{6,7},{7,6},{8,9},{9,8},{10,11... | collective-permute-start | bytes 196616 | tf_op jit(solution)/shard_map/ppermute | solution.py:427
  3.0 3.6 %collective-permute-start.1 = (f32[128,128]{1,0:T(8,128)S(1)}, f32[128,128]{1,0:T(8,128)S(1)}, u32[]{:S(2)}, u32[]{:S(2)}) collective-permute-start(f32[128,128]{1,0:T(8,128)S(1)} %get-tuple-element.46), channel_id=1, source_target_pairs={{0,7},{1,2},{2,1},{3,4},{4,3},{5,6},{6,5},{7,0},{8,15},{9,10},{10,... | collective-permute-start | bytes 196616 | tf_op jit(solution)/shard_map/ppermute | solution.py:427
  6.6 0.4 %prepare.1 = (f32[5,2,144,128]{3,2,1,0:T(8,128)S(1)}, f32[4,2,144,128]{3,2,1,0:T(8,128)S(1)}, s32[2,144,128]{2,1,0:T(8,128)S(1)}, f32[5,6,64,128]{3,2,1,0:T(8,12...) custom-call(s32[4,4]{1,0:T(4,128)S(1)} %get-tuple-element.38.route, ...), custom_call_target="tpu_custom_call" | custom-call | flops 1310720 | bytes 3276800 | tf_op jit(solution)/shard_map/prepare/pallas_call | solution.py:475
  6.9 1.6 %inner.1 = (f32[5,2,144,128]{3,2,1,0:T(8,128)S(1)}, f32[4,2,144,128]{3,2,1,0:T(8,128)S(1)}, s32[2,144,128]{2,1,0:T(8,128)S(1)}) custom-call(f32[5,2,144,128]{3,2,1,0:T(8,128)S(1)} %get-tuple-element.49.refs_0_, f32[4,2,144,128]{3,2,1,0:T(8,128)S(1)} %get-tuple-element.50.refs_1_, ...), custom_call_target="tpu_custom_call", output_to_operand_aliasing={{0}: (0, {}), {1}: (1, {}), {2}: (2, {})} | custom-call | tf_op jit(solution)/shard_map/inner/pallas_call | solution.py:485
  8.5 0.0 collective-permute-done.lon_a
  8.6 0.0 collective-permute-done.1.lon_b
  8.6 0.1 collective-permute-start.2
  8.7 3.3 %collective-permute-start.3 = (f32[120,256]{1,0:T(8,128)S(1)}, f32[120,256]{1,0:T(8,128)S(1)}, u32[]{:S(2)}, u32[]{:S(2)}) collective-permute-start(f32[120,256]{1,0:T(8,128)S(1)} %get-tuple-element.54), channel_id=1, source_target_pairs={{0,8},{8,0},{16,24},{24,16},{1,9},{9,1},{17,25},{25,17},{2,10},{10... | collective-permute-start | bytes 368648 | tf_op jit(solution)/shard_map/ppermute | solution.py:439
  12.0 1.8 %sides.1 = (f32[5,2,144,128]{3,2,1,0:T(8,128)S(1)}, f32[5,6,64,128]{3,2,1,0:T(8,128)S(1)}, f32[4,6,64,128]{3,2,1,0:T(8,128)S(1)}, s32[6,64,128]{2,1,0:T(8,128)S(...) custom-call(s32[8,128]{1,0:T(8,128)S(1)} %get-tuple-element.44.table, ...), custom_call_target="tpu_custom_call", output_to_operand_aliasing={{0}: (3, {}), {1}: (4, {}), {2}: (5, {}), {3}: (6, {}), {4}... | custom-call | tf_op jit(solution)/shard_map/sides/pallas_call | solution.py:508
  13.8 1.4 %collective-permute-start.4 = (f32[5,16,256]{2,1,0:T(8,128)S(1)}, f32[5,16,256]{2,1,0:T(8,128)S(1)}, u32[]{:S(2)}, u32[]{:S(2)}) collective-permute-start(f32[5,16,256]{2,1,0:T(8,128)S(1)} %get-tuple-element.66), channel_id=1, source_target_pairs={{0,24},{8,16},{16,8},{24,0},{1,25},{9,17},{17,9},{25,1},{2,26},{10... | collective-permute-start | bytes 245768 | tf_op jit(solution)/shard_map/ppermute | solution.py:506
  15.2 0.1 collective-permute-start.5
  15.3 2.9 %collective-permute-start.6 = (f32[5,16,256]{2,1,0:T(8,128)S(1)}, f32[5,16,256]{2,1,0:T(8,128)S(1)}, u32[]{:S(2)}, u32[]{:S(2)}) collective-permute-start(f32[5,16,256]{2,1,0:T(8,128)S(1)} %get-tuple-element.68), channel_id=1, source_target_pairs={{0,8},{8,0},{16,24},{24,16},{1,9},{9,1},{17,25},{25,17},{2,10},{10... | collective-permute-start | bytes 245768 | tf_op jit(solution)/shard_map/ppermute | solution.py:506
  18.2 0.0 collective-permute-done.2.lat_b
  18.3 0.0 collective-permute-done.3.lat_a
  18.3 1.6 %outer.1 = (f32[5,2,144,128]{3,2,1,0:T(8,128)S(1)}, f32[5,6,64,128]{3,2,1,0:T(8,128)S(1)}, f32[4,6,64,128]{3,2,1,0:T(8,128)S(1)}, s32[6,64,128]{2,1,0:T(8,128)S(...) custom-call(s32[8,128]{1,0:T(8,128)S(1)} %get-tuple-element.44.table, ...), custom_call_target="tpu_custom_call", output_to_operand_aliasing={{0}: (3, {}), {1}: (4, {}), {2}: (5, {}), {3}: (6, {})} | custom-call | tf_op jit(solution)/shard_map/outer/pallas_call | solution.py:519
  19.9 0.3 collective-permute-start.7
  20.2 1.7 %collective-permute-start.8 = (f32[5,16,256]{2,1,0:T(8,128)S(1)}, f32[5,16,256]{2,1,0:T(8,128)S(1)}, u32[]{:S(2)}, u32[]{:S(2)}) collective-permute-start(f32[5,16,256]{2,1,0:T(8,128)S(1)} %get-tuple-element.71), channel_id=1, source_target_pairs={{0,8},{8,0},{16,24},{24,16},{1,9},{9,1},{17,25},{25,17},{2,10},{10... | collective-permute-start | bytes 245768 | tf_op jit(solution)/shard_map/ppermute | solution.py:506
  21.9 0.0 collective-permute-done.4.refs_0_
  21.9 2.5 %collective-permute-start.9 = (f32[5,16,256]{2,1,0:T(8,128)S(1)}, f32[5,16,256]{2,1,0:T(8,128)S(1)}, u32[]{:S(2)}, u32[]{:S(2)}) collective-permute-start(f32[5,16,256]{2,1,0:T(8,128)S(1)} %get-tuple-element.72), channel_id=1, source_target_pairs={{0,24},{8,16},{16,8},{24,0},{1,25},{9,17},{17,9},{25,1},{2,26},{10... | collective-permute-start | bytes 245768 | tf_op jit(solution)/shard_map/ppermute | solution.py:506
  24.3 0.0 collective-permute-done.5.refs_1_
  24.4 0.0 collective-permute-done.6.refs_2_
  24.4 1.6 %collect.1 = (f32[2,128,256]{2,1,0:T(8,128)}, f32[4,5,32,256]{3,2,1,0:T(8,128)}) custom-call(s32[8,128]{1,0:T(8,128)S(1)} %get-tuple-element.44.table, f32[4,128,256]{2,1,0:T(8,128)S(1)} %get-tuple-element.40.forcing, s32[128,256]{1,0:T(8,128)S(1)} %get-tuple-element.42.ice, f32[5,2,144,128]{3,2,1,0:T(8,128)S(1)} %get-tuple-element.65.live, ...), custom_call_target="tpu_custom_call" | custom-call | tf_op jit(solution)/shard_map/collect/pallas_call | solution.py:530
  26.0 2.8 %collective-permute-done.7.refs_0_ = f32[5,16,256]{2,1,0:T(8,128)S(1)} collective-permute-done((f32[5,16,256]{2,1,0:T(8,128)S(1)}, f32[5,16,256]{2,1,0:T(8,128)S(1)}, u32[]{:S(2)}, u32[]{:S(2)}) %collective-permute-start.7) | collective-permute-done | bytes 81952 | tf_op jit(solution)/shard_map/ppermute | solution.py:506
  28.8 0.0 collective-permute-done.8.refs_1_
  28.8 0.0 collective-permute-done.9.refs_2_
  28.8 0.8 %gather.1 = f32[4,5,32,256]{3,2,1,0:T(8,128)} custom-call(s32[8,128]{1,0:T(8,128)S(1)} %get-tuple-element.44.table, f32[5,16,256]{2,1,0:T(8,128)S(1)} %collective-permute-done.7.refs_0_, f32[5,16,256]{2,1,0:T(8,128)S(1)} %collective-permute-done.8.refs_1_, f32[5,16,256]{2,1,0:T(8,128)S(1)} %collective-permute-done.9.refs_2_, ...), custom_call_target="tpu_custom_call", output_to_operand_aliasing={{}: (4, {})} | custom-call | tf_op jit(solution)/shard_map/gather/pallas_call | solution.py:539
  (1 shorter events, 0.0 us)
Async XLA Ops:
  2.5 6.1 %collective-permute-start = (f32[128,128]{1,0:T(8,128)S(1)}, f32[128,128]{1,0:T(8,128)S(1)}, u32[]{:S(2)}, u32[]{:S(2)}) collective-permute-start(f32[128,128]{1,0:T(8,128)S(1)} %get-tuple-element.45), channel_id=1, source_target_pairs={{0,1},{1,0},{2,3},{3,2},{4,5},{5,4},{6,7},{7,6},{8,9},{9,8},{10,11... | collective-permute-start | bytes 196616 | tf_op jit(solution)/shard_map/ppermute | solution.py:427
  3.0 5.5 %collective-permute-start.1 = (f32[128,128]{1,0:T(8,128)S(1)}, f32[128,128]{1,0:T(8,128)S(1)}, u32[]{:S(2)}, u32[]{:S(2)}) collective-permute-start(f32[128,128]{1,0:T(8,128)S(1)} %get-tuple-element.46), channel_id=1, source_target_pairs={{0,7},{1,2},{2,1},{3,4},{4,3},{5,6},{6,5},{7,0},{8,15},{9,10},{10,... | collective-permute-start | bytes 196616 | tf_op jit(solution)/shard_map/ppermute | solution.py:427
  8.6 9.7 %collective-permute-start.2 = (f32[120,256]{1,0:T(8,128)S(1)}, f32[120,256]{1,0:T(8,128)S(1)}, u32[]{:S(2)}, u32[]{:S(2)}) collective-permute-start(f32[120,256]{1,0:T(8,128)S(1)} %get-tuple-element.53), channel_id=1, source_target_pairs={{0,1},{1,0},{2,3},{3,2},{4,5},{5,4},{6,7},{7,6},{8,16},{9,17},{10,... | collective-permute-start | bytes 368648 | tf_op jit(solution)/shard_map/ppermute | solution.py:439
  8.7 9.6 %collective-permute-start.3 = (f32[120,256]{1,0:T(8,128)S(1)}, f32[120,256]{1,0:T(8,128)S(1)}, u32[]{:S(2)}, u32[]{:S(2)}) collective-permute-start(f32[120,256]{1,0:T(8,128)S(1)} %get-tuple-element.54), channel_id=1, source_target_pairs={{0,8},{8,0},{16,24},{24,16},{1,9},{9,1},{17,25},{25,17},{2,10},{10... | collective-permute-start | bytes 368648 | tf_op jit(solution)/shard_map/ppermute | solution.py:439
  13.8 8.1 %collective-permute-start.4 = (f32[5,16,256]{2,1,0:T(8,128)S(1)}, f32[5,16,256]{2,1,0:T(8,128)S(1)}, u32[]{:S(2)}, u32[]{:S(2)}) collective-permute-start(f32[5,16,256]{2,1,0:T(8,128)S(1)} %get-tuple-element.66), channel_id=1, source_target_pairs={{0,24},{8,16},{16,8},{24,0},{1,25},{9,17},{17,9},{25,1},{2,26},{10... | collective-permute-start | bytes 245768 | tf_op jit(solution)/shard_map/ppermute | solution.py:506
  15.2 9.1 %collective-permute-start.5 = (f32[5,16,256]{2,1,0:T(8,128)S(1)}, f32[5,16,256]{2,1,0:T(8,128)S(1)}, u32[]{:S(2)}, u32[]{:S(2)}) collective-permute-start(f32[5,16,256]{2,1,0:T(8,128)S(1)} %get-tuple-element.67), channel_id=1, source_target_pairs={{0,16},{8,24},{16,0},{24,8},{1,17},{9,25},{17,1},{25,9},{2,18},{10... | collective-permute-start | bytes 245768 | tf_op jit(solution)/shard_map/ppermute | solution.py:506
  15.3 9.0 %collective-permute-start.6 = (f32[5,16,256]{2,1,0:T(8,128)S(1)}, f32[5,16,256]{2,1,0:T(8,128)S(1)}, u32[]{:S(2)}, u32[]{:S(2)}) collective-permute-start(f32[5,16,256]{2,1,0:T(8,128)S(1)} %get-tuple-element.68), channel_id=1, source_target_pairs={{0,8},{8,0},{16,24},{24,16},{1,9},{9,1},{17,25},{25,17},{2,10},{10... | collective-permute-start | bytes 245768 | tf_op jit(solution)/shard_map/ppermute | solution.py:506
  19.9 8.9 %collective-permute-start.7 = (f32[5,16,256]{2,1,0:T(8,128)S(1)}, f32[5,16,256]{2,1,0:T(8,128)S(1)}, u32[]{:S(2)}, u32[]{:S(2)}) collective-permute-start(f32[5,16,256]{2,1,0:T(8,128)S(1)} %get-tuple-element.70), channel_id=1, source_target_pairs={{0,16},{8,24},{16,0},{24,8},{1,17},{9,25},{17,1},{25,9},{2,18},{10... | collective-permute-start | bytes 245768 | tf_op jit(solution)/shard_map/ppermute | solution.py:506
  20.2 8.6 %collective-permute-start.8 = (f32[5,16,256]{2,1,0:T(8,128)S(1)}, f32[5,16,256]{2,1,0:T(8,128)S(1)}, u32[]{:S(2)}, u32[]{:S(2)}) collective-permute-start(f32[5,16,256]{2,1,0:T(8,128)S(1)} %get-tuple-element.71), channel_id=1, source_target_pairs={{0,8},{8,0},{16,24},{24,16},{1,9},{9,1},{17,25},{25,17},{2,10},{10... | collective-permute-start | bytes 245768 | tf_op jit(solution)/shard_map/ppermute | solution.py:506
  21.9 6.9 %collective-permute-start.9 = (f32[5,16,256]{2,1,0:T(8,128)S(1)}, f32[5,16,256]{2,1,0:T(8,128)S(1)}, u32[]{:S(2)}, u32[]{:S(2)}) collective-permute-start(f32[5,16,256]{2,1,0:T(8,128)S(1)} %get-tuple-element.72), channel_id=1, source_target_pairs={{0,24},{8,16},{16,8},{24,0},{1,25},{9,17},{17,9},{25,1},{2,26},{10... | collective-permute-start | bytes 245768 | tf_op jit(solution)/shard_map/ppermute | solution.py:506

commit v6 on v5

--- a/solution.py
+++ b/solution.py
@@ -40,6 +40,12 @@
         strength[at],
         code.astype(jnp.float32),
     ]
+
+
+def rim_rows(depth):
+    depths = [depth] * 2 + [depth - 1] * 3 + [depth - 2] * 2 + [depth - 1] * 2
+    starts = [sum(depths[:field]) for field in range(FIELDS + 1)]
+    return depths, starts
 
 
 def both_axes():
@@ -95,13 +101,14 @@
             last = slotted(raw_fields(*raw, (span, pl.ds(columns - LANES, LANES))), depth, LANES - depth)
             lon_a[span, :] = jnp.where(lon_even, last, first)
             lon_b[span, :] = jnp.where(lon_even, first, last)
+    depths, starts = rim_rows(depth)
     for column in range(0, columns, LANES):
         here = pl.ds(column, LANES)
         first = raw_fields(*raw, (pl.ds(0, 16), here))
         last = raw_fields(*raw, (pl.ds(rows - 16, 16), here))
-        for field in range(FIELDS):
-            span = pl.ds(depth * field, depth)
-            one, two = (first[field][:depth], last[field][16 - depth :])
+        for field, size in enumerate(depths):
+            span = pl.ds(starts[field], size)
+            one, two = (first[field][:size], last[field][16 - size :])
             lat_a[span, here] = jnp.where(lat_even, two, one)
             lat_b[span, here] = jnp.where(lat_even, one, two)
 
@@ -109,7 +116,7 @@
 def corner_kernel(depth, lon_a, lon_b, lat_a, lat_b, after, out_a, out_b):
     rows = lon_a.shape[0]
     lat_even = lax.rem(lax.axis_index("lat"), 2) == 0
-    span = pl.ds(depth * FIELDS, depth)
+    span = pl.ds(rim_rows(depth)[1][-1], depth)
     for source, column in ((lon_a, 0), (lon_b, LANES)):
         first = source[pl.ds(0, 16), :][:depth]
         last = source[pl.ds(rows - 16, 16), :][16 - depth :]
@@ -188,7 +195,7 @@
         place(*side, 0, PAD + top, 32, joined)
 
 
-def sweeps(live, coef, code_ref, rings, count, reach):
+def sweeps(live, coef, code_ref, rings, count):
     size = 8
     lane = lane_index(size)
     first_lane = lane == 0
@@ -213,7 +220,7 @@
 
     for level in range(count):
         left = 2 * (count - level)
-        for ring in rings:
+        for ring, reach in rings:
             for top in reach(left - 1):
                 span = pl.ds(top, size)
                 for tile, du_dx, dv_dx in zip(ring, across(0, ring, top), across(1, ring, top)):
@@ -226,7 +233,7 @@
                     live[2, tile, span, :] = 0.5 * row(2, tile, top) + (scale * (du_dx + half) - base)
                     live[3, tile, span, :] = 0.5 * row(3, tile, top) + (scale * (dv_dy + half) - base)
                     live[4, tile, span, :] = 0.5 * (row(4, tile, top) + scale * (du_dy + dv_dx))
-        for ring in rings:
+        for ring, reach in rings:
             for top in reach(left - 2):
                 span = pl.ds(top, size)
                 for tile, da_dx, dt_dx in zip(ring, across(2, ring, top), across(4, ring, top)):
@@ -289,15 +296,15 @@
             target[field, :, pl.ds(tile * LANES, LANES)] = value
 
 
-def inner_kernel(count, *refs):
+def inner_kernel(depth, count, *refs):
     inner = refs[3:]
     _, tiles, high, _ = inner[0].shape
     rows = high - 2 * PAD
 
     def reach(cells):
-        return range(PAD + (HALF - cells) // 8 * 8, PAD + rows - HALF + cells, 8)
-
-    sweeps(*inner, [range(tiles)], count, reach)
+        return range(PAD + (depth - cells) // 8 * 8, PAD + rows - depth + cells, 8)
+
+    sweeps(*inner, [(range(tiles), reach)], count)
 
 
 def sides_kernel(depth, count, blocks, table, lon_a, lon_b, *refs):
@@ -328,12 +335,12 @@
         side[2][0, span, :] = jnp.where(west | east, code, side[2][0, span, :])
 
     def reach(cells):
-        return range(PAD + (HALF - cells) // 8 * 8, PAD + rows - HALF + cells, 8)
-
-    sweeps(*side, [[0]], count, reach)
-    lane = lane_index(16)
-    for top in range(HALF, rows - HALF, 16):
-        span = pl.ds(PAD + top, 16)
+        return range(PAD + (depth - cells) // 8 * 8, PAD + rows - depth + cells, 8)
+
+    sweeps(*side, [([0], reach)], count)
+    lane = lane_index(8)
+    for top in range(depth // 8 * 8, rows - depth // 8 * 8, 8):
+        span = pl.ds(PAD + top, 8)
         for field in range(5):
             value = side[0][field, 0, span, :]
             for tile, fixed, inside in (
@@ -353,22 +360,27 @@
     tiles = columns // LANES
     tall = rows // blocks
     rim, from_north, from_south = rim_readers(depth, blocks)
-    spans = [pl.ds(depth * f, depth) for f in range(FIELDS + 1)]
-    for ring, top, chosen in ((0, EDGE - depth, from_north), (tiles + 1, 40, from_south)):
+    depths, starts = rim_rows(depth)
+    south = [pl.ds(start, depth) for start in starts]
+    north = [pl.ds(start + size - depth, depth) for start, size in zip(starts, depths)]
+    for ring, top, chosen, spans in ((0, EDGE - depth, from_north, north), (tiles + 1, 40, from_south, south[:-1])):
         for tile in range(tiles):
             here = pl.ds(tile * LANES, LANES)
-            place(*band, ring + tile, top, depth, [chosen(lat_a[s, here], lat_b[s, here]) for s in spans[:-1]])
-        pair = [chosen(lat_a[spans[-1], pl.ds(c, LANES)], lat_b[spans[-1], pl.ds(c, LANES)]) for c in (0, LANES)]
+            place(*band, ring + tile, top, depth, [chosen(lat_a[s, here], lat_b[s, here]) for s in spans])
+        ends = south[-1]
+        pair = [chosen(lat_a[ends, pl.ds(c, LANES)], lat_b[ends, pl.ds(c, LANES)]) for c in (0, LANES)]
         place(*band, ring + tiles, top, depth, rim(*pair))
 
-    def reach(cells):
-        return range((EDGE - cells) // 8 * 8, EDGE + HALF + cells, 8)
-
-    sweeps(*band, [range(tiles + 1), range(tiles + 1, 2 * tiles + 2)], count, reach)
-    for ring, top in ((0, 0), (tiles + 1, rows - HALF)):
+    def reach_from(start):
+        return lambda cells: range((start - cells) // 8 * 8, start + depth + cells, 8)
+
+    below = 40 - depth
+    rings = [(range(tiles + 1), reach_from(EDGE)), (range(tiles + 1, 2 * tiles + 2), reach_from(below))]
+    sweeps(*band, rings, count)
+    for ring, top, start in ((0, 0, EDGE), (tiles + 1, rows - depth, below)):
         for tile in range(tiles):
             for field in range(5):
-                live[field, tile, pl.ds(PAD + top, HALF), :] = band[0][field, ring + tile, pl.ds(EDGE, HALF), :]
+                live[field, tile, pl.ds(PAD + top, depth), :] = band[0][field, ring + tile, pl.ds(start, depth), :]
     for hop, target in zip(later(blocks), outgoing):
         block = table[0, hop]
         emit(live, target, block * tall + outer_half(block, blocks), columns)
@@ -449,7 +461,7 @@
     inputs = (ice_route, ice_state, ocean_forcing, ice_strength, ice_mask, yield_mask)
     shape = jax.ShapeDtypeStruct
     lon_rim = shape((rows, LANES), f32)
-    lat_rim = shape((depth * (FIELDS + 1), columns), f32)
+    lat_rim = shape((rim_rows(depth)[1][-1] + depth, columns), f32)
     tiles = columns // LANES + 1
 
     def fields(tiles, rows):
@@ -483,7 +495,7 @@
     )(route, *raw)
     table = prepared[6]
     live, _, _ = pl.pallas_call(
-        functools.partial(inner_kernel, count),
+        functools.partial(inner_kernel, depth, count),
         out_shape=inner,
         in_specs=[spec()] * 3,
         out_specs=[spec()] * 3,

time: 29.8 us -> 29.7 us (level)
  no operation moved by 1% of the time
where the time goes in v6:
time: 29.7 us; the launch traced here: 29.6 us
  starting transfers between devices  16.3 us (55%)
  Pallas kernels  9.68 us (33%)
  waiting for transfers between devices  2.93 us (10%)
  between operations  0.71 us (2%)
    ppermute x6, starting transfers between devices, send(): return lax.ppermute(part, 'lat', [(i, i ^ hop) for i in range(lats)])  8.91 us
    ppermute x2, starting transfers between devices, lon_swaps(): return (lax.ppermute(a, 'lon', near), lax.ppermute(b, 'lon', far))  4.07 us
    ppermute x2, starting transfers between devices, lat_swaps(): return (lax.ppermute(a, 'lat', near), lax.ppermute(b, ('lat', 'lon'), far))  3.28 us
    ppermute x6, waiting for transfers between devices, send(): return lax.ppermute(part, 'lat', [(i, i ^ hop) for i in range(lats)])  2.92 us
    pallas_call x1, Pallas kernels, per_device(): pl.pallas_call(functools.partial(pack_kernel, depth), out_shape=[lon_rim]...  1.85 us
    pallas_call x1, Pallas kernels, per_device(): pl.pallas_call(functools.partial(sides_kernel, depth, count, lats), out_s...  1.83 us
    pallas_call x1, Pallas kernels, per_device(): pl.pallas_call(functools.partial(inner_kernel, depth, count), out_shape=i...  1.7 us
    pallas_call x1, Pallas kernels, per_device(): pl.pallas_call(functools.partial(collect_kernel, lats), out_shape=[shape(...  1.6 us
  transfers between devices with their start and end apart: 10, of which 1 were waited for; matrix products, arithmetic and copies ran while one was open for 0% of the time, Pallas kernels for 24%

profile of v6, /device:TPU:0, one launch (start us, length us, event | category | flops | bytes accessed | tf_op | source)
XLA Modules:
  0.0 29.6 jit_solution(12409775453395596886)
XLA Ops:
  0.6 1.9 %pack.1 = (f32[128,128]{1,0:T(8,128)S(1)}, f32[128,128]{1,0:T(8,128)S(1)}, f32[111,256]{1,0:T(8,128)S(1)}, f32[111,256]{1,0:T(8,128)S(1)}, s32[4,4]{1,0:T(4,128)...) custom-call(s32[4,4]{1,0:T(4,128)} %refs_0_.1, ...), custom_call_target="tpu_custom_call" | custom-call | tf_op jit(solution)/shard_map/pack/pallas_call | solution.py:477
  2.5 0.5 %collective-permute-start = (f32[128,128]{1,0:T(8,128)S(1)}, f32[128,128]{1,0:T(8,128)S(1)}, u32[]{:S(2)}, u32[]{:S(2)}) collective-permute-start(f32[128,128]{1,0:T(8,128)S(1)} %get-tuple-element.45), channel_id=1, source_target_pairs={{0,1},{1,0},{2,3},{3,2},{4,5},{5,4},{6,7},{7,6},{8,9},{9,8},{10,11... | collective-permute-start | bytes 196616 | tf_op jit(solution)/shard_map/ppermute | solution.py:439
  3.0 3.6 %collective-permute-start.1 = (f32[128,128]{1,0:T(8,128)S(1)}, f32[128,128]{1,0:T(8,128)S(1)}, u32[]{:S(2)}, u32[]{:S(2)}) collective-permute-start(f32[128,128]{1,0:T(8,128)S(1)} %get-tuple-element.46), channel_id=1, source_target_pairs={{0,7},{1,2},{2,1},{3,4},{4,3},{5,6},{6,5},{7,0},{8,15},{9,10},{10,... | collective-permute-start | bytes 196616 | tf_op jit(solution)/shard_map/ppermute | solution.py:439
  6.6 0.4 %prepare.1 = (f32[5,2,144,128]{3,2,1,0:T(8,128)S(1)}, f32[4,2,144,128]{3,2,1,0:T(8,128)S(1)}, s32[2,144,128]{2,1,0:T(8,128)S(1)}, f32[5,6,64,128]{3,2,1,0:T(8,12...) custom-call(s32[4,4]{1,0:T(4,128)S(1)} %get-tuple-element.38.route, ...), custom_call_target="tpu_custom_call" | custom-call | flops 1310720 | bytes 3276800 | tf_op jit(solution)/shard_map/prepare/pallas_call | solution.py:487
  7.0 1.7 %inner.1 = (f32[5,2,144,128]{3,2,1,0:T(8,128)S(1)}, f32[4,2,144,128]{3,2,1,0:T(8,128)S(1)}, s32[2,144,128]{2,1,0:T(8,128)S(1)}) custom-call(f32[5,2,144,128]{3,2,1,0:T(8,128)S(1)} %get-tuple-element.49.refs_0_, f32[4,2,144,128]{3,2,1,0:T(8,128)S(1)} %get-tuple-element.50.refs_1_, ...), custom_call_target="tpu_custom_call", output_to_operand_aliasing={{0}: (0, {}), {1}: (1, {}), {2}: (2, {})} | custom-call | tf_op jit(solution)/shard_map/inner/pallas_call | solution.py:497
  8.7 0.0 collective-permute-done.lon_a
  8.7 0.0 collective-permute-done.1.lon_b
  8.7 0.1 collective-permute-start.2
  8.8 3.2 %collective-permute-start.3 = (f32[111,256]{1,0:T(8,128)S(1)}, f32[111,256]{1,0:T(8,128)S(1)}, u32[]{:S(2)}, u32[]{:S(2)}) collective-permute-start(f32[111,256]{1,0:T(8,128)S(1)} %get-tuple-element.54), channel_id=1, source_target_pairs={{0,8},{8,0},{16,24},{24,16},{1,9},{9,1},{17,25},{25,17},{2,10},{10... | collective-permute-start | bytes 341000 | tf_op jit(solution)/shard_map/ppermute | solution.py:451
  12.0 1.8 %sides.1 = (f32[5,2,144,128]{3,2,1,0:T(8,128)S(1)}, f32[5,6,64,128]{3,2,1,0:T(8,128)S(1)}, f32[4,6,64,128]{3,2,1,0:T(8,128)S(1)}, s32[6,64,128]{2,1,0:T(8,128)S(...) custom-call(s32[8,128]{1,0:T(8,128)S(1)} %get-tuple-element.44.table, ...), custom_call_target="tpu_custom_call", output_to_operand_aliasing={{0}: (3, {}), {1}: (4, {}), {2}: (5, {}), {3}: (6, {}), {4}... | custom-call | tf_op jit(solution)/shard_map/sides/pallas_call | solution.py:520
  13.8 1.4 %collective-permute-start.4 = (f32[5,16,256]{2,1,0:T(8,128)S(1)}, f32[5,16,256]{2,1,0:T(8,128)S(1)}, u32[]{:S(2)}, u32[]{:S(2)}) collective-permute-start(f32[5,16,256]{2,1,0:T(8,128)S(1)} %get-tuple-element.66), channel_id=1, source_target_pairs={{0,24},{8,16},{16,8},{24,0},{1,25},{9,17},{17,9},{25,1},{2,26},{10... | collective-permute-start | bytes 245768 | tf_op jit(solution)/shard_map/ppermute | solution.py:518
  15.2 0.1 collective-permute-start.5
  15.4 2.9 %collective-permute-start.6 = (f32[5,16,256]{2,1,0:T(8,128)S(1)}, f32[5,16,256]{2,1,0:T(8,128)S(1)}, u32[]{:S(2)}, u32[]{:S(2)}) collective-permute-start(f32[5,16,256]{2,1,0:T(8,128)S(1)} %get-tuple-element.68), channel_id=1, source_target_pairs={{0,8},{8,0},{16,24},{24,16},{1,9},{9,1},{17,25},{25,17},{2,10},{10... | collective-permute-start | bytes 245768 | tf_op jit(solution)/shard_map/ppermute | solution.py:518
  18.3 0.0 collective-permute-done.2.lat_b
  18.3 0.0 collective-permute-done.3.lat_a
  18.3 1.5 %outer.1 = (f32[5,2,144,128]{3,2,1,0:T(8,128)S(1)}, f32[5,6,64,128]{3,2,1,0:T(8,128)S(1)}, f32[4,6,64,128]{3,2,1,0:T(8,128)S(1)}, s32[6,64,128]{2,1,0:T(8,128)S(...) custom-call(s32[8,128]{1,0:T(8,128)S(1)} %get-tuple-element.44.table, ...), custom_call_target="tpu_custom_call", output_to_operand_aliasing={{0}: (3, {}), {1}: (4, {}), {2}: (5, {}), {3}: (6, {})} | custom-call | tf_op jit(solution)/shard_map/outer/pallas_call | solution.py:531
  19.8 0.3 collective-permute-start.7
  20.1 1.7 %collective-permute-start.8 = (f32[5,16,256]{2,1,0:T(8,128)S(1)}, f32[5,16,256]{2,1,0:T(8,128)S(1)}, u32[]{:S(2)}, u32[]{:S(2)}) collective-permute-start(f32[5,16,256]{2,1,0:T(8,128)S(1)} %get-tuple-element.71), channel_id=1, source_target_pairs={{0,8},{8,0},{16,24},{24,16},{1,9},{9,1},{17,25},{25,17},{2,10},{10... | collective-permute-start | bytes 245768 | tf_op jit(solution)/shard_map/ppermute | solution.py:518
  21.7 0.0 collective-permute-done.4.refs_0_
  21.7 2.5 %collective-permute-start.9 = (f32[5,16,256]{2,1,0:T(8,128)S(1)}, f32[5,16,256]{2,1,0:T(8,128)S(1)}, u32[]{:S(2)}, u32[]{:S(2)}) collective-permute-start(f32[5,16,256]{2,1,0:T(8,128)S(1)} %get-tuple-element.72), channel_id=1, source_target_pairs={{0,24},{8,16},{16,8},{24,0},{1,25},{9,17},{17,9},{25,1},{2,26},{10... | collective-permute-start | bytes 245768 | tf_op jit(solution)/shard_map/ppermute | solution.py:518
  24.2 0.0 collective-permute-done.5.refs_1_
  24.2 0.0 collective-permute-done.6.refs_2_
  24.2 1.6 %collect.1 = (f32[2,128,256]{2,1,0:T(8,128)}, f32[4,5,32,256]{3,2,1,0:T(8,128)}) custom-call(s32[8,128]{1,0:T(8,128)S(1)} %get-tuple-element.44.table, f32[4,128,256]{2,1,0:T(8,128)S(1)} %get-tuple-element.40.forcing, s32[128,256]{1,0:T(8,128)S(1)} %get-tuple-element.42.ice, f32[5,2,144,128]{3,2,1,0:T(8,128)S(1)} %get-tuple-element.65.live, ...), custom_call_target="tpu_custom_call" | custom-call | tf_op jit(solution)/shard_map/collect/pallas_call | solution.py:542
  25.8 2.9 %collective-permute-done.7.refs_0_ = f32[5,16,256]{2,1,0:T(8,128)S(1)} collective-permute-done((f32[5,16,256]{2,1,0:T(8,128)S(1)}, f32[5,16,256]{2,1,0:T(8,128)S(1)}, u32[]{:S(2)}, u32[]{:S(2)}) %collective-permute-start.7) | collective-permute-done | bytes 81952 | tf_op jit(solution)/shard_map/ppermute | solution.py:518
  28.7 0.0 collective-permute-done.8.refs_1_
  28.8 0.0 collective-permute-done.9.refs_2_
  28.8 0.8 %gather.1 = f32[4,5,32,256]{3,2,1,0:T(8,128)} custom-call(s32[8,128]{1,0:T(8,128)S(1)} %get-tuple-element.44.table, f32[5,16,256]{2,1,0:T(8,128)S(1)} %collective-permute-done.7.refs_0_, f32[5,16,256]{2,1,0:T(8,128)S(1)} %collective-permute-done.8.refs_1_, f32[5,16,256]{2,1,0:T(8,128)S(1)} %collective-permute-done.9.refs_2_, ...), custom_call_target="tpu_custom_call", output_to_operand_aliasing={{}: (4, {})} | custom-call | tf_op jit(solution)/shard_map/gather/pallas_call | solution.py:551
  (1 shorter events, 0.0 us)
Async XLA Ops:
  2.5 6.2 %collective-permute-start = (f32[128,128]{1,0:T(8,128)S(1)}, f32[128,128]{1,0:T(8,128)S(1)}, u32[]{:S(2)}, u32[]{:S(2)}) collective-permute-start(f32[128,128]{1,0:T(8,128)S(1)} %get-tuple-element.45), channel_id=1, source_target_pairs={{0,1},{1,0},{2,3},{3,2},{4,5},{5,4},{6,7},{7,6},{8,9},{9,8},{10,11... | collective-permute-start | bytes 196616 | tf_op jit(solution)/shard_map/ppermute | solution.py:439
  3.0 5.7 %collective-permute-start.1 = (f32[128,128]{1,0:T(8,128)S(1)}, f32[128,128]{1,0:T(8,128)S(1)}, u32[]{:S(2)}, u32[]{:S(2)}) collective-permute-start(f32[128,128]{1,0:T(8,128)S(1)} %get-tuple-element.46), channel_id=1, source_target_pairs={{0,7},{1,2},{2,1},{3,4},{4,3},{5,6},{6,5},{7,0},{8,15},{9,10},{10,... | collective-permute-start | bytes 196616 | tf_op jit(solution)/shard_map/ppermute | solution.py:439
  8.7 9.6 %collective-permute-start.2 = (f32[111,256]{1,0:T(8,128)S(1)}, f32[111,256]{1,0:T(8,128)S(1)}, u32[]{:S(2)}, u32[]{:S(2)}) collective-permute-start(f32[111,256]{1,0:T(8,128)S(1)} %get-tuple-element.53), channel_id=1, source_target_pairs={{0,1},{1,0},{2,3},{3,2},{4,5},{5,4},{6,7},{7,6},{8,16},{9,17},{10,... | collective-permute-start | bytes 341000 | tf_op jit(solution)/shard_map/ppermute | solution.py:451
  8.8 9.5 %collective-permute-start.3 = (f32[111,256]{1,0:T(8,128)S(1)}, f32[111,256]{1,0:T(8,128)S(1)}, u32[]{:S(2)}, u32[]{:S(2)}) collective-permute-start(f32[111,256]{1,0:T(8,128)S(1)} %get-tuple-element.54), channel_id=1, source_target_pairs={{0,8},{8,0},{16,24},{24,16},{1,9},{9,1},{17,25},{25,17},{2,10},{10... | collective-permute-start | bytes 341000 | tf_op jit(solution)/shard_map/ppermute | solution.py:451
  13.8 7.9 %collective-permute-start.4 = (f32[5,16,256]{2,1,0:T(8,128)S(1)}, f32[5,16,256]{2,1,0:T(8,128)S(1)}, u32[]{:S(2)}, u32[]{:S(2)}) collective-permute-start(f32[5,16,256]{2,1,0:T(8,128)S(1)} %get-tuple-element.66), channel_id=1, source_target_pairs={{0,24},{8,16},{16,8},{24,0},{1,25},{9,17},{17,9},{25,1},{2,26},{10... | collective-permute-start | bytes 245768 | tf_op jit(solution)/shard_map/ppermute | solution.py:518
  15.2 9.0 %collective-permute-start.5 = (f32[5,16,256]{2,1,0:T(8,128)S(1)}, f32[5,16,256]{2,1,0:T(8,128)S(1)}, u32[]{:S(2)}, u32[]{:S(2)}) collective-permute-start(f32[5,16,256]{2,1,0:T(8,128)S(1)} %get-tuple-element.67), channel_id=1, source_target_pairs={{0,16},{8,24},{16,0},{24,8},{1,17},{9,25},{17,1},{25,9},{2,18},{10... | collective-permute-start | bytes 245768 | tf_op jit(solution)/shard_map/ppermute | solution.py:518
  15.4 8.9 %collective-permute-start.6 = (f32[5,16,256]{2,1,0:T(8,128)S(1)}, f32[5,16,256]{2,1,0:T(8,128)S(1)}, u32[]{:S(2)}, u32[]{:S(2)}) collective-permute-start(f32[5,16,256]{2,1,0:T(8,128)S(1)} %get-tuple-element.68), channel_id=1, source_target_pairs={{0,8},{8,0},{16,24},{24,16},{1,9},{9,1},{17,25},{25,17},{2,10},{10... | collective-permute-start | bytes 245768 | tf_op jit(solution)/shard_map/ppermute | solution.py:518
  19.8 9.0 %collective-permute-start.7 = (f32[5,16,256]{2,1,0:T(8,128)S(1)}, f32[5,16,256]{2,1,0:T(8,128)S(1)}, u32[]{:S(2)}, u32[]{:S(2)}) collective-permute-start(f32[5,16,256]{2,1,0:T(8,128)S(1)} %get-tuple-element.70), channel_id=1, source_target_pairs={{0,16},{8,24},{16,0},{24,8},{1,17},{9,25},{17,1},{25,9},{2,18},{10... | collective-permute-start | bytes 245768 | tf_op jit(solution)/shard_map/ppermute | solution.py:518
  20.1 8.7 %collective-permute-start.8 = (f32[5,16,256]{2,1,0:T(8,128)S(1)}, f32[5,16,256]{2,1,0:T(8,128)S(1)}, u32[]{:S(2)}, u32[]{:S(2)}) collective-permute-start(f32[5,16,256]{2,1,0:T(8,128)S(1)} %get-tuple-element.71), channel_id=1, source_target_pairs={{0,8},{8,0},{16,24},{24,16},{1,9},{9,1},{17,25},{25,17},{2,10},{10... | collective-permute-start | bytes 245768 | tf_op jit(solution)/shard_map/ppermute | solution.py:518
  21.7 7.0 %collective-permute-start.9 = (f32[5,16,256]{2,1,0:T(8,128)S(1)}, f32[5,16,256]{2,1,0:T(8,128)S(1)}, u32[]{:S(2)}, u32[]{:S(2)}) collective-permute-start(f32[5,16,256]{2,1,0:T(8,128)S(1)} %get-tuple-element.72), channel_id=1, source_target_pairs={{0,24},{8,16},{16,8},{24,0},{1,25},{9,17},{17,9},{25,1},{2,26},{10... | collective-permute-start | bytes 245768 | tf_op jit(solution)/shard_map/ppermute | solution.py:518

commit v7 on v5

--- a/solution.py
+++ b/solution.py
@@ -289,8 +289,9 @@
             target[field, :, pl.ds(tile * LANES, LANES)] = value
 
 
-def inner_kernel(count, *refs):
-    inner = refs[3:]
+def inner_kernel(depth, count, *refs):
+    prepare_kernel(depth, *refs)
+    inner = refs[6:9]
     _, tiles, high, _ = inner[0].shape
     rows = high - 2 * PAD
 
@@ -473,24 +474,16 @@
     )(*[pltpu.with_memory_space_constraint(x, HBM) for x in inputs])
     lon_a, lon_b = lon_swaps(lon_a, lon_b, lons)
     prepared = pl.pallas_call(
-        functools.partial(prepare_kernel, depth),
+        functools.partial(inner_kernel, depth, count),
         out_shape=inner + band + [shape((8, LANES), jnp.int32)] + side,
         in_specs=[spec()] * 6,
         out_specs=[spec()] * 10,
         compiler_params=params(),
         cost_estimate=cost(40 * rows * columns, 100 * rows * columns),
-        name="prepare",
+        name="inner",
     )(route, *raw)
     table = prepared[6]
-    live, _, _ = pl.pallas_call(
-        functools.partial(inner_kernel, count),
-        out_shape=inner,
-        in_specs=[spec()] * 3,
-        out_specs=[spec()] * 3,
-        input_output_aliases={i: i for i in range(3)},
-        compiler_params=params(),
-        name="inner",
-    )(*prepared[:3])
+    live = prepared[0]
     lat_a, lat_b = pl.pallas_call(
         functools.partial(corner_kernel, depth),
         out_shape=[lat_rim] * 2,

time: 29.8 us -> 30.2 us (1.013)
  Pallas kernels: 9.7 us -> 10.5 us
    pallas_call x2 -> x1, Pallas kernels: 1.97 us -> 2.74 us  [per_device(): pl.pallas_call(functools.partial(inner_kernel, depth, count), out_shape=i...]
  transfers between devices with their start and end apart: 10 -> 10, of which waited for: 1 -> 2; matrix products, arithmetic and copies ran while one was open for 0% -> 0% of each run, Pallas kernels for 24% -> 26%
where the time goes in v7:
time: 30.2 us; the launch traced here: 30.1 us
  starting transfers between devices  16.2 us (54%)
  Pallas kernels  10.5 us (35%)
  waiting for transfers between devices  2.73 us (9%)
  between operations  0.68 us (2%)
    ppermute x6, starting transfers between devices, send(): return lax.ppermute(part, 'lat', [(i, i ^ hop) for i in range(lats)])  8.91 us
    ppermute x2, starting transfers between devices, lon_swaps(): return (lax.ppermute(a, 'lon', near), lax.ppermute(b, 'lon', far))  4.07 us
    ppermute x2, starting transfers between devices, lat_swaps(): return (lax.ppermute(a, 'lat', near), lax.ppermute(b, ('lat', 'lon'), far))  3.21 us
    pallas_call x1, Pallas kernels, per_device(): pl.pallas_call(functools.partial(inner_kernel, depth, count), out_shape=i...  2.74 us
    ppermute x6, waiting for transfers between devices, send(): return lax.ppermute(part, 'lat', [(i, i ^ hop) for i in range(lats)])  2.72 us
    pallas_call x1, Pallas kernels, per_device(): pl.pallas_call(functools.partial(pack_kernel, depth), out_shape=[lon_rim]...  1.85 us
    pallas_call x1, Pallas kernels, per_device(): pl.pallas_call(functools.partial(sides_kernel, depth, count, lats), out_s...  1.81 us
    pallas_call x1, Pallas kernels, per_device(): pl.pallas_call(functools.partial(outer_kernel, depth, count, lats), out_s...  1.63 us
  transfers between devices with their start and end apart: 10, of which 2 were waited for; matrix products, arithmetic and copies ran while one was open for 0% of the time, Pallas kernels for 26%

profile of v7, /device:TPU:0, one launch (start us, length us, event | category | flops | bytes accessed | tf_op | source)
XLA Modules:
  0.0 30.1 jit_solution(13827118996467280340)
XLA Ops:
  0.6 1.9 %pack.1 = (f32[128,128]{1,0:T(8,128)S(1)}, f32[128,128]{1,0:T(8,128)S(1)}, f32[120,256]{1,0:T(8,128)S(1)}, f32[120,256]{1,0:T(8,128)S(1)}, s32[4,4]{1,0:T(4,128)...) custom-call(s32[4,4]{1,0:T(4,128)} %refs_0_.1, ...), custom_call_target="tpu_custom_call" | custom-call | tf_op jit(solution)/shard_map/pack/pallas_call | solution.py:466
  2.5 0.5 %collective-permute-start = (f32[128,128]{1,0:T(8,128)S(1)}, f32[128,128]{1,0:T(8,128)S(1)}, u32[]{:S(2)}, u32[]{:S(2)}) collective-permute-start(f32[128,128]{1,0:T(8,128)S(1)} %get-tuple-element.42), channel_id=1, source_target_pairs={{0,1},{1,0},{2,3},{3,2},{4,5},{5,4},{6,7},{7,6},{8,9},{9,8},{10,11... | collective-permute-start | bytes 196616 | tf_op jit(solution)/shard_map/ppermute | solution.py:428
  3.0 3.6 %collective-permute-start.1 = (f32[128,128]{1,0:T(8,128)S(1)}, f32[128,128]{1,0:T(8,128)S(1)}, u32[]{:S(2)}, u32[]{:S(2)}) collective-permute-start(f32[128,128]{1,0:T(8,128)S(1)} %get-tuple-element.43), channel_id=1, source_target_pairs={{0,7},{1,2},{2,1},{3,4},{4,3},{5,6},{6,5},{7,0},{8,15},{9,10},{10,... | collective-permute-start | bytes 196616 | tf_op jit(solution)/shard_map/ppermute | solution.py:428
  6.6 2.7 %inner.1 = (f32[5,2,144,128]{3,2,1,0:T(8,128)S(1)}, f32[4,2,144,128]{3,2,1,0:T(8,128)}, s32[2,144,128]{2,1,0:T(8,128)}, f32[5,6,64,128]{3,2,1,0:T(8,128)S(1)}, f...) custom-call(s32[4,4]{1,0:T(4,128)S(1)} %get-tuple-element.35.refs_0_, ...), custom_call_target="tpu_custom_call" | custom-call | flops 1310720 | bytes 3276800 | tf_op jit(solution)/shard_map/inner/pallas_call | solution.py:476
  9.3 0.0 collective-permute-done.lon_a
  9.3 0.0 collective-permute-done.1.lon_b
  9.3 0.1 collective-permute-start.2
  9.4 3.1 %collective-permute-start.3 = (f32[120,256]{1,0:T(8,128)S(1)}, f32[120,256]{1,0:T(8,128)S(1)}, u32[]{:S(2)}, u32[]{:S(2)}) collective-permute-start(f32[120,256]{1,0:T(8,128)S(1)} %get-tuple-element.48), channel_id=1, source_target_pairs={{0,8},{8,0},{16,24},{24,16},{1,9},{9,1},{17,25},{25,17},{2,10},{10... | collective-permute-start | bytes 368648 | tf_op jit(solution)/shard_map/ppermute | solution.py:440
  12.6 1.8 %sides.1 = (f32[5,2,144,128]{3,2,1,0:T(8,128)S(1)}, f32[5,6,64,128]{3,2,1,0:T(8,128)S(1)}, f32[4,6,64,128]{3,2,1,0:T(8,128)S(1)}, s32[6,64,128]{2,1,0:T(8,128)S(...) custom-call(s32[8,128]{1,0:T(8,128)S(1)} %get-tuple-element.41.table, ...), custom_call_target="tpu_custom_call", output_to_operand_aliasing={{0}: (3, {}), {1}: (4, {}), {2}: (5, {}), {3}: (6, {}), {4}... | custom-call | tf_op jit(solution)/shard_map/sides/pallas_call | solution.py:501
  14.4 1.4 %collective-permute-start.4 = (f32[5,16,256]{2,1,0:T(8,128)S(1)}, f32[5,16,256]{2,1,0:T(8,128)S(1)}, u32[]{:S(2)}, u32[]{:S(2)}) collective-permute-start(f32[5,16,256]{2,1,0:T(8,128)S(1)} %get-tuple-element.60), channel_id=1, source_target_pairs={{0,24},{8,16},{16,8},{24,0},{1,25},{9,17},{17,9},{25,1},{2,26},{10... | collective-permute-start | bytes 245768 | tf_op jit(solution)/shard_map/ppermute | solution.py:499
  15.8 0.1 collective-permute-start.5
  15.9 2.9 %collective-permute-start.6 = (f32[5,16,256]{2,1,0:T(8,128)S(1)}, f32[5,16,256]{2,1,0:T(8,128)S(1)}, u32[]{:S(2)}, u32[]{:S(2)}) collective-permute-start(f32[5,16,256]{2,1,0:T(8,128)S(1)} %get-tuple-element.62), channel_id=1, source_target_pairs={{0,8},{8,0},{16,24},{24,16},{1,9},{9,1},{17,25},{25,17},{2,10},{10... | collective-permute-start | bytes 245768 | tf_op jit(solution)/shard_map/ppermute | solution.py:499
  18.8 0.0 collective-permute-done.2.lat_b
  18.8 0.0 collective-permute-done.3.lat_a
  18.8 1.6 %outer.1 = (f32[5,2,144,128]{3,2,1,0:T(8,128)S(1)}, f32[5,6,64,128]{3,2,1,0:T(8,128)S(1)}, f32[4,6,64,128]{3,2,1,0:T(8,128)S(1)}, s32[6,64,128]{2,1,0:T(8,128)S(...) custom-call(s32[8,128]{1,0:T(8,128)S(1)} %get-tuple-element.41.table, ...), custom_call_target="tpu_custom_call", output_to_operand_aliasing={{0}: (3, {}), {1}: (4, {}), {2}: (5, {}), {3}: (6, {})} | custom-call | tf_op jit(solution)/shard_map/outer/pallas_call | solution.py:512
  20.5 0.3 collective-permute-start.7
  20.7 1.7 %collective-permute-start.8 = (f32[5,16,256]{2,1,0:T(8,128)S(1)}, f32[5,16,256]{2,1,0:T(8,128)S(1)}, u32[]{:S(2)}, u32[]{:S(2)}) collective-permute-start(f32[5,16,256]{2,1,0:T(8,128)S(1)} %get-tuple-element.65), channel_id=1, source_target_pairs={{0,8},{8,0},{16,24},{24,16},{1,9},{9,1},{17,25},{25,17},{2,10},{10... | collective-permute-start | bytes 245768 | tf_op jit(solution)/shard_map/ppermute | solution.py:499
  22.4 0.0 collective-permute-done.4.refs_0_
  22.4 2.5 %collective-permute-start.9 = (f32[5,16,256]{2,1,0:T(8,128)S(1)}, f32[5,16,256]{2,1,0:T(8,128)S(1)}, u32[]{:S(2)}, u32[]{:S(2)}) collective-permute-start(f32[5,16,256]{2,1,0:T(8,128)S(1)} %get-tuple-element.66), channel_id=1, source_target_pairs={{0,24},{8,16},{16,8},{24,0},{1,25},{9,17},{17,9},{25,1},{2,26},{10... | collective-permute-start | bytes 245768 | tf_op jit(solution)/shard_map/ppermute | solution.py:499
  24.9 0.1 collective-permute-done.5.refs_1_
  25.0 0.0 collective-permute-done.6.refs_2_
  25.0 1.6 %collect.1 = (f32[2,128,256]{2,1,0:T(8,128)}, f32[4,5,32,256]{3,2,1,0:T(8,128)}) custom-call(s32[8,128]{1,0:T(8,128)S(1)} %get-tuple-element.41.table, f32[4,128,256]{2,1,0:T(8,128)S(1)} %get-tuple-element.37.refs_2_.forcing, s32[128,256]{1,0:T(8,128)S(1)} %get-tuple-element.39.refs_4_.ice, f32[5,2,144,128]{3,2,1,0:T(8,128)S(1)} %get-tuple-element.59.live, ...), custom_call_target="tpu_custom_call" | custom-call | tf_op jit(solution)/shard_map/collect/pallas_call | solution.py:523
  26.6 2.6 %collective-permute-done.7.refs_0_ = f32[5,16,256]{2,1,0:T(8,128)S(1)} collective-permute-done((f32[5,16,256]{2,1,0:T(8,128)S(1)}, f32[5,16,256]{2,1,0:T(8,128)S(1)}, u32[]{:S(2)}, u32[]{:S(2)}) %collective-permute-start.7) | collective-permute-done | bytes 81952 | tf_op jit(solution)/shard_map/ppermute | solution.py:499
  29.2 0.0 collective-permute-done.8.refs_1_
  29.2 0.0 collective-permute-done.9.refs_2_
  29.2 0.8 %gather.1 = f32[4,5,32,256]{3,2,1,0:T(8,128)} custom-call(s32[8,128]{1,0:T(8,128)S(1)} %get-tuple-element.41.table, f32[5,16,256]{2,1,0:T(8,128)S(1)} %collective-permute-done.7.refs_0_, f32[5,16,256]{2,1,0:T(8,128)S(1)} %collective-permute-done.8.refs_1_, f32[5,16,256]{2,1,0:T(8,128)S(1)} %collective-permute-done.9.refs_2_, ...), custom_call_target="tpu_custom_call", output_to_operand_aliasing={{}: (4, {})} | custom-call | tf_op jit(solution)/shard_map/gather/pallas_call | solution.py:532
  (1 shorter events, 0.0 us)
Async XLA Ops:
  2.5 6.8 %collective-permute-start = (f32[128,128]{1,0:T(8,128)S(1)}, f32[128,128]{1,0:T(8,128)S(1)}, u32[]{:S(2)}, u32[]{:S(2)}) collective-permute-start(f32[128,128]{1,0:T(8,128)S(1)} %get-tuple-element.42), channel_id=1, source_target_pairs={{0,1},{1,0},{2,3},{3,2},{4,5},{5,4},{6,7},{7,6},{8,9},{9,8},{10,11... | collective-permute-start | bytes 196616 | tf_op jit(solution)/shard_map/ppermute | solution.py:428
  3.0 6.3 %collective-permute-start.1 = (f32[128,128]{1,0:T(8,128)S(1)}, f32[128,128]{1,0:T(8,128)S(1)}, u32[]{:S(2)}, u32[]{:S(2)}) collective-permute-start(f32[128,128]{1,0:T(8,128)S(1)} %get-tuple-element.43), channel_id=1, source_target_pairs={{0,7},{1,2},{2,1},{3,4},{4,3},{5,6},{6,5},{7,0},{8,15},{9,10},{10,... | collective-permute-start | bytes 196616 | tf_op jit(solution)/shard_map/ppermute | solution.py:428
  9.3 9.5 %collective-permute-start.2 = (f32[120,256]{1,0:T(8,128)S(1)}, f32[120,256]{1,0:T(8,128)S(1)}, u32[]{:S(2)}, u32[]{:S(2)}) collective-permute-start(f32[120,256]{1,0:T(8,128)S(1)} %get-tuple-element.47), channel_id=1, source_target_pairs={{0,1},{1,0},{2,3},{3,2},{4,5},{5,4},{6,7},{7,6},{8,16},{9,17},{10,... | collective-permute-start | bytes 368648 | tf_op jit(solution)/shard_map/ppermute | solution.py:440
  9.4 9.4 %collective-permute-start.3 = (f32[120,256]{1,0:T(8,128)S(1)}, f32[120,256]{1,0:T(8,128)S(1)}, u32[]{:S(2)}, u32[]{:S(2)}) collective-permute-start(f32[120,256]{1,0:T(8,128)S(1)} %get-tuple-element.48), channel_id=1, source_target_pairs={{0,8},{8,0},{16,24},{24,16},{1,9},{9,1},{17,25},{25,17},{2,10},{10... | collective-permute-start | bytes 368648 | tf_op jit(solution)/shard_map/ppermute | solution.py:440
  14.4 8.1 %collective-permute-start.4 = (f32[5,16,256]{2,1,0:T(8,128)S(1)}, f32[5,16,256]{2,1,0:T(8,128)S(1)}, u32[]{:S(2)}, u32[]{:S(2)}) collective-permute-start(f32[5,16,256]{2,1,0:T(8,128)S(1)} %get-tuple-element.60), channel_id=1, source_target_pairs={{0,24},{8,16},{16,8},{24,0},{1,25},{9,17},{17,9},{25,1},{2,26},{10... | collective-permute-start | bytes 245768 | tf_op jit(solution)/shard_map/ppermute | solution.py:499
  15.8 9.3 %collective-permute-start.5 = (f32[5,16,256]{2,1,0:T(8,128)S(1)}, f32[5,16,256]{2,1,0:T(8,128)S(1)}, u32[]{:S(2)}, u32[]{:S(2)}) collective-permute-start(f32[5,16,256]{2,1,0:T(8,128)S(1)} %get-tuple-element.61), channel_id=1, source_target_pairs={{0,16},{8,24},{16,0},{24,8},{1,17},{9,25},{17,1},{25,9},{2,18},{10... | collective-permute-start | bytes 245768 | tf_op jit(solution)/shard_map/ppermute | solution.py:499
  15.9 9.1 %collective-permute-start.6 = (f32[5,16,256]{2,1,0:T(8,128)S(1)}, f32[5,16,256]{2,1,0:T(8,128)S(1)}, u32[]{:S(2)}, u32[]{:S(2)}) collective-permute-start(f32[5,16,256]{2,1,0:T(8,128)S(1)} %get-tuple-element.62), channel_id=1, source_target_pairs={{0,8},{8,0},{16,24},{24,16},{1,9},{9,1},{17,25},{25,17},{2,10},{10... | collective-permute-start | bytes 245768 | tf_op jit(solution)/shard_map/ppermute | solution.py:499
  20.5 8.8 %collective-permute-start.7 = (f32[5,16,256]{2,1,0:T(8,128)S(1)}, f32[5,16,256]{2,1,0:T(8,128)S(1)}, u32[]{:S(2)}, u32[]{:S(2)}) collective-permute-start(f32[5,16,256]{2,1,0:T(8,128)S(1)} %get-tuple-element.64), channel_id=1, source_target_pairs={{0,16},{8,24},{16,0},{24,8},{1,17},{9,25},{17,1},{25,9},{2,18},{10... | collective-permute-start | bytes 245768 | tf_op jit(solution)/shard_map/ppermute | solution.py:499
  20.7 8.5 %collective-permute-start.8 = (f32[5,16,256]{2,1,0:T(8,128)S(1)}, f32[5,16,256]{2,1,0:T(8,128)S(1)}, u32[]{:S(2)}, u32[]{:S(2)}) collective-permute-start(f32[5,16,256]{2,1,0:T(8,128)S(1)} %get-tuple-element.65), channel_id=1, source_target_pairs={{0,8},{8,0},{16,24},{24,16},{1,9},{9,1},{17,25},{25,17},{2,10},{10... | collective-permute-start | bytes 245768 | tf_op jit(solution)/shard_map/ppermute | solution.py:499
  22.4 6.8 %collective-permute-start.9 = (f32[5,16,256]{2,1,0:T(8,128)S(1)}, f32[5,16,256]{2,1,0:T(8,128)S(1)}, u32[]{:S(2)}, u32[]{:S(2)}) collective-permute-start(f32[5,16,256]{2,1,0:T(8,128)S(1)} %get-tuple-element.66), channel_id=1, source_target_pairs={{0,24},{8,16},{16,8},{24,0},{1,25},{9,17},{17,9},{25,1},{2,26},{10... | collective-permute-start | bytes 245768 | tf_op jit(solution)/shard_map/ppermute | solution.py:499
